TPU v7x, 32 devices: a whole 2x2x4 slice. The times are simulated.
32 devices in a mesh: section: 4 (over x, core), dp: 8 (over z, y).
Axes of the slice: x: 2, y: 2, z: 4, core: 2. Of those that a mesh axis runs over, the one named last changes fastest.
Arguments:
- tokens: bfloat16 [32, 2, 512, 768], P(('section', 'dp')), may hold values from -6 to 6
- doc_ids: int32 [32, 2, 512], replicated, may hold values from 0 to 3, never falling along the last dimension, each value on 1 to 256 neighbouring positions
- reset_flags: int32 [32, 2], replicated, may hold values 0 or 1
- memory_init: bfloat16 [10, 768], replicated, may hold values from -6 to 6
- w_proj: bfloat16 [4, 768, 3072], P('section'), may hold values from -0.375 to 0.375
- vectors: float32 [4, 2, 768], P('section'), may hold values from -0.5 to 1.5
- w_down: bfloat16 [6144, 768], P('section'), may hold values from -0.109375 to 0.109375
- cotangent: bfloat16 [32, 2, 512, 768], P(('section', 'dp')), may hold values from -6 to 6
Outputs:
- block_out: bfloat16 [32, 2, 512, 768], P(('section', 'dp'))
- grad_tokens: bfloat16 [32, 2, 512, 768], P(('section', 'dp'))
- grad_proj: float32 [4, 768, 3072], P('section')
- grad_vectors: float32 [4, 2, 768], P('section')
- grad_down: float32 [6144, 768], P('section')
- grad_memory: float32 [10, 768], P(None, 'section')
All inputs are finite; a program needn't handle non-finite values.
Results may differ from a plain program's by a relative error of at most 0.025.
Values may be sent and summed in bfloat16 or wider, within the bound.
A program may use at most 320 MiB of HBM per device.

v0:
```python
import jax
import jax.numpy as jnp
from jax import lax
from jax.sharding import PartitionSpec as P

HEADS = 12


NORM_EPSILON = 1e-06
NEGATIVE = -1e30


def from_behind(block, axis, distance):
    devices = range(lax.axis_size(axis))
    route = [(i - distance, i) for i in devices if i - distance in devices]
    return lax.ppermute(block, axis, route)


def shifted(shard, axis, by):
    count = lax.axis_size(axis)
    return lax.ppermute(shard, axis, [(i, (i + by) % count) for i in range(count)])


def for_sending(shard):
    return jax.tree.map(lambda a: a.astype(jnp.bfloat16) if a.dtype == jnp.float32 else a, shard)


def norm_stats(summed):
    center = summed - jnp.mean(summed, axis=-1, keepdims=True)
    variance = jnp.mean(center * center, axis=-1, keepdims=True)
    inverse = lax.rsqrt(variance + NORM_EPSILON)
    return (center * inverse, inverse)


def norm_back(grad_out, normed, inverse, gain):
    scaled = grad_out * gain
    grad_sum = inverse * (
        scaled
        - jnp.mean(scaled, axis=-1, keepdims=True)
        - normed * jnp.mean(scaled * normed, axis=-1, keepdims=True)
    )
    return (grad_sum, jnp.stack([jnp.sum(grad_out * normed, axis=0), jnp.sum(grad_out, axis=0)]))


def contract_rows(left, right):
    return lax.dot_general(
        left, right, (((0,), (0,)), ((), ())), preferred_element_type=jnp.float32
    )


def contract_cols(left, right):
    return lax.dot_general(
        left, right, (((1,), (1,)), ((), ())), preferred_element_type=jnp.float32
    )


def visible(documents, memory_count):
    extended = jnp.concatenate([jnp.full((memory_count,), -1, jnp.int32), documents])
    return (
        (extended[:, None] == extended[None, :]) | (extended[:, None] < 0) | (extended[None, :] < 0)
    )


def gelu_slope(pre_act):
    return (
        0.5 * (1.0 + lax.erf(pre_act * 0.7071067811865476))
        + pre_act * jnp.exp(-0.5 * pre_act * pre_act) * 0.3989422804014327
    )


def attention_forward(section_in, weights, allowed, head_count):
    row_count, model_width = section_in.shape
    head_size = model_width // head_count
    projected = jnp.dot(
        section_in, weights[:, : 3 * model_width], preferred_element_type=jnp.float32
    ).astype(jnp.bfloat16)
    queries = projected[:, :model_width].reshape(row_count, head_count, head_size)
    key_rows = projected[:, model_width : 2 * model_width].reshape(row_count, head_count, head_size)
    value_rows = projected[:, 2 * model_width :].reshape(row_count, head_count, head_size)
    scores = jnp.einsum(
        "qhd,khd->hqk", queries, key_rows, preferred_element_type=jnp.float32
    ) * head_size ** (-0.5)
    scores = jnp.where(allowed[None], scores, NEGATIVE)
    attn_probs = jax.nn.softmax(scores, axis=-1)
    probs_low = attn_probs.astype(jnp.bfloat16)
    mixed_rows = jnp.einsum(
        "hqk,khd->qhd", probs_low, value_rows, preferred_element_type=jnp.float32
    )
    mixed_rows = mixed_rows.reshape(row_count, model_width).astype(jnp.bfloat16)
    summed = section_in.astype(jnp.float32) + jnp.dot(
        mixed_rows, weights[:, 3 * model_width :], preferred_element_type=jnp.float32
    )
    return (summed, (queries, key_rows, value_rows, attn_probs, probs_low, mixed_rows))


def attention_backward(section_in, weights, vector, allowed, head_count, grad_out):
    row_count, model_width = section_in.shape
    head_size = model_width // head_count
    summed, saved_parts = attention_forward(section_in, weights, allowed, head_count)
    queries, key_rows, value_rows, attn_probs, probs_low, mixed_rows = saved_parts
    normed, inverse = norm_stats(summed)
    grad_sum, grad_vector = norm_back(grad_out, normed, inverse, vector[0])
    grad_branch = grad_sum.astype(jnp.bfloat16)
    grad_output_proj = contract_rows(mixed_rows, grad_branch)
    grad_mixed = contract_cols(grad_branch, weights[:, 3 * model_width :]).astype(jnp.bfloat16)
    grad_mixed = grad_mixed.reshape(row_count, head_count, head_size)
    grad_probs = jnp.einsum(
        "qhd,khd->hqk", grad_mixed, value_rows, preferred_element_type=jnp.float32
    )
    grad_values = jnp.einsum(
        "hqk,qhd->khd", probs_low, grad_mixed, preferred_element_type=jnp.float32
    ).astype(jnp.bfloat16)
    grad_scores = attn_probs * (
        grad_probs - jnp.sum(attn_probs * grad_probs, axis=-1, keepdims=True)
    )
    grad_scores = grad_scores.astype(jnp.bfloat16)
    score_scale = head_size ** (-0.5)
    grad_queries = (
        jnp.einsum("hqk,khd->qhd", grad_scores, key_rows, preferred_element_type=jnp.float32)
        * score_scale
    ).astype(jnp.bfloat16)
    grad_keys = (
        jnp.einsum("hqk,qhd->khd", grad_scores, queries, preferred_element_type=jnp.float32)
        * score_scale
    ).astype(jnp.bfloat16)
    grad_projected = jnp.concatenate(
        [
            grad_queries.reshape(row_count, model_width),
            grad_keys.reshape(row_count, model_width),
            grad_values.reshape(row_count, model_width),
        ],
        axis=1,
    )
    grad_input_proj = contract_rows(section_in, grad_projected)
    grad_in = (grad_sum + contract_cols(grad_projected, weights[:, : 3 * model_width])).astype(
        jnp.bfloat16
    )
    return (grad_in, jnp.concatenate([grad_input_proj, grad_output_proj], axis=1), grad_vector)


def feed_forward(section_in, first_matrix, second_matrix):
    pre_act = jnp.dot(section_in, first_matrix, preferred_element_type=jnp.float32)
    activated = jax.nn.gelu(pre_act, approximate=False).astype(jnp.bfloat16)
    summed = section_in.astype(jnp.float32) + jnp.dot(
        activated, second_matrix, preferred_element_type=jnp.float32
    )
    return (pre_act, summed)


def feed_backward(section_in, first_matrix, second_matrix, vector, pre_act, summed, grad_out):
    normed, inverse = norm_stats(summed)
    grad_sum, grad_vector = norm_back(grad_out, normed, inverse, vector[0])
    grad_branch = grad_sum.astype(jnp.bfloat16)
    activated = jax.nn.gelu(pre_act, approximate=False).astype(jnp.bfloat16)
    grad_second = contract_rows(activated, grad_branch)
    grad_hidden = contract_cols(grad_branch, second_matrix)
    grad_pre = (grad_hidden * gelu_slope(pre_act)).astype(jnp.bfloat16)
    grad_first = contract_rows(section_in, grad_pre)
    grad_in = (grad_sum + contract_cols(grad_pre, first_matrix)).astype(jnp.bfloat16)
    return (grad_in, grad_first, grad_vector, grad_second)


def write_row(buffer, position, new_rows, flag_value):
    previous = lax.dynamic_index_in_dim(buffer, position, 0, keepdims=False)
    return lax.dynamic_update_index_in_dim(
        buffer, jnp.where(flag_value, new_rows, previous), position, 0
    )


def write_cell(buffer, item_slot, segment, new_rows, flag_value):
    previous = buffer[item_slot, segment]
    anchor = jnp.zeros((), jnp.int32)
    return lax.dynamic_update_slice(
        buffer,
        jnp.where(flag_value, new_rows, previous)[None, None],
        (item_slot, segment, anchor, anchor),
    )


def body(tokens, doc_ids, reset_flags, memory_init, w_proj, vectors, w_down, cotangent):
    section_count = lax.axis_size("section")
    data_count = lax.axis_size("dp")
    section_index = lax.axis_index("section")
    data_index = lax.axis_index("dp")
    is_attention = section_index % 2 == 0
    token_all, cotangent_all = (
        lax.all_gather(tokens, "section", axis=0, tiled=True),
        lax.all_gather(cotangent, "section", axis=0, tiled=True),
    )
    pipe_items, segments, seg_tokens, model_width = token_all.shape
    memory_count = memory_init.shape[0]
    row_count = memory_count + seg_tokens
    micro_count = pipe_items * segments
    hidden_width = w_proj.shape[2]
    item_ids = jnp.arange(pipe_items, dtype=jnp.int32) * data_count + data_index
    pipe_docs = jnp.take(doc_ids, item_ids, axis=0)
    pipe_flags = jnp.take(reset_flags, item_ids, axis=0)
    weights = w_proj[0]
    vector = vectors[0]
    borrowed = from_behind(w_down, "section", 1)
    second_matrix = jnp.concatenate([borrowed, w_down], axis=0)

    def locate(micro_index):
        clipped = jnp.clip(micro_index, 0, micro_count - 1)
        return (clipped, clipped % pipe_items, clipped // pipe_items)

    def fresh_memory(item_slot, segment):
        return (segment == 0) | (pipe_flags[item_slot, segment] == 1)

    def forward_work(micro_index, incoming, kept_in, kept_pre, kept_sum, out_rows):
        is_valid = (micro_index >= 0) & (micro_index < micro_count)
        clipped, item_slot, segment = locate(micro_index)
        token_rows = token_all[item_slot, segment]
        memory_rows = jnp.where(
            fresh_memory(item_slot, segment), memory_init, incoming[:memory_count]
        )
        first_rows = jnp.concatenate([memory_rows, token_rows], axis=0)
        section_in = jnp.where(section_index == 0, first_rows, incoming)
        allowed = visible(pipe_docs[item_slot, segment], memory_count)

        def run_attention():
            summed, saved_parts = attention_forward(section_in, weights, allowed, HEADS)
            return (summed, jnp.zeros((row_count, hidden_width), jnp.float32))

        def run_feed():
            pre_act, summed = feed_forward(section_in, weights, second_matrix)
            return (summed, pre_act)

        def run_spare():
            return (
                jnp.zeros((row_count, model_width), jnp.float32),
                jnp.zeros((row_count, hidden_width), jnp.float32),
            )

        selector = jnp.where(is_valid, jnp.where(is_attention, 0, 1), 2)
        summed, pre_act = lax.switch(selector, [run_attention, run_feed, run_spare])
        normed, inverse = norm_stats(summed)
        produced = (normed * vector[0] + vector[1]).astype(jnp.bfloat16)
        kept_in = write_row(kept_in, clipped, section_in, is_valid)
        kept_pre = write_row(kept_pre, clipped, pre_act, is_valid)
        kept_sum = write_row(kept_sum, clipped, summed, is_valid)
        last_section = (section_index == section_count - 1) & is_valid
        out_rows = write_cell(out_rows, item_slot, segment, produced[memory_count:], last_section)
        return (produced, kept_in, kept_pre, kept_sum, out_rows)

    def backward_work(micro_index, is_valid, incoming, kept_in, kept_pre, kept_sum, totals):
        grad_proj, grad_vec, grad_down, grad_memory, grad_rows = totals
        clipped, item_slot, segment = locate(micro_index)
        next_segment = jnp.minimum(segment + 1, segments - 1)
        carry_back = (segment + 1 < segments) & (pipe_flags[item_slot, next_segment] == 0)
        memory_grad = jnp.where(
            carry_back,
            incoming[:memory_count],
            jnp.zeros((memory_count, model_width), jnp.bfloat16),
        )
        last_grad = jnp.concatenate([memory_grad, cotangent_all[item_slot, segment]], axis=0)
        grad_out = jnp.where(section_index == section_count - 1, last_grad, incoming).astype(
            jnp.float32
        )
        section_in = kept_in[clipped]
        allowed = visible(pipe_docs[item_slot, segment], memory_count)

        def back_attention():
            grad_in, grad_weights, grad_vector = attention_backward(
                section_in, weights, vector, allowed, HEADS, grad_out
            )
            return (grad_in, grad_weights, grad_vector, jnp.zeros(second_matrix.shape, jnp.float32))

        def back_feed():
            pre_act = kept_pre[clipped]
            summed = kept_sum[clipped]
            return feed_backward(
                section_in, weights, second_matrix, vector, pre_act, summed, grad_out
            )

        def back_spare():
            return (
                jnp.zeros((row_count, model_width), jnp.bfloat16),
                jnp.zeros(weights.shape, jnp.float32),
                jnp.zeros(vector.shape, jnp.float32),
                jnp.zeros(second_matrix.shape, jnp.float32),
            )

        selector = jnp.where(is_valid, jnp.where(is_attention, 0, 1), 2)
        grad_in, grad_weights, grad_vector, grad_second = lax.switch(
            selector, [back_attention, back_feed, back_spare]
        )
        grad_proj = grad_proj + grad_weights
        grad_vec = grad_vec + grad_vector
        grad_down = grad_down + grad_second
        first_section = (section_index == 0) & is_valid
        is_fresh = first_section & fresh_memory(item_slot, segment)
        grad_memory = grad_memory + jnp.where(
            is_fresh, grad_in[:memory_count].astype(jnp.float32), 0.0
        )
        grad_rows = write_cell(grad_rows, item_slot, segment, grad_in[memory_count:], first_section)
        return (grad_in, (grad_proj, grad_vec, grad_down, grad_memory, grad_rows))

    kept_pre = jnp.zeros((micro_count, row_count, hidden_width), jnp.float32)
    kept_sum = jnp.zeros((micro_count, row_count, model_width), jnp.float32)
    kept_in = jnp.zeros((micro_count, row_count, model_width), jnp.bfloat16)
    out_rows = jnp.zeros((pipe_items, segments, seg_tokens, model_width), jnp.bfloat16)
    empty_hand = jnp.zeros((row_count, model_width), jnp.bfloat16)
    grad_start = (
        jnp.zeros(weights.shape, jnp.float32),
        jnp.zeros(vector.shape, jnp.float32),
        jnp.zeros(second_matrix.shape, jnp.float32),
        jnp.zeros((memory_count, model_width), jnp.float32),
        jnp.zeros((pipe_items, segments, seg_tokens, model_width), jnp.bfloat16),
    )

    def forward_tick(tick_index, state_carry):
        incoming, kept_in, kept_pre, kept_sum, out_rows = state_carry
        produced, kept_in, kept_pre, kept_sum, out_rows = forward_work(
            tick_index - section_index, incoming, kept_in, kept_pre, kept_sum, out_rows
        )
        incoming = shifted(produced, "section", 1)
        return (incoming, kept_in, kept_pre, kept_sum, out_rows)

    forward_end = lax.fori_loop(
        0,
        micro_count + section_count - 1,
        forward_tick,
        (empty_hand, kept_in, kept_pre, kept_sum, out_rows),
    )
    kept_in, kept_pre, kept_sum, out_rows = (
        forward_end[1],
        forward_end[2],
        forward_end[3],
        forward_end[4],
    )

    def backward_tick(tick_index, state_carry):
        incoming, totals = state_carry
        micro_index = micro_count - 1 - tick_index + (section_count - 1) - section_index
        is_valid = (micro_index >= 0) & (micro_index < micro_count)
        grad_in, totals = backward_work(
            micro_index, is_valid, incoming, kept_in, kept_pre, kept_sum, totals
        )
        incoming = jax.tree.map(
            lambda part, own: part.astype(own.dtype),
            shifted(for_sending(grad_in), "section", -1),
            grad_in,
        )
        return (incoming, totals)

    backward_end = lax.fori_loop(
        0, micro_count + section_count - 1, backward_tick, (empty_hand, grad_start)
    )
    totals = backward_end[1]
    grad_proj, grad_vec, grad_down, grad_memory, grad_rows = totals
    half_rows = w_down.shape[0]
    total_proj, total_vec, total_down = (
        lax.psum(grad_proj.astype(jnp.bfloat16), "dp").astype(jnp.float32),
        lax.psum(grad_vec.astype(jnp.bfloat16), "dp").astype(jnp.float32),
        lax.psum(grad_down.astype(jnp.bfloat16), "dp").astype(jnp.float32),
    )
    returned = from_behind(total_down[:half_rows].astype(jnp.bfloat16), "section", -1).astype(
        jnp.float32
    )
    down_part = jnp.where(is_attention, returned, total_down[half_rows:])
    memory_share = lax.psum_scatter(grad_memory, "section", scatter_dimension=1, tiled=True)
    memory_total = lax.psum(memory_share, "dp")
    block_from, input_from = (
        lax.all_to_all(out_rows, "section", split_axis=0, concat_axis=0, tiled=True),
        lax.all_to_all(grad_rows, "section", split_axis=0, concat_axis=0, tiled=True),
    )
    block_rows = block_from[section_count - 1 : section_count]
    input_rows = input_from[0:1]
    return (block_rows, input_rows, total_proj[None], total_vec[None], down_part, memory_total)


def solution(mesh):
    placed = (
        P(("section", "dp"), None, None, None),
        P(),
        P(),
        P(),
        P("section", None, None),
        P("section", None, None),
        P("section", None),
        P(("section", "dp"), None, None, None),
    )
    return jax.shard_map(
        body,
        mesh=mesh,
        in_specs=placed,
        out_specs=(
            P(("section", "dp"), None, None, None),
            P(("section", "dp"), None, None, None),
            P("section", None, None),
            P("section", None, None),
            P("section", None),
            P(None, "section"),
        ),
        check_vma=False,
    )
```

profile of v0, /device:TPU:0, one launch (start us, length us, event | category | flops | bytes accessed | tf_op | source)
XLA Modules:
  0.0 2578.9 jit_solution(8418329717607443785)
XLA Ops:
  20.1 51.8 %all-gather.3.cloned.1.call-done = bf16[4,2,512,768]{3,2,1,0:T(8,128)(2,1)} async-done(((bf16[1,2,512,768]{3,2,1,0:T(8,128)(2,1)}), bf16[4,2,512,768]{3,2,1,0:T(8,128)(2,1)}) %all-gather.3.cloned.1.call-update) | async-done | bytes 6291472 | tf_op jit(solution)/shard_map/all_gather | solution.py:187
  102.3 632.9 %while.49 = (s32[]{:T(128)}, bf16[522,768]{1,0:T(8,128)(2,1)S(1)}, bf16[8,522,768]{2,1,0:T(8,128)(2,1)}, f32[8,522,3072]{2,1,0:T(8,128)}, f32[8,522,768]{2,1,0:T...) while((s32[]{:T(128)}, bf16[522,768]{1,0:T(8,128)(2,1)S(1)}, ...), condition=%wide.region_9.10_spmd, body=%wide.region_0.9_spmd.sunk | while | flops 5039664128 | bytes 122319144 | solution.py:320
  108.2 32.1 %conditional.5 = (f32[522,768]{1,0:T(8,128)S(1)}, f32[522,3072]{1,0:T(8,128)}, f32[522,1]{0,1:T(1,128)S(1)}) conditional(s32[]{:T(128)} %clamp.26, (bf16[522,768]{1,0:T(8,128)(2,1)S(1)}, bf16[768,3072]{1,0:T(8,128)(2,1)}, s32[4,2,512]{2,1,0:T(2,128)}, s32[]{:T(128)}, s32[]{:T(128)}) %tuple.148, (bf16[522,768]{1,0:T(8,128)(2,1)S(1)}, ...), branch_computations={%region_1.4_spmd, %region_5.6_spmd, %region_7.7_spmd} | conditional | flops 5031645184 | bytes 63563588 | solution.py:236
  168.3 32.1 %conditional.5 = (f32[522,768]{1,0:T(8,128)S(1)}, f32[522,3072]{1,0:T(8,128)}, f32[522,1]{0,1:T(1,128)S(1)}) conditional(s32[]{:T(128)} %clamp.26, (bf16[522,768]{1,0:T(8,128)(2,1)S(1)}, bf16[768,3072]{1,0:T(8,128)(2,1)}, s32[4,2,512]{2,1,0:T(2,128)}, s32[]{:T(128)}, s32[]{:T(128)}) %tuple.148, (bf16[522,768]{1,0:T(8,128)(2,1)S(1)}, ...), branch_computations={%region_1.4_spmd, %region_5.6_spmd, %region_7.7_spmd} | conditional | flops 5031645184 | bytes 63563588 | solution.py:236
  288.0 32.1 %conditional.5 = (f32[522,768]{1,0:T(8,128)S(1)}, f32[522,3072]{1,0:T(8,128)}, f32[522,1]{0,1:T(1,128)S(1)}) conditional(s32[]{:T(128)} %clamp.26, (bf16[522,768]{1,0:T(8,128)(2,1)S(1)}, bf16[768,3072]{1,0:T(8,128)(2,1)}, s32[4,2,512]{2,1,0:T(2,128)}, s32[]{:T(128)}, s32[]{:T(128)}) %tuple.148, (bf16[522,768]{1,0:T(8,128)(2,1)S(1)}, ...), branch_computations={%region_1.4_spmd, %region_5.6_spmd, %region_7.7_spmd} | conditional | flops 5031645184 | bytes 63563588 | solution.py:236
  348.0 32.1 %conditional.5 = (f32[522,768]{1,0:T(8,128)S(1)}, f32[522,3072]{1,0:T(8,128)}, f32[522,1]{0,1:T(1,128)S(1)}) conditional(s32[]{:T(128)} %clamp.26, (bf16[522,768]{1,0:T(8,128)(2,1)S(1)}, bf16[768,3072]{1,0:T(8,128)(2,1)}, s32[4,2,512]{2,1,0:T(2,128)}, s32[]{:T(128)}, s32[]{:T(128)}) %tuple.148, (bf16[522,768]{1,0:T(8,128)(2,1)S(1)}, ...), branch_computations={%region_1.4_spmd, %region_5.6_spmd, %region_7.7_spmd} | conditional | flops 5031645184 | bytes 63563588 | solution.py:236
  407.9 32.1 %conditional.5 = (f32[522,768]{1,0:T(8,128)S(1)}, f32[522,3072]{1,0:T(8,128)}, f32[522,1]{0,1:T(1,128)S(1)}) conditional(s32[]{:T(128)} %clamp.26, (bf16[522,768]{1,0:T(8,128)(2,1)S(1)}, bf16[768,3072]{1,0:T(8,128)(2,1)}, s32[4,2,512]{2,1,0:T(2,128)}, s32[]{:T(128)}, s32[]{:T(128)}) %tuple.148, (bf16[522,768]{1,0:T(8,128)(2,1)S(1)}, ...), branch_computations={%region_1.4_spmd, %region_5.6_spmd, %region_7.7_spmd} | conditional | flops 5031645184 | bytes 63563588 | solution.py:236
  467.9 32.1 %conditional.5 = (f32[522,768]{1,0:T(8,128)S(1)}, f32[522,3072]{1,0:T(8,128)}, f32[522,1]{0,1:T(1,128)S(1)}) conditional(s32[]{:T(128)} %clamp.26, (bf16[522,768]{1,0:T(8,128)(2,1)S(1)}, bf16[768,3072]{1,0:T(8,128)(2,1)}, s32[4,2,512]{2,1,0:T(2,128)}, s32[]{:T(128)}, s32[]{:T(128)}) %tuple.148, (bf16[522,768]{1,0:T(8,128)(2,1)S(1)}, ...), branch_computations={%region_1.4_spmd, %region_5.6_spmd, %region_7.7_spmd} | conditional | flops 5031645184 | bytes 63563588 | solution.py:236
  527.8 32.1 %conditional.5 = (f32[522,768]{1,0:T(8,128)S(1)}, f32[522,3072]{1,0:T(8,128)}, f32[522,1]{0,1:T(1,128)S(1)}) conditional(s32[]{:T(128)} %clamp.26, (bf16[522,768]{1,0:T(8,128)(2,1)S(1)}, bf16[768,3072]{1,0:T(8,128)(2,1)}, s32[4,2,512]{2,1,0:T(2,128)}, s32[]{:T(128)}, s32[]{:T(128)}) %tuple.148, (bf16[522,768]{1,0:T(8,128)(2,1)S(1)}, ...), branch_computations={%region_1.4_spmd, %region_5.6_spmd, %region_7.7_spmd} | conditional | flops 5031645184 | bytes 63563588 | solution.py:236
  738.4 1436.7 %while.50 = (s32[]{:T(128)}, bf16[522,768]{1,0:T(8,128)(2,1)S(1)}, f32[768,3072]{0,1:T(8,128)}, f32[2,768]{1,0:T(2,128)}, f32[3072,768]{1,0:T(8,128)}, /*index=5...) while((s32[]{:T(128)}, bf16[522,768]{1,0:T(8,128)(2,1)S(1)}, ...), condition=%wide.region_29.30_spmd.clone, body=%wide.region_10.29_spmd.clone.sunk | while | flops 9994588160 | bytes 357377504 | solution.py:347
  766.8 46.1 %collective-permute-start.1 = (bf16[522,768]{1,0:T(8,128)(2,1)}, bf16[522,768]{1,0:T(8,128)(2,1)S(1)}, u32[]{:S(2)}, u32[]{:S(2)}) collective-permute-start(bf16[522,768]{1,0:T(8,128)(2,1)} %get-tuple-element.1509), channel_id=1, source_target_pairs={{0,24},{8,0},{16,8},{24,16},{1,25},{9,1},{17,9},{25,17},{2,26},{10... | collective-permute-start | bytes 2405384 | tf_op jit(solution)/shard_map/while/body/eval_jaxpr/ppermute | solution.py:21
  863.1 35.3 %collective-permute-start.1 = (bf16[522,768]{1,0:T(8,128)(2,1)}, bf16[522,768]{1,0:T(8,128)(2,1)S(1)}, u32[]{:S(2)}, u32[]{:S(2)}) collective-permute-start(bf16[522,768]{1,0:T(8,128)(2,1)} %get-tuple-element.1509), channel_id=1, source_target_pairs={{0,24},{8,0},{16,8},{24,16},{1,25},{9,1},{17,9},{25,17},{2,26},{10... | collective-permute-start | bytes 2405384 | tf_op jit(solution)/shard_map/while/body/eval_jaxpr/ppermute | solution.py:21
  954.1 65.3 %collective-permute-start.1 = (bf16[522,768]{1,0:T(8,128)(2,1)}, bf16[522,768]{1,0:T(8,128)(2,1)S(1)}, u32[]{:S(2)}, u32[]{:S(2)}) collective-permute-start(bf16[522,768]{1,0:T(8,128)(2,1)} %get-tuple-element.1509), channel_id=1, source_target_pairs={{0,24},{8,0},{16,8},{24,16},{1,25},{9,1},{17,9},{25,17},{2,26},{10... | collective-permute-start | bytes 2405384 | tf_op jit(solution)/shard_map/while/body/eval_jaxpr/ppermute | solution.py:21
  1052.7 107.2 %conditional.6 = (bf16[522,768]{1,0:T(8,128)(2,1)}, f32[768,3072]{0,1:T(8,128)}, f32[2,768]{1,0:T(2,128)S(1)}, f32[3072,768]{1,0:T(8,128)}) conditional(s32[]{:T(128)} %clamp.27, (bf16[522,768]{1,0:T(8,128)(2,1)}, bf16[768,3072]{1,0:T(8,128)(2,1)}, s32[4,2,512]{2,1,0:T(2,128)}, s32[]{:T(128)}, s32[]{:T(128)}, ...), branch_computations={%region_11.20_spmd, %region_21.27_spmd, %region_28.28_spmd} | conditional | flops 9982310400 | bytes 286784000 | solution.py:285
  1193.5 107.2 %conditional.6 = (bf16[522,768]{1,0:T(8,128)(2,1)}, f32[768,3072]{0,1:T(8,128)}, f32[2,768]{1,0:T(2,128)S(1)}, f32[3072,768]{1,0:T(8,128)}) conditional(s32[]{:T(128)} %clamp.27, (bf16[522,768]{1,0:T(8,128)(2,1)}, bf16[768,3072]{1,0:T(8,128)(2,1)}, s32[4,2,512]{2,1,0:T(2,128)}, s32[]{:T(128)}, s32[]{:T(128)}, ...), branch_computations={%region_11.20_spmd, %region_21.27_spmd, %region_28.28_spmd} | conditional | flops 9982310400 | bytes 286784000 | solution.py:285
  1334.0 107.2 %conditional.6 = (bf16[522,768]{1,0:T(8,128)(2,1)}, f32[768,3072]{0,1:T(8,128)}, f32[2,768]{1,0:T(2,128)S(1)}, f32[3072,768]{1,0:T(8,128)}) conditional(s32[]{:T(128)} %clamp.27, (bf16[522,768]{1,0:T(8,128)(2,1)}, bf16[768,3072]{1,0:T(8,128)(2,1)}, s32[4,2,512]{2,1,0:T(2,128)}, s32[]{:T(128)}, s32[]{:T(128)}, ...), branch_computations={%region_11.20_spmd, %region_21.27_spmd, %region_28.28_spmd} | conditional | flops 9982310400 | bytes 286784000 | solution.py:285
  1474.7 107.2 %conditional.6 = (bf16[522,768]{1,0:T(8,128)(2,1)}, f32[768,3072]{0,1:T(8,128)}, f32[2,768]{1,0:T(2,128)S(1)}, f32[3072,768]{1,0:T(8,128)}) conditional(s32[]{:T(128)} %clamp.27, (bf16[522,768]{1,0:T(8,128)(2,1)}, bf16[768,3072]{1,0:T(8,128)(2,1)}, s32[4,2,512]{2,1,0:T(2,128)}, s32[]{:T(128)}, s32[]{:T(128)}, ...), branch_computations={%region_11.20_spmd, %region_21.27_spmd, %region_28.28_spmd} | conditional | flops 9982310400 | bytes 286784000 | solution.py:285
  1615.2 107.2 %conditional.6 = (bf16[522,768]{1,0:T(8,128)(2,1)}, f32[768,3072]{0,1:T(8,128)}, f32[2,768]{1,0:T(2,128)S(1)}, f32[3072,768]{1,0:T(8,128)}) conditional(s32[]{:T(128)} %clamp.27, (bf16[522,768]{1,0:T(8,128)(2,1)}, bf16[768,3072]{1,0:T(8,128)(2,1)}, s32[4,2,512]{2,1,0:T(2,128)}, s32[]{:T(128)}, s32[]{:T(128)}, ...), branch_computations={%region_11.20_spmd, %region_21.27_spmd, %region_28.28_spmd} | conditional | flops 9982310400 | bytes 286784000 | solution.py:285
  1755.9 107.2 %conditional.6 = (bf16[522,768]{1,0:T(8,128)(2,1)}, f32[768,3072]{0,1:T(8,128)}, f32[2,768]{1,0:T(2,128)S(1)}, f32[3072,768]{1,0:T(8,128)}) conditional(s32[]{:T(128)} %clamp.27, (bf16[522,768]{1,0:T(8,128)(2,1)}, bf16[768,3072]{1,0:T(8,128)(2,1)}, s32[4,2,512]{2,1,0:T(2,128)}, s32[]{:T(128)}, s32[]{:T(128)}, ...), branch_computations={%region_11.20_spmd, %region_21.27_spmd, %region_28.28_spmd} | conditional | flops 9982310400 | bytes 286784000 | solution.py:285
  1896.4 107.2 %conditional.6 = (bf16[522,768]{1,0:T(8,128)(2,1)}, f32[768,3072]{0,1:T(8,128)}, f32[2,768]{1,0:T(2,128)S(1)}, f32[3072,768]{1,0:T(8,128)}) conditional(s32[]{:T(128)} %clamp.27, (bf16[522,768]{1,0:T(8,128)(2,1)}, bf16[768,3072]{1,0:T(8,128)(2,1)}, s32[4,2,512]{2,1,0:T(2,128)}, s32[]{:T(128)}, s32[]{:T(128)}, ...), branch_computations={%region_11.20_spmd, %region_21.27_spmd, %region_28.28_spmd} | conditional | flops 9982310400 | bytes 286784000 | solution.py:285
  2037.2 107.2 %conditional.6 = (bf16[522,768]{1,0:T(8,128)(2,1)}, f32[768,3072]{0,1:T(8,128)}, f32[2,768]{1,0:T(2,128)S(1)}, f32[3072,768]{1,0:T(8,128)}) conditional(s32[]{:T(128)} %clamp.27, (bf16[522,768]{1,0:T(8,128)(2,1)}, bf16[768,3072]{1,0:T(8,128)(2,1)}, s32[4,2,512]{2,1,0:T(2,128)}, s32[]{:T(128)}, s32[]{:T(128)}, ...), branch_computations={%region_11.20_spmd, %region_21.27_spmd, %region_28.28_spmd} | conditional | flops 9982310400 | bytes 286784000 | solution.py:285
  2189.1 77.4 %all_to_all.10 = bf16[4,2,512,768]{3,2,1,0:T(8,128)(2,1)} all-to-all(bf16[4,2,512,768]{3,2,1,0:T(8,128)(2,1)} %get-tuple-element.969), channel_id=1, replica_groups=mesh['section'=4,'dp'=8] {'section'}, dimensions={0} | all-to-all | bytes 12582912 | tf_op jit(solution)/shard_map/all_to_all | solution.py:366
  2271.9 216.7 %all-reduce.5.cloned.1.call-done = (bf16[1,768,3072]{2,1,0:T(8,128)(2,1)}, bf16[3072,768]{1,0:T(8,128)(2,1)}) async-done(((bf16[1,768,3072]{2,1,0:T(8,128)(2,1)}, bf16[3072,768]{1,0:T(8,128)(2,1)}), (bf16[1,768,3072]{2,1,0:T(8,128)(2,1)}, bf16[3072,768]{1,0:T(8,128)(2,1)})) %all-reduce.5.cloned.1.call-update) | async-done | bytes 9437200 | tf_op jit(solution)/shard_map/psum | solution.py:354
  2516.9 37.7 %psum.31 = f32[10,192]{1,0:T(8,128)} all-reduce(f32[10,192]{1,0:T(8,128)S(1)} %copy.72), channel_id=1, replica_groups=mesh['section'=4,'dp'=8] {'dp'}, use_global_device_ids=true, to_apply=%region_34.35 | all-reduce | flops 1920 | bytes 15360 | tf_op jit(solution)/shard_map/psum | solution.py:363
  (1143 shorter events, 2046.8 us)
Async XLA Ops:
  7.2 64.7 %all-gather.3.cloned.1.call-start = ((), (), s32[]{:S(2)}) async-start(), calls=%async_computation.3 | async-start | bytes 7864320 | tf_op jit(solution)/shard_map/all_gather | solution.py:187
  7.9 727.3 %all-gather.5.cloned.1.call-start = ((), (), s32[]{:S(2)}) async-start(), calls=%async_computation.4 | async-start | bytes 7864320 | tf_op jit(solution)/shard_map/all_gather | solution.py:188
  11.8 2476.8 %all-reduce.5.cloned.1.call-start = ((), (), s32[]{:S(2)}) async-start(), calls=%async_computation.6 | async-start | bytes 18874368 | tf_op jit(solution)/shard_map/psum | solution.py:354
  141.8 20.8 collective-permute-start
  381.5 20.7 collective-permute-start
  441.5 20.8 collective-permute-start
  561.3 20.9 collective-permute-start
  593.0 37.6 %collective-permute-start = (bf16[522,768]{1,0:T(8,128)(2,1)S(1)}, bf16[522,768]{1,0:T(8,128)(2,1)S(1)}, u32[]{:S(2)}, u32[]{:S(2)}) collective-permute-start(bf16[522,768]{1,0:T(8,128)(2,1)S(1)} %add_convert_fusion.4), channel_id=1, source_target_pairs={{0,8},{8,16},{16,24},{24,0},{1,9},{9,17},{17,25},{25,1},{2,10},{10... | collective-permute-start | bytes 2405384 | tf_op jit(solution)/shard_map/while/body/eval_jaxpr/ppermute | solution.py:21
  641.5 39.7 %collective-permute-start = (bf16[522,768]{1,0:T(8,128)(2,1)S(1)}, bf16[522,768]{1,0:T(8,128)(2,1)S(1)}, u32[]{:S(2)}, u32[]{:S(2)}) collective-permute-start(bf16[522,768]{1,0:T(8,128)(2,1)S(1)} %add_convert_fusion.4), channel_id=1, source_target_pairs={{0,8},{8,16},{16,24},{24,0},{1,9},{9,17},{17,25},{25,1},{2,10},{10... | collective-permute-start | bytes 2405384 | tf_op jit(solution)/shard_map/while/body/eval_jaxpr/ppermute | solution.py:21
  692.1 43.1 %collective-permute-start = (bf16[522,768]{1,0:T(8,128)(2,1)S(1)}, bf16[522,768]{1,0:T(8,128)(2,1)S(1)}, u32[]{:S(2)}, u32[]{:S(2)}) collective-permute-start(bf16[522,768]{1,0:T(8,128)(2,1)S(1)} %add_convert_fusion.4), channel_id=1, source_target_pairs={{0,8},{8,16},{16,24},{24,0},{1,9},{9,17},{17,25},{25,1},{2,10},{10... | collective-permute-start | bytes 2405384 | tf_op jit(solution)/shard_map/while/body/eval_jaxpr/ppermute | solution.py:21
  766.8 68.2 %collective-permute-start.1 = (bf16[522,768]{1,0:T(8,128)(2,1)}, bf16[522,768]{1,0:T(8,128)(2,1)S(1)}, u32[]{:S(2)}, u32[]{:S(2)}) collective-permute-start(bf16[522,768]{1,0:T(8,128)(2,1)} %get-tuple-element.1509), channel_id=1, source_target_pairs={{0,24},{8,0},{16,8},{24,16},{1,25},{9,1},{17,9},{25,17},{2,26},{10... | collective-permute-start | bytes 2405384 | tf_op jit(solution)/shard_map/while/body/eval_jaxpr/ppermute | solution.py:21
  863.1 62.7 %collective-permute-start.1 = (bf16[522,768]{1,0:T(8,128)(2,1)}, bf16[522,768]{1,0:T(8,128)(2,1)S(1)}, u32[]{:S(2)}, u32[]{:S(2)}) collective-permute-start(bf16[522,768]{1,0:T(8,128)(2,1)} %get-tuple-element.1509), channel_id=1, source_target_pairs={{0,24},{8,0},{16,8},{24,16},{1,25},{9,1},{17,9},{25,17},{2,26},{10... | collective-permute-start | bytes 2405384 | tf_op jit(solution)/shard_map/while/body/eval_jaxpr/ppermute | solution.py:21
  954.1 92.7 %collective-permute-start.1 = (bf16[522,768]{1,0:T(8,128)(2,1)}, bf16[522,768]{1,0:T(8,128)(2,1)S(1)}, u32[]{:S(2)}, u32[]{:S(2)}) collective-permute-start(bf16[522,768]{1,0:T(8,128)(2,1)} %get-tuple-element.1509), channel_id=1, source_target_pairs={{0,24},{8,0},{16,8},{24,16},{1,25},{9,1},{17,9},{25,17},{2,26},{10... | collective-permute-start | bytes 2405384 | tf_op jit(solution)/shard_map/while/body/eval_jaxpr/ppermute | solution.py:21
  1159.9 27.5 %collective-permute-start.1 = (bf16[522,768]{1,0:T(8,128)(2,1)}, bf16[522,768]{1,0:T(8,128)(2,1)S(1)}, u32[]{:S(2)}, u32[]{:S(2)}) collective-permute-start(bf16[522,768]{1,0:T(8,128)(2,1)} %get-tuple-element.1509), channel_id=1, source_target_pairs={{0,24},{8,0},{16,8},{24,16},{1,25},{9,1},{17,9},{25,17},{2,26},{10... | collective-permute-start | bytes 2405384 | tf_op jit(solution)/shard_map/while/body/eval_jaxpr/ppermute | solution.py:21
  1300.7 27.5 %collective-permute-start.1 = (bf16[522,768]{1,0:T(8,128)(2,1)}, bf16[522,768]{1,0:T(8,128)(2,1)S(1)}, u32[]{:S(2)}, u32[]{:S(2)}) collective-permute-start(bf16[522,768]{1,0:T(8,128)(2,1)} %get-tuple-element.1509), channel_id=1, source_target_pairs={{0,24},{8,0},{16,8},{24,16},{1,25},{9,1},{17,9},{25,17},{2,26},{10... | collective-permute-start | bytes 2405384 | tf_op jit(solution)/shard_map/while/body/eval_jaxpr/ppermute | solution.py:21
  1441.2 27.5 %collective-permute-start.1 = (bf16[522,768]{1,0:T(8,128)(2,1)}, bf16[522,768]{1,0:T(8,128)(2,1)S(1)}, u32[]{:S(2)}, u32[]{:S(2)}) collective-permute-start(bf16[522,768]{1,0:T(8,128)(2,1)} %get-tuple-element.1509), channel_id=1, source_target_pairs={{0,24},{8,0},{16,8},{24,16},{1,25},{9,1},{17,9},{25,17},{2,26},{10... | collective-permute-start | bytes 2405384 | tf_op jit(solution)/shard_map/while/body/eval_jaxpr/ppermute | solution.py:21
  1581.9 27.5 %collective-permute-start.1 = (bf16[522,768]{1,0:T(8,128)(2,1)}, bf16[522,768]{1,0:T(8,128)(2,1)S(1)}, u32[]{:S(2)}, u32[]{:S(2)}) collective-permute-start(bf16[522,768]{1,0:T(8,128)(2,1)} %get-tuple-element.1509), channel_id=1, source_target_pairs={{0,24},{8,0},{16,8},{24,16},{1,25},{9,1},{17,9},{25,17},{2,26},{10... | collective-permute-start | bytes 2405384 | tf_op jit(solution)/shard_map/while/body/eval_jaxpr/ppermute | solution.py:21
  1722.4 27.5 %collective-permute-start.1 = (bf16[522,768]{1,0:T(8,128)(2,1)}, bf16[522,768]{1,0:T(8,128)(2,1)S(1)}, u32[]{:S(2)}, u32[]{:S(2)}) collective-permute-start(bf16[522,768]{1,0:T(8,128)(2,1)} %get-tuple-element.1509), channel_id=1, source_target_pairs={{0,24},{8,0},{16,8},{24,16},{1,25},{9,1},{17,9},{25,17},{2,26},{10... | collective-permute-start | bytes 2405384 | tf_op jit(solution)/shard_map/while/body/eval_jaxpr/ppermute | solution.py:21
  1863.1 27.5 %collective-permute-start.1 = (bf16[522,768]{1,0:T(8,128)(2,1)}, bf16[522,768]{1,0:T(8,128)(2,1)S(1)}, u32[]{:S(2)}, u32[]{:S(2)}) collective-permute-start(bf16[522,768]{1,0:T(8,128)(2,1)} %get-tuple-element.1509), channel_id=1, source_target_pairs={{0,24},{8,0},{16,8},{24,16},{1,25},{9,1},{17,9},{25,17},{2,26},{10... | collective-permute-start | bytes 2405384 | tf_op jit(solution)/shard_map/while/body/eval_jaxpr/ppermute | solution.py:21
  2003.6 27.5 %collective-permute-start.1 = (bf16[522,768]{1,0:T(8,128)(2,1)}, bf16[522,768]{1,0:T(8,128)(2,1)S(1)}, u32[]{:S(2)}, u32[]{:S(2)}) collective-permute-start(bf16[522,768]{1,0:T(8,128)(2,1)} %get-tuple-element.1509), channel_id=1, source_target_pairs={{0,24},{8,0},{16,8},{24,16},{1,25},{9,1},{17,9},{25,17},{2,26},{10... | collective-permute-start | bytes 2405384 | tf_op jit(solution)/shard_map/while/body/eval_jaxpr/ppermute | solution.py:21
  2144.3 27.5 %collective-permute-start.1 = (bf16[522,768]{1,0:T(8,128)(2,1)}, bf16[522,768]{1,0:T(8,128)(2,1)S(1)}, u32[]{:S(2)}, u32[]{:S(2)}) collective-permute-start(bf16[522,768]{1,0:T(8,128)(2,1)} %get-tuple-element.1509), channel_id=1, source_target_pairs={{0,24},{8,0},{16,8},{24,16},{1,25},{9,1},{17,9},{25,17},{2,26},{10... | collective-permute-start | bytes 2405384 | tf_op jit(solution)/shard_map/while/body/eval_jaxpr/ppermute | solution.py:21
  2266.5 290.7 %all-to-all-start = ((bf16[4,2,512,768]{3,2,1,0:T(8,128)(2,1)}), bf16[4,2,512,768]{3,2,1,0:T(8,128)(2,1)}, u32[]{:S(2)}, u32[]{:S(2)}) async-start(bf16[4,2,512,768]{3,2,1,0:T(8,128)(2,1)} %get-tuple-element.965), calls=%async_computation | async-start | bytes 12582912 | tf_op jit(solution)/shard_map/all_to_all | solution.py:365
  2271.9 244.1 %reduce-scatter.4.cloned.1.call-start = ((), (), s32[]{:S(2)}) async-start(), calls=%async_computation.5 | async-start | bytes 491520
  2490.4 77.1 %collective-permute-start.3 = (bf16[1536,768]{1,0:T(8,128)(2,1)S(1)}, bf16[1536,768]{1,0:T(8,128)(2,1)}, u32[]{:S(2)}, u32[]{:S(2)}) collective-permute-start(bf16[1536,768]{1,0:T(8,128)(2,1)S(1)} %slice.156), channel_id=1, source_target_pairs={{8,0},{16,8},{24,16},{9,1},{17,9},{25,17},{10,2},{18,10},{26,18},{... | collective-permute-start | bytes 7077896 | tf_op jit(solution)/shard_map/ppermute | solution.py:16
  (172 other events, 2004.8 us)
Sparse Core Ops, SparseCore 0:
  9.6 62.2 all-gather.2
  73.4 50.1 all-gather.4
  2189.2 299.2 all-reduce.4
  2492.8 23.0 reduce-scatter.3
where the time goes:
time: 2600 us; the launch traced here: 2580 us
  matrix products  735 us (28%)
  other arithmetic  627 us (24%)
  local copies, waits for them, and re-layouts  477 us (18%)
  waiting for transfers between devices  294 us (11%)
  starting transfers between devices  200 us (8%)
  blocking collectives  134 us (5%)
  loops' own time  97.6 us (4%)
    psum x1, waiting for transfers between devices, body(): lax.psum(grad_proj.astype(jnp.bfloat16), 'dp').astype(jnp.float32)  217 us
    ppermute x22, starting transfers between devices, shifted(): lax.ppermute(shard, axis, [(i, (i + by) % count) for i in range(count)])  190 us
    sub x16, matrix products, attention_forward(): attn_probs = jax.nn.softmax(scores, axis=-1)  158 us
    dynamic_update_slice x33, other arithmetic, write_row(): lax.dynamic_update_index_in_dim(buffer, jnp.where(flag_value, new_rows, p...  125 us
    add x11, other arithmetic, backward_work(): grad_proj = grad_proj + grad_weights  122 us
    dot_general x16, matrix products, attention_forward(): jnp.einsum('hqk,khd->qhd', probs_low, value_rows, preferred_element_type=...  121 us
    add x11, other arithmetic, backward_work(): grad_down = grad_down + grad_second  119 us
    dot_general x8, matrix products, attention_backward(): jnp.einsum('qhd,khd->hqk', grad_mixed, value_rows, preferred_element_type...  114 us
  transfers between devices with their start and end apart: 29, of which 5 were waited for; matrix products, arithmetic and copies ran while one was open for 35% of the time, Pallas kernels for 0%

commit v1 on v0

v1 whole, which is shorter than its diff:
```python
import functools

import jax
import jax.numpy as jnp
from jax import lax
from jax.experimental import pallas as pl
from jax.experimental.pallas import tpu as pltpu
from jax.sharding import PartitionSpec as P

HEADS = 12
NORM_EPSILON = 1e-06
NEGATIVE = -1e30
BF16 = jnp.bfloat16
F32 = jnp.float32
VMEM_BYTES = 56 * 2**20
GROUP = 4
FF_BLOCK = 1024
SLOTS = 5
SPARE = 4

SWAP_CORE = [(0, 1), (1, 0), (2, 3), (3, 2)]
TO_SECOND = [(0, 2), (1, 3)]
TO_FIRST = [(2, 0), (3, 1)]


def mm(left, right, ca=1, cb=0):
    return lax.dot_general(
        left, right, (((ca,), (cb,)), ((), ())), preferred_element_type=F32
    )


def shape_of(shape, dtype=BF16):
    return jax.ShapeDtypeStruct(shape, dtype)


def whole(shape):
    return pl.BlockSpec(shape, lambda g, info: (0,) * len(shape))


def in_slot(rows, cols, moving=True):
    if moving:
        return pl.BlockSpec((None, rows, cols), lambda g, info: (info[0], 0, g))
    return pl.BlockSpec((None, rows, cols), lambda g, info: (info[0], 0, 0))


def staged_call(kernel, steps, info, inputs, in_specs, outs, scratch, stacks, name):
    stacked = [i for i, out in enumerate(outs) if out[3]]
    count = len(inputs)
    extra, aliases = [], {}
    if stacks is not None:
        for position, (index, stack) in enumerate(zip(stacked, stacks)):
            extra.append(stack)
            aliases[1 + count + position] = index

    def wrapped(info_ref, *refs):
        ins = refs[:count]
        rest = refs[count + len(extra):]
        kernel(info_ref, *ins, *rest)

    result = pl.pallas_call(
        wrapped,
        grid_spec=pltpu.PrefetchScalarGridSpec(
            num_scalar_prefetch=1,
            grid=(steps,),
            in_specs=list(in_specs) + [pl.BlockSpec(memory_space=pl.ANY)] * len(extra),
            out_specs=[out[2] for out in outs],
            scratch_shapes=scratch,
        ),
        out_shape=[shape_of(out[0], out[1]) for out in outs],
        input_output_aliases=aliases,
        compiler_params=pltpu.CompilerParams(vmem_limit_bytes=VMEM_BYTES),
        name=name,
    )(info, *inputs, *extra)
    kept = [result[i] for i in stacked]
    loose = [result[i] for i in range(len(outs)) if i not in stacked]
    return kept, loose


def normalise(summed):
    center = summed - jnp.mean(summed, axis=-1, keepdims=True)
    variance = jnp.mean(center * center, axis=-1, keepdims=True)
    inverse = lax.rsqrt(variance + NORM_EPSILON)
    return center * inverse, inverse


def finish_norm(summed, vec_ref, n_ref, r_ref, y_refs):
    normed, inverse = normalise(summed)
    n_ref[...] = normed.astype(BF16)
    r_ref[...] = jnp.broadcast_to(inverse, r_ref.shape)
    y = (normed * vec_ref[0:1, :] + vec_ref[1:2, :]).astype(BF16)
    for ref in y_refs:
        ref[...] = y


def attn_fwd_kernel(info_ref, x_ref, wq_ref, wk_ref, wv_ref, wo_ref, vec_ref, drow_ref, dcol_ref,
                    q_ref, k_ref, v_ref, p_ref, o_ref, n_ref, r_ref, y_ref, keep_ref,
                    bias_ref, acc_ref, *, head, group):
    step = pl.program_id(0)
    last = pl.num_programs(0) - 1

    @pl.when(info_ref[1] == 1)
    def _():
        @pl.when(step == 0)
        def _():
            rows = dcol_ref[:, 0:1]
            cols = drow_ref[...]
            allowed = ((rows == cols) | (rows < 0) | (cols == -1)) & (cols > -2)
            bias_ref[...] = jnp.where(allowed, 0.0, NEGATIVE)
            keep_ref[...] = x_ref[...]

        x = x_ref[...]
        scale = head ** (-0.5)
        q_ref[...] = mm(x, wq_ref[...]).astype(BF16)
        k_ref[...] = mm(x, wk_ref[...]).astype(BF16)
        v_ref[...] = mm(x, wv_ref[...]).astype(BF16)

        def score(h):
            cut = pl.ds(h * head, head)
            return mm(q_ref[:, cut] * scale, k_ref[:, cut], 1, 1) + bias_ref[...]

        s = score(0)
        for h in range(group):
            cut = pl.ds(h * head, head)
            following = score(h + 1) if h + 1 < group else None
            m = jnp.max(s, axis=-1, keepdims=True)
            e = jnp.exp(s - m)
            l = jnp.sum(e, axis=-1, keepdims=True)
            p = (e * (1.0 / l)).astype(BF16)
            p_ref[h] = p
            o_ref[:, cut] = mm(p, v_ref[:, cut]).astype(BF16)
            s = following
        part = mm(o_ref[...], wo_ref[...])

        @pl.when(step == 0)
        def _():
            acc_ref[...] = x.astype(F32) + part

        @pl.when(step > 0)
        def _():
            acc_ref[...] += part

        @pl.when(step == last)
        def _():
            finish_norm(acc_ref[...], vec_ref, n_ref, r_ref, [y_ref])


def attn_forward(info, x, weights, vec, drow, dcol, stacks):
    rows, width = x.shape
    head = width // HEADS
    cols = GROUP * head
    steps = HEADS // GROUP

    def wcols(part):
        return pl.BlockSpec((None, width, cols), lambda g, info: (0, 0, part * steps + g))

    stack = (SLOTS, rows, width)
    return staged_call(
        functools.partial(attn_fwd_kernel, head=head, group=GROUP), steps, info,
        [x, weights, weights, weights, weights, vec, drow, dcol],
        [whole((rows, width)), wcols(0), wcols(1), wcols(2),
         pl.BlockSpec((None, cols, width), lambda g, info: (0, g, 3)),
         whole((2, width)), whole((1, rows)), whole((rows, 128))],
        [(stack, BF16, in_slot(rows, cols), True)] * 3
        + [((SLOTS, HEADS, rows, rows), BF16,
            pl.BlockSpec((None, GROUP, rows, rows), lambda g, info: (info[0], g, 0, 0)), True),
           (stack, BF16, in_slot(rows, cols), True),
           (stack, BF16, in_slot(rows, width, False), True),
           ((SLOTS, rows, 128), F32, in_slot(rows, 128, False), True),
           (stack, BF16, in_slot(rows, width, False), True),
           (stack, BF16, in_slot(rows, width, False), True)],
        [pltpu.VMEM((rows, rows), F32), pltpu.VMEM((rows, width), F32)], stacks, "attn_fwd")


def gelu_parts(a):
    half = 0.5 * (1.0 + lax.erf(a * 0.7071067811865476))
    return a * half, half + a * jnp.exp(-0.5 * a * a) * 0.3989422804014327


def ff_fwd_kernel(info_ref, x_ref, w1_ref, w2_ref, vec_ref, h_ref, g_ref, n_ref, r_ref, y_ref, acc_ref):
    step = pl.program_id(0)
    last = pl.num_programs(0) - 1

    @pl.when(info_ref[1] == 1)
    def _():
        x = x_ref[...]
        act, slope = gelu_parts(mm(x, w1_ref[...]))
        h_ref[...] = act.astype(BF16)
        g_ref[...] = slope.astype(BF16)
        part = mm(h_ref[...], w2_ref[...])

        @pl.when(step == 0)
        def _():
            acc_ref[...] = x.astype(F32) + part

        @pl.when(step > 0)
        def _():
            acc_ref[...] += part

        @pl.when(step == last)
        def _():
            finish_norm(acc_ref[...], vec_ref, n_ref, r_ref, [y_ref])


def ff_forward(info, x, w1, w2, vec, stacks):
    _, rows, width = x.shape
    hidden = w1.shape[2]
    return staged_call(
        ff_fwd_kernel, hidden // FF_BLOCK, info, [x, w1, w2, vec],
        [in_slot(rows, width, False), pl.BlockSpec((None, width, FF_BLOCK), lambda g, info: (1, 0, g)),
         pl.BlockSpec((FF_BLOCK, width), lambda g, info: (g, 0)), whole((2, width))],
        [((SLOTS, rows, hidden), BF16, in_slot(rows, FF_BLOCK), True)] * 2
        + [((SLOTS, rows, width), BF16, in_slot(rows, width, False), True),
           ((SLOTS, rows, 128), F32, in_slot(rows, 128, False), True),
           ((rows, width), BF16, whole((rows, width)), False)],
        [pltpu.VMEM((rows, width), F32)], stacks, "ff_fwd")


def norm_back(g_ref, n_ref, r_ref, vec_ref, gv_ref):
    g = g_ref[...].astype(F32)
    n = n_ref[...].astype(F32)
    u = g * vec_ref[0:1, :]
    dz = r_ref[:, 0:1] * (u - jnp.mean(u, axis=-1, keepdims=True)
                          - n * jnp.mean(u * n, axis=-1, keepdims=True))
    gv_ref[0:1, :] = jnp.sum(g * n, axis=0, keepdims=True)
    gv_ref[1:2, :] = jnp.sum(g, axis=0, keepdims=True)
    return dz


def ff_bwd_kernel(info_ref, g_ref, n_ref, r_ref, vec_ref, slope_ref, w1_ref, w2_ref,
                  df_ref, da_ref, gv_ref, dx_ref, acc_ref):
    step = pl.program_id(0)
    last = pl.num_programs(0) - 1

    @pl.when(info_ref[1] == 1)
    def _():
        @pl.when(step == 0)
        def _():
            dz = norm_back(g_ref, n_ref, r_ref, vec_ref, gv_ref)
            df_ref[...] = dz.astype(BF16)
            acc_ref[...] = dz

        dh = mm(df_ref[...], w2_ref[...], 1, 1)
        da_ref[...] = (dh * slope_ref[...].astype(F32)).astype(BF16)
        acc_ref[...] += mm(da_ref[...], w1_ref[...], 1, 1)

        @pl.when(step == last)
        def _():
            dx_ref[...] = acc_ref[...].astype(BF16)


def ff_backward(info, g, n, r, vec, slope, w1, w2, stacks):
    rows, width = g.shape
    hidden = w1.shape[2]
    return staged_call(
        ff_bwd_kernel, hidden // FF_BLOCK, info, [g, n, r, vec, slope, w1, w2],
        [whole((rows, width)), in_slot(rows, width, False), in_slot(rows, 128, False), whole((2, width)),
         in_slot(rows, FF_BLOCK), pl.BlockSpec((None, width, FF_BLOCK), lambda g, info: (1, 0, g)),
         pl.BlockSpec((FF_BLOCK, width), lambda g, info: (g, 0))],
        [((SLOTS, rows, width), BF16, in_slot(rows, width, False), True),
         ((SLOTS, rows, hidden), BF16, in_slot(rows, FF_BLOCK), True),
         ((SLOTS, 2, width), F32, in_slot(2, width, False), True),
         ((rows, width), BF16, whole((rows, width)), False)],
        [pltpu.VMEM((rows, width), F32)], stacks, "ff_bwd")


def attn_bwd_kernel(info_ref, g_ref, n_ref, r_ref, vec_ref, q_ref, k_ref, v_ref, p_ref, o_ref,
                    wq_ref, wk_ref, wv_ref, wo_ref,
                    db_ref, dq_ref, dk_ref, dv_ref, gv_ref, dx_ref, acc_ref, do_ref, *, head, group):
    step = pl.program_id(0)
    last = pl.num_programs(0) - 1

    @pl.when(info_ref[1] == 1)
    def _():
        @pl.when(step == 0)
        def _():
            dz = norm_back(g_ref, n_ref, r_ref, vec_ref, gv_ref)
            db_ref[...] = dz.astype(BF16)
            acc_ref[...] = dz

        scale = head ** (-0.5)
        do_ref[...] = mm(db_ref[...], wo_ref[...], 1, 1).astype(BF16)

        def grad_probs(h):
            cut = pl.ds(h * head, head)
            return mm(do_ref[:, cut], v_ref[:, cut], 1, 1)

        dp = grad_probs(0)
        for h in range(group):
            cut = pl.ds(h * head, head)
            following = grad_probs(h + 1) if h + 1 < group else None
            do = do_ref[:, cut]
            p = p_ref[h]
            mean = jnp.sum(do.astype(F32) * o_ref[:, cut].astype(F32), axis=-1, keepdims=True)
            ds = (p.astype(F32) * (dp - mean)).astype(BF16)
            dv_ref[:, cut] = mm(p, do, 0, 0).astype(BF16)
            dq_ref[:, cut] = (mm(ds, k_ref[:, cut]) * scale).astype(BF16)
            dk_ref[:, cut] = (mm(ds, q_ref[:, cut], 0, 0) * scale).astype(BF16)
            dp = following
        acc_ref[...] += (mm(dq_ref[...], wq_ref[...], 1, 1) + mm(dk_ref[...], wk_ref[...], 1, 1)
                         + mm(dv_ref[...], wv_ref[...], 1, 1))

        @pl.when(step == last)
        def _():
            dx_ref[...] = acc_ref[...].astype(BF16)


def attn_backward(info, g, n, r, vec, q, k, v, p, o, weights, stacks):
    rows, width = g.shape
    head = width // HEADS
    cols = GROUP * head
    steps = HEADS // GROUP

    def wcols(part):
        return pl.BlockSpec((None, width, cols), lambda g, info: (0, 0, part * steps + g))

    stack = (SLOTS, rows, width)
    return staged_call(
        functools.partial(attn_bwd_kernel, head=head, group=GROUP), steps, info,
        [g, n, r, vec, q, k, v, p, o, weights, weights, weights, weights],
        [whole((rows, width)), in_slot(rows, width, False), in_slot(rows, 128, False), whole((2, width)),
         in_slot(rows, cols), in_slot(rows, cols), in_slot(rows, cols),
         pl.BlockSpec((None, GROUP, rows, rows), lambda g, info: (info[0], g, 0, 0)), in_slot(rows, cols),
         wcols(0), wcols(1), wcols(2), pl.BlockSpec((None, cols, width), lambda g, info: (0, g, 3))],
        [(stack, BF16, in_slot(rows, width, False), True)]
        + [(stack, BF16, in_slot(rows, cols), True)] * 3
        + [((SLOTS, 2, width), F32, in_slot(2, width, False), True),
           ((rows, width), BF16, whole((rows, width)), False)],
        [pltpu.VMEM((rows, width), F32), pltpu.VMEM((rows, cols), BF16)], stacks, "attn_bwd")


def grad_kernel(left_ref, right_ref, out_ref):
    left = left_ref[...].reshape(-1, left_ref.shape[2])
    right = right_ref[...].reshape(-1, right_ref.shape[2])
    out_ref[...] = mm(left, right, 0, 0).astype(out_ref.dtype)


def weight_grad(left, right, lblock, rblock):
    _, rows, wide = left.shape
    cols = right.shape[2]
    return pl.pallas_call(
        grad_kernel,
        grid=(wide // lblock, cols // rblock),
        in_specs=[pl.BlockSpec((SPARE, rows, lblock), lambda i, j: (0, 0, i)),
                  pl.BlockSpec((SPARE, rows, rblock), lambda i, j: (0, 0, j))],
        out_specs=pl.BlockSpec((lblock, rblock), lambda i, j: (i, j)),
        out_shape=shape_of((wide, cols)),
        compiler_params=pltpu.CompilerParams(vmem_limit_bytes=VMEM_BYTES),
        name="weight_grad",
    )(left, right)


def body(tokens, doc_ids, reset_flags, memory_init, w_proj, vectors, w_down, cotangent):
    data_count = lax.axis_size("dp")
    section = lax.axis_index("section")
    data = lax.axis_index("dp")
    stage = section // 2
    core = section % 2
    first = stage == 0
    _, segments, seg_tokens, width = tokens.shape
    memory_count = memory_init.shape[0]
    pad = -(memory_count + seg_tokens) % 16
    rows = seg_tokens + memory_count + pad
    pairs = [[0, 1], [2, 3]]

    proj = lax.all_gather(w_proj[0], "section", axis=0, axis_index_groups=pairs)
    down = lax.all_gather(w_down, "section", axis=0, tiled=True, axis_index_groups=pairs)
    vecs = lax.all_gather(vectors[0], "section", axis=0, axis_index_groups=pairs)

    def send(block, route):
        return lax.ppermute(block, "section", route)

    other_tokens = [send(tokens[0, k], TO_FIRST) for k in range(segments)]
    other_cot = [send(cotangent[0, k], TO_SECOND) for k in range(segments)]
    item_a = core * data_count + data
    item_b = (core + 2) * data_count + data
    micros = [(item, k) for k in range(segments) for item in (0, 1)]
    items = (item_a, item_b)
    micro_docs = []
    for item, k in micros:
        docs = lax.dynamic_index_in_dim(doc_ids, items[item], 0, keepdims=False)[k]
        micro_docs.append(jnp.concatenate(
            [docs, jnp.full((memory_count,), -1, jnp.int32), jnp.full((pad,), -2, jnp.int32)]))
    flags = [lax.dynamic_index_in_dim(reset_flags, items[i], 0, keepdims=False) for i in (0, 1)]
    pad_rows = jnp.zeros((pad, width), BF16)

    def fresh(item, k):
        return jnp.bool_(True) if k == 0 else flags[item][k] == 1

    def pick(choice, yes, no):
        return jnp.where(choice, yes, no)

    count = len(micros)
    attn_stacks = ff_stacks = None
    carried = jnp.zeros((rows, width), BF16)
    memory_back = {}
    outs = {}
    for tick in range(count + 1):
        here = min(tick, count - 1)
        item, k = micros[here]
        valid = pick(first, tick < count, tick > 0).astype(jnp.int32)
        slot = pick(first, tick, tick - 1)
        slot = pick(valid == 1, slot, SPARE)
        info = jnp.stack([slot, valid]).astype(jnp.int32)
        if k == 0:
            entering = memory_init
        else:
            entering = pick(fresh(item, k), memory_init, memory_back[(item, k - 1)][:memory_count])
        rows_in = tokens[0, k] if item == 0 else other_tokens[k]
        start = jnp.concatenate([rows_in, entering, pad_rows], axis=0)
        x = pick(first, start, carried)
        docs = pick(first, micro_docs[here], micro_docs[max(tick - 1, 0)])
        drow = docs[None, :]
        dcol = jnp.broadcast_to(docs[:, None], (rows, 128))
        attn_stacks, _ = attn_forward(info, x, proj, vecs[0], drow, dcol, attn_stacks)
        ff_stacks, (y,) = ff_forward(info, attn_stacks[7], proj, down, vecs[1], ff_stacks)
        if tick < count:
            carried = send(y, TO_SECOND)
        if tick > 0:
            done = micros[tick - 1]
            if done[1] + 1 < segments:
                memory_back[done] = send(y[seg_tokens:], TO_FIRST)
            outs[done] = y[:seg_tokens]
    q, k_rows, v, p, o, n1, r1, y1, x_in = attn_stacks
    h, slope, n2, r2 = ff_stacks

    order = [m for k in reversed(range(segments)) for m in range(count) if micros[m][1] == k]
    ffb_stacks = ab_stacks = None
    returning = jnp.zeros((rows, width), BF16)
    memory_forward = {}
    grads = {}
    grad_memory = jnp.zeros((memory_count, width), F32)
    for tick in range(count + 1):
        mine = order[min(tick, count - 1)]
        before = order[max(tick - 1, 0)]
        item, k = micros[mine]
        valid = pick(first, tick > 0, tick < count).astype(jnp.int32)
        slot = pick(valid == 1, pick(first, before, mine), SPARE)
        info = jnp.stack([slot, valid]).astype(jnp.int32)
        if k + 1 < segments:
            memory_grad = memory_forward[(item, k + 1)]
        else:
            memory_grad = jnp.zeros((rows - seg_tokens, width), BF16)
        rows_in = cotangent[0, k] if item == 1 else other_cot[k]
        start = jnp.concatenate([rows_in, memory_grad], axis=0)
        g = pick(first, returning, start)
        ffb_stacks, (dy,) = ff_backward(info, g, n2, r2, vecs[1], slope, proj, down, ffb_stacks)
        ab_stacks, (dx,) = attn_backward(info, dy, n1, r1, vecs[0], q, k_rows, v, p, o, proj, ab_stacks)
        if tick < count:
            returning = send(dx, TO_FIRST)
        if tick > 0:
            done = micros[before]
            grads[done] = dx[:seg_tokens]
            is_fresh = fresh(*done)
            memory_rows = dx[seg_tokens:]
            if done[1] > 0:
                memory_forward[done] = send(pick(is_fresh, jnp.zeros_like(memory_rows), memory_rows), TO_SECOND)
            grad_memory = grad_memory + pick(
                first & is_fresh, memory_rows[:memory_count].astype(F32), 0.0)
    df, da, gv2 = ffb_stacks
    db, dq, dk, dv, gv1 = ab_stacks

    vec_pair = jnp.stack([gv1[:SPARE].sum(axis=0), gv2[:SPARE].sum(axis=0)])
    small = jnp.zeros((4, 2, width), F32)
    small = lax.dynamic_update_slice(small, vec_pair, (stage * 2, 0, 0))
    small = jnp.concatenate([small.reshape(8, width), grad_memory], axis=0)
    small = lax.psum(small, ("section", "dp"))
    total_vec = lax.dynamic_slice(small[:8].reshape(4, 2, width), (section, 0, 0), (1, 2, width))
    share = width // 4
    memory_total = lax.dynamic_slice(small[8:], (0, section * share), (memory_count, share))

    grad_ff1 = weight_grad(y1, da, width, 512)
    grad_ff2 = weight_grad(h, df, 512, width)
    grad_attn = jnp.concatenate(
        [weight_grad(x_in, dq, width, 384), weight_grad(x_in, dk, width, 384),
         weight_grad(x_in, dv, width, 384), weight_grad(o, db, width, 384)], axis=1)
    low = core == 0
    half = w_down.shape[0]
    got_proj = send(pick(low, grad_ff1, grad_attn), SWAP_CORE)
    got_down = send(pick(low, grad_ff2[half:], grad_ff2[:half]), SWAP_CORE)
    my_proj = (pick(low, grad_attn, grad_ff1).astype(F32) + got_proj.astype(F32)).astype(BF16)
    my_down = (pick(low, grad_ff2[:half], grad_ff2[half:]).astype(F32) + got_down.astype(F32)).astype(BF16)
    total_proj = lax.psum(my_proj, "dp").astype(F32)
    total_down = lax.psum(my_down, "dp").astype(F32)

    def collect(done, table, route, keep_first):
        item_own, item_other = (0, 1) if keep_first else (1, 0)
        blocks = []
        for k in range(segments):
            if keep_first:
                got = send(table[(1, k)], route)
                blocks.append(pick(first, table[(0, k)], got))
            else:
                got = send(table[(0, k)], route)
                blocks.append(pick(first, got, table[(1, k)]))
        return jnp.stack(blocks)[None]

    block_rows = collect(None, outs, TO_FIRST, False)
    input_rows = collect(None, grads, TO_SECOND, True)
    return (block_rows, input_rows, total_proj[None], total_vec, total_down, memory_total)


def solution(mesh):
    items = P(("section", "dp"), None, None, None)
    return jax.shard_map(
        body,
        mesh=mesh,
        in_specs=(items, P(), P(), P(), P("section", None, None), P("section", None, None),
                  P("section", None), items),
        out_specs=(items, items, P("section", None, None), P("section", None, None),
                   P("section", None), P(None, "section")),
        check_vma=False,
    )
```

time: 2600 us -> 908 us (0.35)
  matrix products: 735 us -> 0 us
  other arithmetic: 627 us -> 56.7 us
  local copies, waits for them, and re-layouts: 477 us -> 17 us
  Pallas kernels: 0 us -> 387 us
  starting transfers between devices: 200 us -> 50.6 us
  loops' own time: 97.6 us -> 0 us
  blocking collectives: 134 us -> 56.2 us
    dot_general x112 -> x0, matrix products: 576 us -> none  [the longest x16 121 us: attention_forward(): jnp.einsum('hqk,khd->qhd', probs_low, value_rows, preferred_element_type=...]
    pallas_call x0 -> x26, Pallas kernels: none -> 387 us  [the longest x20 326 us: staged_call(): pl.pallas_call(wrapped, grid_spec=pltpu.PrefetchScalarGridSpec(num_scalar...]
    add x44 -> x1, other arithmetic: 250 us -> 0.77 us  [body(): grad_memory + pick(first & is_fresh, memory_rows[:memory_count].astype(F3...]
    dynamic_update_slice x55 -> x1, other arithmetic: 164 us -> 0.02 us  [body(): small = lax.dynamic_update_slice(small, vec_pair, (stage * 2, 0, 0))]
    dynamic_slice x93 -> x3, local copies, waits for them, and re-layouts: 165 us -> 1.36 us  [the longest x1 0.68 us: body(): lax.dynamic_slice(small[8:], (0, section * share), (memory_count, share))]
    sub x16 -> x0, matrix products: 158 us -> none  [attention_forward(): attn_probs = jax.nn.softmax(scores, axis=-1)]
    ppermute x24 -> x22, starting transfers between devices: 195 us -> 50.5 us  [send(): return lax.ppermute(block, 'section', route)]
    ppermute x24 -> x22, waiting for transfers between devices: 21.6 us -> 164 us  [send(): return lax.ppermute(block, 'section', route)]
  transfers between devices with their start and end apart: 29 -> 25, of which waited for: 5 -> 16; matrix products, arithmetic and copies ran while one was open for 35% -> 4% of each run, Pallas kernels for 0% -> 7%
where the time goes in v1:
time: 908 us; the launch traced here: 899 us
  Pallas kernels  387 us (43%)
  waiting for transfers between devices  316 us (35%)
  other arithmetic  56.7 us (6%)
  blocking collectives  56.2 us (6%)
  starting transfers between devices  50.6 us (6%)
  local copies, waits for them, and re-layouts  17 us (2%)
  between operations  15.9 us (2%)
    pallas_call x20, Pallas kernels, staged_call(): pl.pallas_call(wrapped, grid_spec=pltpu.PrefetchScalarGridSpec(num_scalar...  326 us
    ppermute x22, waiting for transfers between devices, send(): return lax.ppermute(block, 'section', route)  164 us
    psum x1, waiting for transfers between devices, body(): total_proj = lax.psum(my_proj, 'dp').astype(F32)  132 us
    pallas_call x6, Pallas kernels, weight_grad(): pl.pallas_call(grad_kernel, grid=(wide // lblock, cols // rblock), in_spe...  60.7 us
    psum x1, blocking collectives, body(): small = lax.psum(small, ('section', 'dp'))  54.2 us
    ppermute x22, starting transfers between devices, send(): return lax.ppermute(block, 'section', route)  50.5 us
    select_n x17, other arithmetic, pick(): return jnp.where(choice, yes, no)  24.6 us
    all_gather x1, waiting for transfers between devices, body(): proj = lax.all_gather(w_proj[0], 'section', axis=0, axis_index_groups=pairs)  18.8 us
  transfers between devices with their start and end apart: 25, of which 16 were waited for; matrix products, arithmetic and copies ran while one was open for 4% of the time, Pallas kernels for 7%

profile of v1, /device:TPU:0, one launch (start us, length us, event | category | flops | bytes accessed | tf_op | source)
XLA Modules:
  0.0 899.4 jit_solution(3305041711019966181)
XLA Ops:
  15.4 18.8 %all-gather.3.cloned.1.call-done.refs_1_.refs_2_.refs_3_.refs_4_.refs_5_.refs_9_.refs_10_.refs_11_.refs_12_ = bf16[2,768,3072]{2,1,0:T(8,128)(2,1)} async-done(((bf16[1,768,3072]{2,1,0:T(8,128)(2,1)}), bf16[2,768,3072]{2,1,0:T(8,128)(2,1)}) %all-gather.3.cloned.1.call-update) | async-done | bytes 9437200 | tf_op jit(solution)/shard_map/all_gather | solution.py:365
  35.0 18.7 %attn_fwd.5 = (bf16[5,528,768]{2,1,0:T(8,128)(2,1)}, bf16[5,528,768]{2,1,0:T(8,128)(2,1)}, bf16[5,528,768]{2,1,0:T(8,128)(2,1)}, bf16[5,12,528,528]{3,2,1,0:T(8,...) custom-call(s32[2]{0:T(128)} %pad_add_fusion.14.info_ref, ...), custom_call_target="tpu_custom_call" | custom-call | tf_op jit(solution)/shard_map/attn_fwd/pallas_call | solution.py:60
  53.7 13.2 %ff_fwd.5 = (bf16[5,528,3072]{2,1,0:T(8,128)(2,1)}, bf16[5,528,3072]{2,1,0:T(8,128)(2,1)}, bf16[5,528,768]{2,1,0:T(8,128)(2,1)}, f32[5,528,128]{2,1,0:T(8,128)}, bf16[528,768]{1,0:T(8,128)(2,1)}) custom-call(s32[2]{0:T(128)} %pad_add_fusion.14.info_ref, bf16[5,528,768]{2,1,0:T(8,128)(2,1)} %get-tuple-element.126.refs_0_.refs_15_, ...), custom_call_target="tpu_custom_call" | custom-call | tf_op jit(solution)/shard_map/ff_fwd/pallas_call | solution.py:60
  71.1 18.8 %collective-permute-done = bf16[512,768]{1,0:T(8,128)(2,1)} collective-permute-done((bf16[512,768]{1,0:T(8,128)(2,1)S(1)}, bf16[512,768]{1,0:T(8,128)(2,1)}, u32[]{:S(2)}, u32[]{:S(2)}) %collective-permute-start) | collective-permute-done | bytes 786464 | tf_op jit(solution)/shard_map/ppermute | solution.py:370
  93.1 18.7 %attn_fwd.6 = (bf16[5,528,768]{2,1,0:T(8,128)(2,1)}, bf16[5,528,768]{2,1,0:T(8,128)(2,1)}, bf16[5,528,768]{2,1,0:T(8,128)(2,1)}, bf16[5,12,528,528]{3,2,1,0:T(8,...) custom-call(s32[2]{0:T(128)} %pad_add_fusion.13.info_ref, ...), custom_call_target="tpu_custom_call", output_to_operand_aliasing={{0}: (9, {}), {1}: (10, {}), {2}: (11, {}), {3}: (12, {}), ... | custom-call | tf_op jit(solution)/shard_map/attn_fwd/pallas_call | solution.py:60
  111.8 13.2 %ff_fwd.6 = (bf16[5,528,3072]{2,1,0:T(8,128)(2,1)}, bf16[5,528,3072]{2,1,0:T(8,128)(2,1)}, bf16[5,528,768]{2,1,0:T(8,128)(2,1)}, f32[5,528,128]{2,1,0:T(8,128)}, bf16[528,768]{1,0:T(8,128)(2,1)}) custom-call(s32[2]{0:T(128)} %pad_add_fusion.13.info_ref, ...), custom_call_target="tpu_custom_call", output_to_operand_aliasing={{0}: (5, {}), {1}: (6, {}), {2}: (7, {}), {3}: (8, {})} | custom-call | tf_op jit(solution)/shard_map/ff_fwd/pallas_call | solution.py:60
  145.8 18.7 %attn_fwd.7 = (bf16[5,528,768]{2,1,0:T(8,128)(2,1)}, bf16[5,528,768]{2,1,0:T(8,128)(2,1)}, bf16[5,528,768]{2,1,0:T(8,128)(2,1)}, bf16[5,12,528,528]{3,2,1,0:T(8,...) custom-call(s32[2]{0:T(128)} %pad_add_fusion.12.info_ref, ...), custom_call_target="tpu_custom_call", output_to_operand_aliasing={{0}: (9, {}), {1}: (10, {}), {2}: (11, {}), {3}: (12, {}), ... | custom-call | tf_op jit(solution)/shard_map/attn_fwd/pallas_call | solution.py:60
  164.4 13.3 %ff_fwd.7 = (bf16[5,528,3072]{2,1,0:T(8,128)(2,1)}, bf16[5,528,3072]{2,1,0:T(8,128)(2,1)}, bf16[5,528,768]{2,1,0:T(8,128)(2,1)}, f32[5,528,128]{2,1,0:T(8,128)}, bf16[528,768]{1,0:T(8,128)(2,1)}) custom-call(s32[2]{0:T(128)} %pad_add_fusion.12.info_ref, ...), custom_call_target="tpu_custom_call", output_to_operand_aliasing={{0}: (5, {}), {1}: (6, {}), {2}: (7, {}), {3}: (8, {})} | custom-call | tf_op jit(solution)/shard_map/ff_fwd/pallas_call | solution.py:60
  204.5 18.7 %attn_fwd.8 = (bf16[5,528,768]{2,1,0:T(8,128)(2,1)}, bf16[5,528,768]{2,1,0:T(8,128)(2,1)}, bf16[5,528,768]{2,1,0:T(8,128)(2,1)}, bf16[5,12,528,528]{3,2,1,0:T(8,...) custom-call(s32[2]{0:T(128)} %pad_add_fusion.11.info_ref, ...), custom_call_target="tpu_custom_call", output_to_operand_aliasing={{0}: (9, {}), {1}: (10, {}), {2}: (11, {}), {3}: (12, {}), ... | custom-call | tf_op jit(solution)/shard_map/attn_fwd/pallas_call | solution.py:60
  223.1 13.1 %ff_fwd.8 = (bf16[5,528,3072]{2,1,0:T(8,128)(2,1)}, bf16[5,528,3072]{2,1,0:T(8,128)(2,1)}, bf16[5,528,768]{2,1,0:T(8,128)(2,1)}, f32[5,528,128]{2,1,0:T(8,128)}, bf16[528,768]{1,0:T(8,128)(2,1)}) custom-call(s32[2]{0:T(128)} %pad_add_fusion.11.info_ref, ...), custom_call_target="tpu_custom_call", output_to_operand_aliasing={{0}: (5, {}), {1}: (6, {}), {2}: (7, {}), {3}: (8, {})} | custom-call | tf_op jit(solution)/shard_map/ff_fwd/pallas_call | solution.py:60
  292.3 53.1 %collective-permute-done.11 = bf16[528,768]{1,0:T(8,128)(2,1)S(1)} collective-permute-done((bf16[528,768]{1,0:T(8,128)(2,1)}, bf16[528,768]{1,0:T(8,128)(2,1)S(1)}, u32[]{:S(2)}, u32[]{:S(2)}) %collective-permute-start.11) | collective-permute-done | bytes 811040 | tf_op jit(solution)/shard_map/ppermute | solution.py:370
  346.5 13.6 %ff_bwd.6 = (bf16[5,528,768]{2,1,0:T(8,128)(2,1)}, bf16[5,528,3072]{2,1,0:T(8,128)(2,1)}, f32[5,2,768]{2,1,0:T(2,128)}, bf16[528,768]{1,0:T(8,128)(2,1)}) custom-call(s32[2]{0:T(128)} %pad_add_fusion.8.info_ref, bf16[528,768]{1,0:T(8,128)(2,1)} %pad_select_fusion.refs_0_, ...), custom_call_target="tpu_custom_call", output_to_operand_aliasing={{0}: (8, {}), {1}: (9, {}), {2}: (10, {})} | custom-call | tf_op jit(solution)/shard_map/ff_bwd/pallas_call | solution.py:60
  360.1 27.6 %attn_bwd.6 = (bf16[5,528,768]{2,1,0:T(8,128)(2,1)}, bf16[5,528,768]{2,1,0:T(8,128)(2,1)}, bf16[5,528,768]{2,1,0:T(8,128)(2,1)}, bf16[5,528,768]{2,1,0:T(8,128)(...) custom-call(s32[2]{0:T(128)} %pad_add_fusion.8.info_ref, ...), custom_call_target="tpu_custom_call", output_to_operand_aliasing={{0}: (14, {}), {1}: (15, {}), {2}: (16, {}), {3}: (17, {}),... | custom-call | tf_op jit(solution)/shard_map/attn_bwd/pallas_call | solution.py:60
  406.7 13.2 %ff_bwd.7 = (bf16[5,528,768]{2,1,0:T(8,128)(2,1)}, bf16[5,528,3072]{2,1,0:T(8,128)(2,1)}, f32[5,2,768]{2,1,0:T(2,128)}, bf16[528,768]{1,0:T(8,128)(2,1)}) custom-call(s32[2]{0:T(128)} %pad_add_fusion.9.info_ref, bf16[528,768]{1,0:T(8,128)(2,1)} %maximum_select_fusion.1.refs_0_, ...), custom_call_target="tpu_custom_call", output_to_operand_aliasing={{0}: (8, {}), {1}: (9, {}), {2}: (10, {})} | custom-call | tf_op jit(solution)/shard_map/ff_bwd/pallas_call | solution.py:60
  419.9 27.4 %attn_bwd.7 = (bf16[5,528,768]{2,1,0:T(8,128)(2,1)}, bf16[5,528,768]{2,1,0:T(8,128)(2,1)}, bf16[5,528,768]{2,1,0:T(8,128)(2,1)}, bf16[5,528,768]{2,1,0:T(8,128)(...) custom-call(s32[2]{0:T(128)} %pad_add_fusion.9.info_ref, ...), custom_call_target="tpu_custom_call", output_to_operand_aliasing={{0}: (14, {}), {1}: (15, {}), {2}: (16, {}), {3}: (17, {}),... | custom-call | tf_op jit(solution)/shard_map/attn_bwd/pallas_call | solution.py:60
  464.1 13.3 %ff_bwd.8 = (bf16[5,528,768]{2,1,0:T(8,128)(2,1)}, bf16[5,528,3072]{2,1,0:T(8,128)(2,1)}, f32[5,2,768]{2,1,0:T(2,128)}, bf16[528,768]{1,0:T(8,128)(2,1)}) custom-call(s32[2]{0:T(128)} %pad_add_fusion.10.info_ref, bf16[528,768]{1,0:T(8,128)(2,1)} %broadcast_select_fusion.3.refs_0_, ...), custom_call_target="tpu_custom_call", output_to_operand_aliasing={{0}: (8, {}), {1}: (9, {}), {2}: (10, {})} | custom-call | tf_op jit(solution)/shard_map/ff_bwd/pallas_call | solution.py:60
  477.4 27.3 %attn_bwd.8 = (bf16[5,528,768]{2,1,0:T(8,128)(2,1)}, bf16[5,528,768]{2,1,0:T(8,128)(2,1)}, bf16[5,528,768]{2,1,0:T(8,128)(2,1)}, bf16[5,528,768]{2,1,0:T(8,128)(...) custom-call(s32[2]{0:T(128)} %pad_add_fusion.10.info_ref, ...), custom_call_target="tpu_custom_call", output_to_operand_aliasing={{0}: (14, {}), {1}: (15, {}), {2}: (16, {}), {3}: (17, {}),... | custom-call | tf_op jit(solution)/shard_map/attn_bwd/pallas_call | solution.py:60
  520.7 13.7 %ff_bwd.9 = (bf16[5,528,768]{2,1,0:T(8,128)(2,1)}, bf16[5,528,3072]{2,1,0:T(8,128)(2,1)}, f32[5,2,768]{2,1,0:T(2,128)}, bf16[528,768]{1,0:T(8,128)(2,1)}) custom-call(s32[2]{0:T(128)} %pad_add_fusion.17.info_ref, bf16[528,768]{1,0:T(8,128)(2,1)} %broadcast_select_fusion.2.refs_0_, ...), custom_call_target="tpu_custom_call", output_to_operand_aliasing={{0}: (8, {}), {1}: (9, {}), {2}: (10, {})} | custom-call | tf_op jit(solution)/shard_map/ff_bwd/pallas_call | solution.py:60
  534.4 27.4 %attn_bwd.9 = (bf16[5,528,768]{2,1,0:T(8,128)(2,1)}, bf16[5,528,768]{2,1,0:T(8,128)(2,1)}, bf16[5,528,768]{2,1,0:T(8,128)(2,1)}, bf16[5,528,768]{2,1,0:T(8,128)(...) custom-call(s32[2]{0:T(128)} %pad_add_fusion.17.info_ref, ...), custom_call_target="tpu_custom_call", output_to_operand_aliasing={{0}: (14, {}), {1}: (15, {}), {2}: (16, {}), {3}: (17, {}),... | custom-call | tf_op jit(solution)/shard_map/attn_bwd/pallas_call | solution.py:60
  590.9 15.8 %weight_grad.10 = bf16[768,3072]{1,0:T(8,128)(2,1)} custom-call(bf16[5,528,768]{2,1,0:T(8,128)(2,1)} %get-tuple-element.178.refs_0_.left_ref, bf16[5,528,3072]{2,1,0:T(8,128)(2,1)} %get-tuple-element.241.right_ref), custom_call_target="tpu_custom_call" | custom-call | tf_op jit(solution)/shard_map/weight_grad/pallas_call | solution.py:340
  612.8 15.8 %weight_grad.11 = bf16[3072,768]{1,0:T(8,128)(2,1)} custom-call(bf16[5,528,3072]{2,1,0:T(8,128)(2,1)} %get-tuple-element.244.left_ref, bf16[5,528,768]{2,1,0:T(8,128)(2,1)} %get-tuple-element.245.right_ref), custom_call_target="tpu_custom_call" | custom-call | tf_op jit(solution)/shard_map/weight_grad/pallas_call | solution.py:340
  671.0 15.0 %collective-permute-done.8 = bf16[512,768]{1,0:T(8,128)(2,1)S(1)} collective-permute-done((bf16[512,768]{1,0:T(8,128)(2,1)}, bf16[512,768]{1,0:T(8,128)(2,1)S(1)}, u32[]{:S(2)}, u32[]{:S(2)}) %collective-permute-start.8) | collective-permute-done | bytes 786464 | tf_op jit(solution)/shard_map/ppermute | solution.py:370
  694.0 54.2 %psum.22 = f32[18,768]{1,0:T(8,128)S(1)} all-reduce(f32[18,768]{1,0:T(8,128)S(1)} %pad_maximum_fusion.4), channel_id=1, replica_groups=mesh['section'=4,'dp'=8] {'section','dp'}, use_global_device_ids=true, to_apply=%region_3.4 | all-reduce | flops 13824 | bytes 110592 | tf_op jit(solution)/shard_map/psum | solution.py:466
  751.0 131.6 %all-reduce.5.cloned.1.call-done = (bf16[1,768,3072]{2,1,0:T(8,128)(2,1)}, bf16[1536,768]{1,0:T(8,128)(2,1)}) async-done(((bf16[1,768,3072]{2,1,0:T(8,128)(2,1)}, bf16[1536,768]{1,0:T(8,128)(2,1)}), (bf16[1,768,3072]{2,1,0:T(8,128)(2,1)}, bf16[1536,768]{1,0:T(8,128)(2,1)})) %all-reduce.5.cloned.1.call-update) | async-done | bytes 7077904 | tf_op jit(solution)/shard_map/psum | solution.py:482
  (182 shorter events, 269.2 us)
Async XLA Ops:
  7.2 27.0 %all-gather.3.cloned.1.call-start = ((), (), s32[]{:S(2)}) async-start(), calls=%async_computation | async-start | bytes 14155776 | tf_op jit(solution)/shard_map/all_gather | solution.py:365
  7.9 45.8 %all-gather.5.cloned.1.call-start = ((), (), s32[]{:S(2)}) async-start(), calls=%async_computation.1 | async-start | bytes 7077888 | tf_op jit(solution)/shard_map/all_gather | solution.py:366
  8.7 873.9 %all-reduce.5.cloned.1.call-start = ((), (), s32[]{:S(2)}) async-start(), calls=%async_computation.2 | async-start | bytes 14155776 | tf_op jit(solution)/shard_map/psum | solution.py:482
  66.9 23.0 %collective-permute-start.1 = (bf16[528,768]{1,0:T(8,128)(2,1)}, bf16[528,768]{1,0:T(8,128)(2,1)S(1)}, u32[]{:S(2)}, u32[]{:S(2)}) collective-permute-start(bf16[528,768]{1,0:T(8,128)(2,1)} %get-tuple-element.127), channel_id=1, source_target_pairs={{0,16},{8,24},{1,17},{9,25},{2,18},{10,26},{3,19},{11,27},{4,20},{... | collective-permute-start | bytes 2433032 | tf_op jit(solution)/shard_map/ppermute | solution.py:370
  68.2 21.7 %collective-permute-start = (bf16[512,768]{1,0:T(8,128)(2,1)S(1)}, bf16[512,768]{1,0:T(8,128)(2,1)}, u32[]{:S(2)}, u32[]{:S(2)}) collective-permute-start(bf16[512,768]{1,0:T(8,128)(2,1)S(1)} %get-tuple-element.251), channel_id=1, source_target_pairs={{16,0},{24,8},{17,1},{25,9},{18,2},{26,10},{19,3},{27,11},{20,4},{... | collective-permute-start | bytes 2359304 | tf_op jit(solution)/shard_map/ppermute | solution.py:370
  125.0 18.8 %collective-permute-start.4 = (bf16[528,768]{1,0:T(8,128)(2,1)}, bf16[528,768]{1,0:T(8,128)(2,1)S(1)}, u32[]{:S(2)}, u32[]{:S(2)}) collective-permute-start(bf16[528,768]{1,0:T(8,128)(2,1)} %get-tuple-element.141), channel_id=1, source_target_pairs={{0,16},{8,24},{1,17},{9,25},{2,18},{10,26},{3,19},{11,27},{4,20},{... | collective-permute-start | bytes 2433032 | tf_op jit(solution)/shard_map/ppermute | solution.py:370
  127.2 5.7 collective-permute-start.3
  177.8 24.6 %collective-permute-start.7 = (bf16[528,768]{1,0:T(8,128)(2,1)}, bf16[528,768]{1,0:T(8,128)(2,1)S(1)}, u32[]{:S(2)}, u32[]{:S(2)}) collective-permute-start(bf16[528,768]{1,0:T(8,128)(2,1)} %get-tuple-element.155), channel_id=1, source_target_pairs={{0,16},{8,24},{1,17},{9,25},{2,18},{10,26},{3,19},{11,27},{4,20},{... | collective-permute-start | bytes 2433032 | tf_op jit(solution)/shard_map/ppermute | solution.py:370
  182.1 20.3 %collective-permute-start.5 = (bf16[512,768]{1,0:T(8,128)(2,1)S(1)}, bf16[512,768]{1,0:T(8,128)(2,1)S(1)}, u32[]{:S(2)}, u32[]{:S(2)}) collective-permute-start(bf16[512,768]{1,0:T(8,128)(2,1)S(1)} %get-tuple-element.250), channel_id=1, source_target_pairs={{16,0},{24,8},{17,1},{25,9},{18,2},{26,10},{19,3},{27,11},{20,4},{... | collective-permute-start | bytes 2359304 | tf_op jit(solution)/shard_map/ppermute | solution.py:370
  184.4 56.8 %collective-permute-start.10 = (bf16[512,768]{1,0:T(8,128)(2,1)S(1)}, bf16[512,768]{1,0:T(8,128)(2,1)}, u32[]{:S(2)}, u32[]{:S(2)}) collective-permute-start(bf16[512,768]{1,0:T(8,128)(2,1)S(1)} %get-tuple-element.249), channel_id=1, source_target_pairs={{0,16},{8,24},{1,17},{9,25},{2,18},{10,26},{3,19},{11,27},{4,20},{... | collective-permute-start | bytes 2359304 | tf_op jit(solution)/shard_map/ppermute | solution.py:370
  190.6 11.8 %collective-permute-start.6 = (bf16[16,768]{1,0:T(8,128)(2,1)S(1)}, bf16[16,768]{1,0:T(8,128)(2,1)S(1)}, u32[]{:S(2)}, u32[]{:S(2)}) collective-permute-start(bf16[16,768]{1,0:T(8,128)(2,1)S(1)} %slice.162), channel_id=1, source_target_pairs={{16,0},{24,8},{17,1},{25,9},{18,2},{26,10},{19,3},{27,11},{20,4},{... | collective-permute-start | bytes 73736 | tf_op jit(solution)/shard_map/ppermute | solution.py:370
  236.3 16.9 %collective-permute-start.9 = (bf16[528,768]{1,0:T(8,128)(2,1)}, bf16[528,768]{1,0:T(8,128)(2,1)S(1)}, u32[]{:S(2)}, u32[]{:S(2)}) collective-permute-start(bf16[528,768]{1,0:T(8,128)(2,1)} %get-tuple-element.169), channel_id=1, source_target_pairs={{0,16},{8,24},{1,17},{9,25},{2,18},{10,26},{3,19},{11,27},{4,20},{... | collective-permute-start | bytes 2433032 | tf_op jit(solution)/shard_map/ppermute | solution.py:370
  290.3 55.1 %collective-permute-start.11 = (bf16[528,768]{1,0:T(8,128)(2,1)}, bf16[528,768]{1,0:T(8,128)(2,1)S(1)}, u32[]{:S(2)}, u32[]{:S(2)}) collective-permute-start(bf16[528,768]{1,0:T(8,128)(2,1)} %get-tuple-element.195), channel_id=1, source_target_pairs={{16,0},{24,8},{17,1},{25,9},{18,2},{26,10},{19,3},{27,11},{20,4},{... | collective-permute-start | bytes 2433032 | tf_op jit(solution)/shard_map/ppermute | solution.py:370
  387.7 17.9 %collective-permute-start.12 = (bf16[528,768]{1,0:T(8,128)(2,1)}, bf16[528,768]{1,0:T(8,128)(2,1)S(1)}, u32[]{:S(2)}, u32[]{:S(2)}) collective-permute-start(bf16[528,768]{1,0:T(8,128)(2,1)} %get-tuple-element.205), channel_id=1, source_target_pairs={{16,0},{24,8},{17,1},{25,9},{18,2},{26,10},{19,3},{27,11},{20,4},{... | collective-permute-start | bytes 2433032 | tf_op jit(solution)/shard_map/ppermute | solution.py:370
  389.0 16.3 %collective-permute-start.13 = (bf16[512,768]{1,0:T(8,128)(2,1)S(1)}, bf16[512,768]{1,0:T(8,128)(2,1)S(1)}, u32[]{:S(2)}, u32[]{:S(2)}) collective-permute-start(bf16[512,768]{1,0:T(8,128)(2,1)S(1)} %copy-done.5), channel_id=1, source_target_pairs={{0,16},{8,24},{1,17},{9,25},{2,18},{10,26},{3,19},{11,27},{4,20},{... | collective-permute-start | bytes 2359304 | tf_op jit(solution)/shard_map/ppermute | solution.py:370
  394.4 11.2 %collective-permute-start.14 = (bf16[16,768]{1,0:T(8,128)(2,1)S(1)}, bf16[16,768]{1,0:T(8,128)(2,1)S(1)}, u32[]{:S(2)}, u32[]{:S(2)}) collective-permute-start(bf16[16,768]{1,0:T(8,128)(2,1)S(1)} %slice_select_fusion.3), channel_id=1, source_target_pairs={{0,16},{8,24},{1,17},{9,25},{2,18},{10,26},{3,19},{11,27},{4,20},{... | collective-permute-start | bytes 73736 | tf_op jit(solution)/shard_map/ppermute | solution.py:370
  447.3 15.8 %collective-permute-start.15 = (bf16[528,768]{1,0:T(8,128)(2,1)}, bf16[528,768]{1,0:T(8,128)(2,1)S(1)}, u32[]{:S(2)}, u32[]{:S(2)}) collective-permute-start(bf16[528,768]{1,0:T(8,128)(2,1)} %get-tuple-element.215), channel_id=1, source_target_pairs={{16,0},{24,8},{17,1},{25,9},{18,2},{26,10},{19,3},{27,11},{20,4},{... | collective-permute-start | bytes 2433032 | tf_op jit(solution)/shard_map/ppermute | solution.py:370
  449.3 6.1 collective-permute-start.16
  504.7 14.8 %collective-permute-start.17 = (bf16[528,768]{1,0:T(8,128)(2,1)}, bf16[528,768]{1,0:T(8,128)(2,1)S(1)}, u32[]{:S(2)}, u32[]{:S(2)}) collective-permute-start(bf16[528,768]{1,0:T(8,128)(2,1)} %get-tuple-element.225), channel_id=1, source_target_pairs={{16,0},{24,8},{17,1},{25,9},{18,2},{26,10},{19,3},{27,11},{20,4},{... | collective-permute-start | bytes 2433032 | tf_op jit(solution)/shard_map/ppermute | solution.py:370
  612.8 25.8 %collective-permute-start.20 = (bf16[768,3072]{1,0:T(8,128)(2,1)}, bf16[768,3072]{1,0:T(8,128)(2,1)}, u32[]{:S(2)}, u32[]{:S(2)}) collective-permute-start(bf16[768,3072]{1,0:T(8,128)(2,1)} %broadcast_select_fusion), channel_id=1, source_target_pairs={{0,8},{8,0},{16,24},{24,16},{1,9},{9,1},{17,25},{25,17},{2,10},{10... | collective-permute-start | bytes 14155784 | tf_op jit(solution)/shard_map/ppermute | solution.py:370
  647.1 22.6 %collective-permute-start.2 = (bf16[512,768]{1,0:T(8,128)(2,1)}, bf16[512,768]{1,0:T(8,128)(2,1)}, u32[]{:S(2)}, u32[]{:S(2)}) collective-permute-start(bf16[512,768]{1,0:T(8,128)(2,1)} %slice.154), channel_id=1, source_target_pairs={{16,0},{24,8},{17,1},{25,9},{18,2},{26,10},{19,3},{27,11},{20,4},{... | collective-permute-start | bytes 2359304 | tf_op jit(solution)/shard_map/ppermute | solution.py:370
  649.4 36.5 %collective-permute-start.8 = (bf16[512,768]{1,0:T(8,128)(2,1)}, bf16[512,768]{1,0:T(8,128)(2,1)S(1)}, u32[]{:S(2)}, u32[]{:S(2)}) collective-permute-start(bf16[512,768]{1,0:T(8,128)(2,1)} %slice.165), channel_id=1, source_target_pairs={{16,0},{24,8},{17,1},{25,9},{18,2},{26,10},{19,3},{27,11},{20,4},{... | collective-permute-start | bytes 2359304 | tf_op jit(solution)/shard_map/ppermute | solution.py:370
  651.6 36.9 %collective-permute-start.19 = (bf16[512,768]{1,0:T(8,128)(2,1)}, bf16[512,768]{1,0:T(8,128)(2,1)}, u32[]{:S(2)}, u32[]{:S(2)}) collective-permute-start(bf16[512,768]{1,0:T(8,128)(2,1)} %slice.174), channel_id=1, source_target_pairs={{0,16},{8,24},{1,17},{9,25},{2,18},{10,26},{3,19},{11,27},{4,20},{... | collective-permute-start | bytes 2359304 | tf_op jit(solution)/shard_map/ppermute | solution.py:370
  689.5 60.1 %collective-permute-start.18 = (bf16[512,768]{1,0:T(8,128)(2,1)}, bf16[512,768]{1,0:T(8,128)(2,1)}, u32[]{:S(2)}, u32[]{:S(2)}) collective-permute-start(bf16[512,768]{1,0:T(8,128)(2,1)} %slice.172), channel_id=1, source_target_pairs={{0,16},{8,24},{1,17},{9,25},{2,18},{10,26},{3,19},{11,27},{4,20},{... | collective-permute-start | bytes 2359304 | tf_op jit(solution)/shard_map/ppermute | solution.py:370
  (25 other events, 302.9 us)
Sparse Core Ops, SparseCore 0:
  9.6 24.5 all-gather.2
  35.7 15.5 all-gather.4
  645.2 237.3 all-reduce.4

commit v2 on v1

--- a/solution.py
+++ b/solution.py
@@ -18,7 +18,6 @@
 SLOTS = 5
 SPARE = 4
 
-SWAP_CORE = [(0, 1), (1, 0), (2, 3), (3, 2)]
 TO_SECOND = [(0, 2), (1, 3)]
 TO_FIRST = [(2, 0), (3, 1)]
 
@@ -328,25 +327,188 @@
         [pltpu.VMEM((rows, width), F32), pltpu.VMEM((rows, cols), BF16)], stacks, "attn_bwd")
 
 
-def grad_kernel(left_ref, right_ref, out_ref):
-    left = left_ref[...].reshape(-1, left_ref.shape[2])
-    right = right_ref[...].reshape(-1, right_ref.shape[2])
-    out_ref[...] = mm(left, right, 0, 0).astype(out_ref.dtype)
-
-
-def weight_grad(left, right, lblock, rblock):
-    _, rows, wide = left.shape
-    cols = right.shape[2]
+def grad_kernel(*refs, lefts):
+    left_refs, right_refs = refs[:lefts], refs[lefts:2 * lefts]
+    out_ref = refs[-1]
+
+    def multiply(left_ref, right_ref):
+        left = left_ref[...].reshape(-1, left_ref.shape[2])
+        right = right_ref[...].reshape(-1, right_ref.shape[2])
+        out_ref[...] = mm(left, right, 0, 0).astype(out_ref.dtype)
+
+    if lefts == 1:
+        multiply(left_refs[0], right_refs[0])
+    else:
+        for t in range(lefts):
+            pl.when(pl.program_id(0) == t)(functools.partial(multiply, left_refs[t], right_refs[t]))
+
+
+def weight_grads(lefts, rights, tiles, left_moves, place, total, earlier, name):
+    _, rows, width = rights[0].shape if left_moves else lefts[0].shape
+    count = len(lefts)
+
+    def spec(moves):
+        if moves:
+            return pl.BlockSpec((SPARE, rows, width), lambda t: (0, 0, t))
+        return pl.BlockSpec((SPARE, rows, width), lambda t: (0, 0, 0), pipeline_mode=pl.Buffered(buffer_count=1))
+
+    moving = count == 1
+    extra = [] if earlier is None else [earlier]
     return pl.pallas_call(
-        grad_kernel,
-        grid=(wide // lblock, cols // rblock),
-        in_specs=[pl.BlockSpec((SPARE, rows, lblock), lambda i, j: (0, 0, i)),
-                  pl.BlockSpec((SPARE, rows, rblock), lambda i, j: (0, 0, j))],
-        out_specs=pl.BlockSpec((lblock, rblock), lambda i, j: (i, j)),
-        out_shape=shape_of((wide, cols)),
+        functools.partial(grad_kernel, lefts=count),
+        grid=(tiles,),
+        in_specs=[spec(moving and left_moves)] * count + [spec(moving and not left_moves)] * count
+        + [pl.BlockSpec(memory_space=pl.ANY)] * len(extra),
+        out_specs=pl.BlockSpec((None, width, width), lambda t: place(t) + (0,)),
+        out_shape=shape_of((2, total, width)),
+        input_output_aliases={2 * count: 0} if extra else {},
         compiler_params=pltpu.CompilerParams(vmem_limit_bytes=VMEM_BYTES),
-        name="weight_grad",
-    )(left, right)
+        name=name,
+    )(*lefts, *rights, *extra)
+
+
+def widen_kernel(in_ref, out_ref):
+    out_ref[...] = in_ref[...].astype(F32)
+
+
+def widen(data, blocks, offset, by_column):
+    width = data.shape[1]
+    if by_column:
+        shape, spec = (width, blocks * width), pl.BlockSpec((width, width), lambda b: (0, b))
+    else:
+        shape, spec = (blocks * width, width), pl.BlockSpec((width, width), lambda b: (b, 0))
+    return pl.pallas_call(
+        widen_kernel, grid=(blocks,),
+        in_specs=[pl.BlockSpec((width, width), lambda b: (offset + b, 0))],
+        out_specs=spec, out_shape=shape_of(shape, F32),
+        compiler_params=pltpu.CompilerParams(vmem_limit_bytes=VMEM_BYTES), name="widen",
+    )(data)
+
+
+def ring_layout(n, want):
+    subs = 2 if n <= 8 else 1
+    unit = 2 * n * subs
+    piece = -(-want // unit)
+    piece += -piece % 16
+    return subs, piece, unit * piece
+
+
+def ring_kernel(data_ref, out_ref, mine, got, final, start, slots, load_sem, store_sem, swap_send, swap_recv,
+                sum_send, sum_recv, full_send, full_recv, *, n, subs, piece):
+    section = lax.axis_index("section")
+    data = lax.axis_index("dp")
+    core = lax.rem(section, 2)
+    partner = section + 1 - 2 * core
+    half = n // 2
+
+    def place(p):
+        p = lax.rem(p + 2 * n, n)
+        return jnp.where(p < half, 2 * p, 2 * (n - 1 - p) + 1)
+
+    me = jnp.where(lax.rem(data, 2) == 0, data // 2, n - 1 - data // 2)
+    peers = (place(me + 1), place(me - 1))
+    signs = (1, -1)
+    span = subs * piece
+
+    def chunk(index):
+        return lax.rem(index + 2 * n, n)
+
+    def first_row(index, d):
+        return pl.multiple_of((chunk(index) * 2 + d) * span, 16)
+
+    loads, swaps = {}, {}
+    for j in range(n):
+        for d in (0, 1):
+            rows = pl.ds(first_row(me - signs[d] * j, d), span)
+            loads[j, d] = pltpu.make_async_copy(data_ref.at[core, rows], mine.at[rows], load_sem.at[d, j])
+            loads[j, d].start()
+    barrier = pltpu.get_barrier_semaphore()
+    pl.semaphore_signal(barrier, inc=1, device_id={"section": partner}, device_id_type=pl.DeviceIdType.MESH)
+    for d in (0, 1):
+        pl.semaphore_signal(barrier, inc=1, device_id={"dp": peers[d]}, device_id_type=pl.DeviceIdType.MESH)
+    pl.semaphore_wait(barrier, 3)
+    for j in range(n):
+        for d in (0, 1):
+            rows = pl.ds(first_row(me - signs[d] * j, d), span)
+            swaps[j, d] = pltpu.make_async_remote_copy(
+                src_ref=data_ref.at[1 - core, rows], dst_ref=got.at[rows],
+                send_sem=swap_send.at[d, j], recv_sem=swap_recv.at[d, j],
+                device_id={"section": partner}, device_id_type=pl.DeviceIdType.MESH)
+            swaps[j, d].start()
+
+    sums, fulls, stores = {}, {}, []
+
+    def own(j, d, u):
+        row = pl.multiple_of(first_row(me - signs[d] * j, d) + u * piece, 16)
+        rows = pl.ds(row, piece)
+        return mine[rows, :].astype(F32) + got[rows, :].astype(F32)
+
+    for s in range(n):
+        for d in (0, 1):
+            loads[s, d].wait()
+            swaps[s, d].wait_recv()
+        for u in range(subs):
+            for d in (0, 1):
+                value = own(s, d, u)
+                if s == 0:
+                    source = start.at[d, u]
+                else:
+                    sums[s - 1, d, u].wait_recv()
+                    source = slots.at[d, u, s - 1]
+                    value = value + source[...].astype(F32)
+                if s < n - 1:
+                    source[...] = value.astype(BF16)
+                    sums[s, d, u] = pltpu.make_async_remote_copy(
+                        src_ref=source, dst_ref=slots.at[d, u, s],
+                        send_sem=sum_send.at[d, u, s], recv_sem=sum_recv.at[d, u, s],
+                        device_id={"dp": peers[d]}, device_id_type=pl.DeviceIdType.MESH)
+                    sums[s, d, u].start()
+                else:
+                    row = pl.multiple_of(first_row(me - signs[d] * s, d) + u * piece, 16)
+                    final[pl.ds(row, piece), :] = value.astype(BF16)
+    for s in range(n):
+        for u in range(subs):
+            for d in (0, 1):
+                row = pl.multiple_of(first_row(me + signs[d] * (1 - s), d) + u * piece, 16)
+                rows = pl.ds(row, piece)
+                if s > 0:
+                    fulls[s - 1, d, u].wait_recv()
+                if s < n - 1:
+                    fulls[s, d, u] = pltpu.make_async_remote_copy(
+                        src_ref=final.at[rows], dst_ref=final.at[rows],
+                        send_sem=full_send.at[d, u, s], recv_sem=full_recv.at[d, u, s],
+                        device_id={"dp": peers[d]}, device_id_type=pl.DeviceIdType.MESH)
+                    fulls[s, d, u].start()
+                copy = pltpu.make_async_copy(final.at[rows], out_ref.at[rows], store_sem.at[d, u, s])
+                copy.start()
+                stores.append(copy)
+    for copy in swaps.values():
+        copy.wait_send()
+    for copy in sums.values():
+        copy.wait_send()
+    for copy in fulls.values():
+        copy.wait_send()
+    for copy in stores:
+        copy.wait()
+
+
+def ring_sum(data, n, subs, piece):
+    total, width = data.shape[1:]
+    dma = pltpu.SemaphoreType.DMA
+    return pl.pallas_call(
+        functools.partial(ring_kernel, n=n, subs=subs, piece=piece),
+        in_specs=[pl.BlockSpec(memory_space=pl.ANY)],
+        out_specs=pl.BlockSpec(memory_space=pl.ANY),
+        out_shape=shape_of((total, width)),
+        scratch_shapes=[
+            pltpu.VMEM((total, width), BF16), pltpu.VMEM((total, width), BF16), pltpu.VMEM((total, width), BF16),
+            pltpu.VMEM((2, subs, piece, width), BF16), pltpu.VMEM((2, subs, n - 1, piece, width), BF16),
+            dma((2, n)), dma((2, subs, n)), dma((2, n)), dma((2, n)),
+            dma((2, subs, n - 1)), dma((2, subs, n - 1)), dma((2, subs, n - 1)), dma((2, subs, n - 1))],
+        compiler_params=pltpu.CompilerParams(
+            vmem_limit_bytes=VMEM_BYTES, collective_id=0, has_side_effects=True),
+        name="ring_sum",
+    )(data)
 
 
 def body(tokens, doc_ids, reset_flags, memory_init, w_proj, vectors, w_down, cotangent):
@@ -358,6 +520,7 @@
     first = stage == 0
     _, segments, seg_tokens, width = tokens.shape
     memory_count = memory_init.shape[0]
+    hidden = w_proj.shape[2]
     pad = -(memory_count + seg_tokens) % 16
     rows = seg_tokens + memory_count + pad
     pairs = [[0, 1], [2, 3]]
@@ -468,19 +631,15 @@
     share = width // 4
     memory_total = lax.dynamic_slice(small[8:], (0, section * share), (memory_count, share))
 
-    grad_ff1 = weight_grad(y1, da, width, 512)
-    grad_ff2 = weight_grad(h, df, 512, width)
-    grad_attn = jnp.concatenate(
-        [weight_grad(x_in, dq, width, 384), weight_grad(x_in, dk, width, 384),
-         weight_grad(x_in, dv, width, 384), weight_grad(o, db, width, 384)], axis=1)
-    low = core == 0
-    half = w_down.shape[0]
-    got_proj = send(pick(low, grad_ff1, grad_attn), SWAP_CORE)
-    got_down = send(pick(low, grad_ff2[half:], grad_ff2[:half]), SWAP_CORE)
-    my_proj = (pick(low, grad_attn, grad_ff1).astype(F32) + got_proj.astype(F32)).astype(BF16)
-    my_down = (pick(low, grad_ff2[:half], grad_ff2[half:]).astype(F32) + got_down.astype(F32)).astype(BF16)
-    total_proj = lax.psum(my_proj, "dp").astype(F32)
-    total_down = lax.psum(my_down, "dp").astype(F32)
+    blocks = hidden // width
+    half = w_down.shape[0] // width
+    subs, piece, total = ring_layout(data_count, (blocks + half) * width)
+    stack = weight_grads([h], [df], blocks, True, lambda t: (t // half, blocks + t % half), total, None, "grad_down")
+    stack = weight_grads([y1], [da], blocks, False, lambda t: (1, t), total, stack, "grad_up")
+    stack = weight_grads([x_in] * 3 + [o], [dq, dk, dv, db], blocks, False, lambda t: (0, t), total, stack, "grad_attn")
+    summed = ring_sum(stack, data_count, subs, piece)
+    total_proj = widen(summed, blocks, 0, True)
+    total_down = widen(summed, half, blocks, False)
 
     def collect(done, table, route, keep_first):
         item_own, item_other = (0, 1) if keep_first else (1, 0)

time: 908 us -> 845 us (0.931)
  waiting for transfers between devices: 316 us -> 149 us
  Pallas kernels: 387 us -> 533 us
  other arithmetic: 56.7 us -> 29.8 us
    pallas_call x6, Pallas kernels: 60.7 us -> 207 us  [the longest x1 143 us: ring_sum(): pl.pallas_call(functools.partial(ring_kernel, n=n, subs=subs, piece=piece...]
    psum x1 -> x0, waiting for transfers between devices: 132 us -> none  [body(): total_proj = lax.psum(my_proj, 'dp').astype(F32)]
    ppermute x22 -> x20, waiting for transfers between devices: 164 us -> 129 us  [send(): return lax.ppermute(block, 'section', route)]
    broadcast_in_dim x2 -> x0, other arithmetic: 14 us -> none  [body(): total_proj[None]]
    select_n x17 -> x15, other arithmetic: 24.6 us -> 15.8 us  [pick(): return jnp.where(choice, yes, no)]
    ppermute x22 -> x20, starting transfers between devices: 50.5 us -> 44.5 us  [send(): return lax.ppermute(block, 'section', route)]
  transfers between devices with their start and end apart: 25 -> 22, of which waited for: 16 -> 11; matrix products, arithmetic and copies ran while one was open for 4% -> 4% of each run, Pallas kernels for 7% -> 36%
where the time goes in v2:
time: 845 us; the launch traced here: 837 us
  Pallas kernels  533 us (63%)
  waiting for transfers between devices  149 us (18%)
  blocking collectives  47.3 us (6%)
  starting transfers between devices  44.6 us (5%)
  other arithmetic  29.8 us (4%)
  between operations  16.4 us (2%)
  local copies, waits for them, and re-layouts  16.3 us (2%)
    pallas_call x20, Pallas kernels, staged_call(): pl.pallas_call(wrapped, grid_spec=pltpu.PrefetchScalarGridSpec(num_scalar...  326 us
    pallas_call x1, Pallas kernels, ring_sum(): pl.pallas_call(functools.partial(ring_kernel, n=n, subs=subs, piece=piece...  143 us
    ppermute x20, waiting for transfers between devices, send(): return lax.ppermute(block, 'section', route)  129 us
    pallas_call x3, Pallas kernels, weight_grads(): pl.pallas_call(functools.partial(grad_kernel, lefts=count), grid=(tiles,)...  53.6 us
    psum x1, blocking collectives, body(): small = lax.psum(small, ('section', 'dp'))  45.3 us
    ppermute x20, starting transfers between devices, send(): return lax.ppermute(block, 'section', route)  44.5 us
    all_gather x1, waiting for transfers between devices, body(): proj = lax.all_gather(w_proj[0], 'section', axis=0, axis_index_groups=pairs)  18.9 us
  transfers between devices with their start and end apart: 22, of which 11 were waited for; matrix products, arithmetic and copies ran while one was open for 4% of the time, Pallas kernels for 36%

profile of v2, /device:TPU:0, one launch (start us, length us, event | category | flops | bytes accessed | tf_op | source)
XLA Modules:
  0.0 836.6 jit_solution(13131925739945724458)
XLA Ops:
  15.3 18.9 %all-gather.3.cloned.1.call-done.refs_1_.refs_2_.refs_3_.refs_4_.refs_5_.refs_9_.refs_10_.refs_11_.refs_12_ = bf16[2,768,3072]{2,1,0:T(8,128)(2,1)} async-done(((bf16[1,768,3072]{2,1,0:T(8,128)(2,1)}), bf16[2,768,3072]{2,1,0:T(8,128)(2,1)}) %all-gather.3.cloned.1.call-update) | async-done | bytes 9437200 | tf_op jit(solution)/shard_map/all_gather | solution.py:528
  35.0 18.7 %attn_fwd.5 = (bf16[5,528,768]{2,1,0:T(8,128)(2,1)}, bf16[5,528,768]{2,1,0:T(8,128)(2,1)}, bf16[5,528,768]{2,1,0:T(8,128)(2,1)}, bf16[5,12,528,528]{3,2,1,0:T(8,...) custom-call(s32[2]{0:T(128)} %pad_add_fusion.14.info_ref, ...), custom_call_target="tpu_custom_call" | custom-call | tf_op jit(solution)/shard_map/attn_fwd/pallas_call | solution.py:59
  53.7 13.2 %ff_fwd.5 = (bf16[5,528,3072]{2,1,0:T(8,128)(2,1)}, bf16[5,528,3072]{2,1,0:T(8,128)(2,1)}, bf16[5,528,768]{2,1,0:T(8,128)(2,1)}, f32[5,528,128]{2,1,0:T(8,128)}, bf16[528,768]{1,0:T(8,128)(2,1)}) custom-call(s32[2]{0:T(128)} %pad_add_fusion.14.info_ref, bf16[5,528,768]{2,1,0:T(8,128)(2,1)} %get-tuple-element.126.refs_0_.refs_15_, ...), custom_call_target="tpu_custom_call" | custom-call | tf_op jit(solution)/shard_map/ff_fwd/pallas_call | solution.py:59
  71.1 18.8 %collective-permute-done = bf16[512,768]{1,0:T(8,128)(2,1)} collective-permute-done((bf16[512,768]{1,0:T(8,128)(2,1)S(1)}, bf16[512,768]{1,0:T(8,128)(2,1)}, u32[]{:S(2)}, u32[]{:S(2)}) %collective-permute-start) | collective-permute-done | bytes 786464 | tf_op jit(solution)/shard_map/ppermute | solution.py:533
  93.1 18.7 %attn_fwd.6 = (bf16[5,528,768]{2,1,0:T(8,128)(2,1)}, bf16[5,528,768]{2,1,0:T(8,128)(2,1)}, bf16[5,528,768]{2,1,0:T(8,128)(2,1)}, bf16[5,12,528,528]{3,2,1,0:T(8,...) custom-call(s32[2]{0:T(128)} %pad_add_fusion.13.info_ref, ...), custom_call_target="tpu_custom_call", output_to_operand_aliasing={{0}: (9, {}), {1}: (10, {}), {2}: (11, {}), {3}: (12, {}), ... | custom-call | tf_op jit(solution)/shard_map/attn_fwd/pallas_call | solution.py:59
  111.7 13.2 %ff_fwd.6 = (bf16[5,528,3072]{2,1,0:T(8,128)(2,1)}, bf16[5,528,3072]{2,1,0:T(8,128)(2,1)}, bf16[5,528,768]{2,1,0:T(8,128)(2,1)}, f32[5,528,128]{2,1,0:T(8,128)}, bf16[528,768]{1,0:T(8,128)(2,1)}) custom-call(s32[2]{0:T(128)} %pad_add_fusion.13.info_ref, ...), custom_call_target="tpu_custom_call", output_to_operand_aliasing={{0}: (5, {}), {1}: (6, {}), {2}: (7, {}), {3}: (8, {})} | custom-call | tf_op jit(solution)/shard_map/ff_fwd/pallas_call | solution.py:59
  145.7 18.7 %attn_fwd.7 = (bf16[5,528,768]{2,1,0:T(8,128)(2,1)}, bf16[5,528,768]{2,1,0:T(8,128)(2,1)}, bf16[5,528,768]{2,1,0:T(8,128)(2,1)}, bf16[5,12,528,528]{3,2,1,0:T(8,...) custom-call(s32[2]{0:T(128)} %pad_add_fusion.12.info_ref, ...), custom_call_target="tpu_custom_call", output_to_operand_aliasing={{0}: (9, {}), {1}: (10, {}), {2}: (11, {}), {3}: (12, {}), ... | custom-call | tf_op jit(solution)/shard_map/attn_fwd/pallas_call | solution.py:59
  164.4 13.3 %ff_fwd.7 = (bf16[5,528,3072]{2,1,0:T(8,128)(2,1)}, bf16[5,528,3072]{2,1,0:T(8,128)(2,1)}, bf16[5,528,768]{2,1,0:T(8,128)(2,1)}, f32[5,528,128]{2,1,0:T(8,128)}, bf16[528,768]{1,0:T(8,128)(2,1)}) custom-call(s32[2]{0:T(128)} %pad_add_fusion.12.info_ref, ...), custom_call_target="tpu_custom_call", output_to_operand_aliasing={{0}: (5, {}), {1}: (6, {}), {2}: (7, {}), {3}: (8, {})} | custom-call | tf_op jit(solution)/shard_map/ff_fwd/pallas_call | solution.py:59
  204.4 18.7 %attn_fwd.8 = (bf16[5,528,768]{2,1,0:T(8,128)(2,1)}, bf16[5,528,768]{2,1,0:T(8,128)(2,1)}, bf16[5,528,768]{2,1,0:T(8,128)(2,1)}, bf16[5,12,528,528]{3,2,1,0:T(8,...) custom-call(s32[2]{0:T(128)} %pad_add_fusion.11.info_ref, ...), custom_call_target="tpu_custom_call", output_to_operand_aliasing={{0}: (9, {}), {1}: (10, {}), {2}: (11, {}), {3}: (12, {}), ... | custom-call | tf_op jit(solution)/shard_map/attn_fwd/pallas_call | solution.py:59
  223.1 13.2 %ff_fwd.8 = (bf16[5,528,3072]{2,1,0:T(8,128)(2,1)}, bf16[5,528,3072]{2,1,0:T(8,128)(2,1)}, bf16[5,528,768]{2,1,0:T(8,128)(2,1)}, f32[5,528,128]{2,1,0:T(8,128)}, bf16[528,768]{1,0:T(8,128)(2,1)}) custom-call(s32[2]{0:T(128)} %pad_add_fusion.11.info_ref, ...), custom_call_target="tpu_custom_call", output_to_operand_aliasing={{0}: (5, {}), {1}: (6, {}), {2}: (7, {}), {3}: (8, {})} | custom-call | tf_op jit(solution)/shard_map/ff_fwd/pallas_call | solution.py:59
  292.3 53.3 %collective-permute-done.11 = bf16[528,768]{1,0:T(8,128)(2,1)S(1)} collective-permute-done((bf16[528,768]{1,0:T(8,128)(2,1)}, bf16[528,768]{1,0:T(8,128)(2,1)S(1)}, u32[]{:S(2)}, u32[]{:S(2)}) %collective-permute-start.11) | collective-permute-done | bytes 811040 | tf_op jit(solution)/shard_map/ppermute | solution.py:533
  346.7 13.4 %ff_bwd.6 = (bf16[5,528,768]{2,1,0:T(8,128)(2,1)}, bf16[5,528,3072]{2,1,0:T(8,128)(2,1)}, f32[5,2,768]{2,1,0:T(2,128)}, bf16[528,768]{1,0:T(8,128)(2,1)}) custom-call(s32[2]{0:T(128)} %pad_add_fusion.8.info_ref, bf16[528,768]{1,0:T(8,128)(2,1)} %pad_select_fusion.refs_0_, ...), custom_call_target="tpu_custom_call", output_to_operand_aliasing={{0}: (8, {}), {1}: (9, {}), {2}: (10, {})} | custom-call | tf_op jit(solution)/shard_map/ff_bwd/pallas_call | solution.py:59
  360.1 27.6 %attn_bwd.6 = (bf16[5,528,768]{2,1,0:T(8,128)(2,1)}, bf16[5,528,768]{2,1,0:T(8,128)(2,1)}, bf16[5,528,768]{2,1,0:T(8,128)(2,1)}, bf16[5,528,768]{2,1,0:T(8,128)(...) custom-call(s32[2]{0:T(128)} %pad_add_fusion.8.info_ref, ...), custom_call_target="tpu_custom_call", output_to_operand_aliasing={{0}: (14, {}), {1}: (15, {}), {2}: (16, {}), {3}: (17, {}),... | custom-call | tf_op jit(solution)/shard_map/attn_bwd/pallas_call | solution.py:59
  406.7 13.3 %ff_bwd.7 = (bf16[5,528,768]{2,1,0:T(8,128)(2,1)}, bf16[5,528,3072]{2,1,0:T(8,128)(2,1)}, f32[5,2,768]{2,1,0:T(2,128)}, bf16[528,768]{1,0:T(8,128)(2,1)}) custom-call(s32[2]{0:T(128)} %pad_add_fusion.9.info_ref, bf16[528,768]{1,0:T(8,128)(2,1)} %maximum_select_fusion.1.refs_0_, ...), custom_call_target="tpu_custom_call", output_to_operand_aliasing={{0}: (8, {}), {1}: (9, {}), {2}: (10, {})} | custom-call | tf_op jit(solution)/shard_map/ff_bwd/pallas_call | solution.py:59
  419.9 27.7 %attn_bwd.7 = (bf16[5,528,768]{2,1,0:T(8,128)(2,1)}, bf16[5,528,768]{2,1,0:T(8,128)(2,1)}, bf16[5,528,768]{2,1,0:T(8,128)(2,1)}, bf16[5,528,768]{2,1,0:T(8,128)(...) custom-call(s32[2]{0:T(128)} %pad_add_fusion.9.info_ref, ...), custom_call_target="tpu_custom_call", output_to_operand_aliasing={{0}: (14, {}), {1}: (15, {}), {2}: (16, {}), {3}: (17, {}),... | custom-call | tf_op jit(solution)/shard_map/attn_bwd/pallas_call | solution.py:59
  471.8 13.4 %ff_bwd.8 = (bf16[5,528,768]{2,1,0:T(8,128)(2,1)}, bf16[5,528,3072]{2,1,0:T(8,128)(2,1)}, f32[5,2,768]{2,1,0:T(2,128)}, bf16[528,768]{1,0:T(8,128)(2,1)}) custom-call(s32[2]{0:T(128)} %pad_add_fusion.10.info_ref, bf16[528,768]{1,0:T(8,128)(2,1)} %broadcast_select_fusion.1.refs_0_, ...), custom_call_target="tpu_custom_call", output_to_operand_aliasing={{0}: (8, {}), {1}: (9, {}), {2}: (10, {})} | custom-call | tf_op jit(solution)/shard_map/ff_bwd/pallas_call | solution.py:59
  485.2 27.6 %attn_bwd.8 = (bf16[5,528,768]{2,1,0:T(8,128)(2,1)}, bf16[5,528,768]{2,1,0:T(8,128)(2,1)}, bf16[5,528,768]{2,1,0:T(8,128)(2,1)}, bf16[5,528,768]{2,1,0:T(8,128)(...) custom-call(s32[2]{0:T(128)} %pad_add_fusion.10.info_ref, ...), custom_call_target="tpu_custom_call", output_to_operand_aliasing={{0}: (14, {}), {1}: (15, {}), {2}: (16, {}), {3}: (17, {}),... | custom-call | tf_op jit(solution)/shard_map/attn_bwd/pallas_call | solution.py:59
  528.5 13.2 %ff_bwd.9 = (bf16[5,528,768]{2,1,0:T(8,128)(2,1)}, bf16[5,528,3072]{2,1,0:T(8,128)(2,1)}, f32[5,2,768]{2,1,0:T(2,128)}, bf16[528,768]{1,0:T(8,128)(2,1)}) custom-call(s32[2]{0:T(128)} %pad_add_fusion.17.info_ref, bf16[528,768]{1,0:T(8,128)(2,1)} %broadcast_select_fusion.refs_0_, ...), custom_call_target="tpu_custom_call", output_to_operand_aliasing={{0}: (8, {}), {1}: (9, {}), {2}: (10, {})} | custom-call | tf_op jit(solution)/shard_map/ff_bwd/pallas_call | solution.py:59
  541.7 27.6 %attn_bwd.9 = (bf16[5,528,768]{2,1,0:T(8,128)(2,1)}, bf16[5,528,768]{2,1,0:T(8,128)(2,1)}, bf16[5,528,768]{2,1,0:T(8,128)(2,1)}, bf16[5,528,768]{2,1,0:T(8,128)(...) custom-call(s32[2]{0:T(128)} %pad_add_fusion.17.info_ref, ...), custom_call_target="tpu_custom_call", output_to_operand_aliasing={{0}: (14, {}), {1}: (15, {}), {2}: (16, {}), {3}: (17, {}),... | custom-call | tf_op jit(solution)/shard_map/attn_bwd/pallas_call | solution.py:59
  574.3 45.3 %psum.7 = f32[18,768]{1,0:T(8,128)S(1)} all-reduce(f32[18,768]{1,0:T(8,128)S(1)} %pad_maximum_fusion.3), channel_id=1, replica_groups=mesh['section'=4,'dp'=8] {'section','dp'}, use_global_device_ids=true, to_apply=%region_2.3 | all-reduce | flops 13824 | bytes 110592 | tf_op jit(solution)/shard_map/psum | solution.py:629
  619.7 15.9 %grad_down.1.refs_2_ = bf16[2,4608,768]{2,1,0:T(8,128)(2,1)} custom-call(bf16[5,528,3072]{2,1,0:T(8,128)(2,1)} %get-tuple-element.242.refs_0_, bf16[5,528,768]{2,1,0:T(8,128)(2,1)} %get-tuple-element.243.refs_1_), custom_call_target="tpu_custom_call" | custom-call | tf_op jit(solution)/shard_map/grad_down/pallas_call | solution.py:357
  635.6 15.8 %grad_up.1.refs_8_ = bf16[2,4608,768]{2,1,0:T(8,128)(2,1)} custom-call(bf16[5,528,768]{2,1,0:T(8,128)(2,1)} %get-tuple-element.178.refs_0_, bf16[5,528,3072]{2,1,0:T(8,128)(2,1)} %get-tuple-element.241.refs_1_, bf16[2,4608,768]{2,1,0:T(8,128)(2,1)} %grad_down.1.refs_2_), custom_call_target="tpu_custom_call", output_to_operand_aliasing={{}: (2, {})} | custom-call | tf_op jit(solution)/shard_map/grad_up/pallas_call | solution.py:357
  651.4 21.9 %grad_attn.1.data_ref = bf16[2,4608,768]{2,1,0:T(8,128)(2,1)} custom-call(bf16[5,528,768]{2,1,0:T(8,128)(2,1)} %get-tuple-element.236.refs_0_.refs_1_.refs_2_, bf16[5,528,768]{2,1,0:T(8,128)(2,1)} %get-tuple-element.236.refs_0_.refs_1_.refs_2_, bf16[5,528,768]{2,1,0:T(8,128)(2,1)} %get-tuple-element.236.refs_0_.refs_1_.refs_2_, ...), custom_call_target="tpu_custom_call", output_to_operand_aliasing={{}: (8, {})} | custom-call | tf_op jit(solution)/shard_map/grad_attn/pallas_call | solution.py:357
  673.3 143.1 %ring_sum.1.in_ref = bf16[4608,768]{1,0:T(8,128)(2,1)} custom-call(bf16[2,4608,768]{2,1,0:T(8,128)(2,1)} %grad_attn.1.data_ref), custom_call_target="tpu_custom_call" | custom-call | tf_op jit(solution)/shard_map/ring_sum/pallas_call | solution.py:498
  (152 shorter events, 195.8 us)
Async XLA Ops:
  7.2 27.0 %all-gather.3.cloned.1.call-start = ((), (), s32[]{:S(2)}) async-start(), calls=%async_computation | async-start | bytes 14155776 | tf_op jit(solution)/shard_map/all_gather | solution.py:528
  7.9 45.8 %all-gather.5.cloned.1.call-start = ((), (), s32[]{:S(2)}) async-start(), calls=%async_computation.1 | async-start | bytes 7077888 | tf_op jit(solution)/shard_map/all_gather | solution.py:529
  66.9 23.0 %collective-permute-start.1 = (bf16[528,768]{1,0:T(8,128)(2,1)}, bf16[528,768]{1,0:T(8,128)(2,1)S(1)}, u32[]{:S(2)}, u32[]{:S(2)}) collective-permute-start(bf16[528,768]{1,0:T(8,128)(2,1)} %get-tuple-element.127), channel_id=1, source_target_pairs={{0,16},{8,24},{1,17},{9,25},{2,18},{10,26},{3,19},{11,27},{4,20},{... | collective-permute-start | bytes 2433032 | tf_op jit(solution)/shard_map/ppermute | solution.py:533
  68.2 21.7 %collective-permute-start = (bf16[512,768]{1,0:T(8,128)(2,1)S(1)}, bf16[512,768]{1,0:T(8,128)(2,1)}, u32[]{:S(2)}, u32[]{:S(2)}) collective-permute-start(bf16[512,768]{1,0:T(8,128)(2,1)S(1)} %get-tuple-element.249), channel_id=1, source_target_pairs={{16,0},{24,8},{17,1},{25,9},{18,2},{26,10},{19,3},{27,11},{20,4},{... | collective-permute-start | bytes 2359304 | tf_op jit(solution)/shard_map/ppermute | solution.py:533
  124.9 18.8 %collective-permute-start.4 = (bf16[528,768]{1,0:T(8,128)(2,1)}, bf16[528,768]{1,0:T(8,128)(2,1)S(1)}, u32[]{:S(2)}, u32[]{:S(2)}) collective-permute-start(bf16[528,768]{1,0:T(8,128)(2,1)} %get-tuple-element.141), channel_id=1, source_target_pairs={{0,16},{8,24},{1,17},{9,25},{2,18},{10,26},{3,19},{11,27},{4,20},{... | collective-permute-start | bytes 2433032 | tf_op jit(solution)/shard_map/ppermute | solution.py:533
  127.2 5.7 collective-permute-start.3
  177.7 24.7 %collective-permute-start.7 = (bf16[528,768]{1,0:T(8,128)(2,1)}, bf16[528,768]{1,0:T(8,128)(2,1)S(1)}, u32[]{:S(2)}, u32[]{:S(2)}) collective-permute-start(bf16[528,768]{1,0:T(8,128)(2,1)} %get-tuple-element.155), channel_id=1, source_target_pairs={{0,16},{8,24},{1,17},{9,25},{2,18},{10,26},{3,19},{11,27},{4,20},{... | collective-permute-start | bytes 2433032 | tf_op jit(solution)/shard_map/ppermute | solution.py:533
  182.1 20.3 %collective-permute-start.5 = (bf16[512,768]{1,0:T(8,128)(2,1)S(1)}, bf16[512,768]{1,0:T(8,128)(2,1)S(1)}, u32[]{:S(2)}, u32[]{:S(2)}) collective-permute-start(bf16[512,768]{1,0:T(8,128)(2,1)S(1)} %get-tuple-element.248), channel_id=1, source_target_pairs={{16,0},{24,8},{17,1},{25,9},{18,2},{26,10},{19,3},{27,11},{20,4},{... | collective-permute-start | bytes 2359304 | tf_op jit(solution)/shard_map/ppermute | solution.py:533
  184.4 56.9 %collective-permute-start.10 = (bf16[512,768]{1,0:T(8,128)(2,1)S(1)}, bf16[512,768]{1,0:T(8,128)(2,1)}, u32[]{:S(2)}, u32[]{:S(2)}) collective-permute-start(bf16[512,768]{1,0:T(8,128)(2,1)S(1)} %get-tuple-element.247), channel_id=1, source_target_pairs={{0,16},{8,24},{1,17},{9,25},{2,18},{10,26},{3,19},{11,27},{4,20},{... | collective-permute-start | bytes 2359304 | tf_op jit(solution)/shard_map/ppermute | solution.py:533
  190.6 11.7 %collective-permute-start.6 = (bf16[16,768]{1,0:T(8,128)(2,1)S(1)}, bf16[16,768]{1,0:T(8,128)(2,1)S(1)}, u32[]{:S(2)}, u32[]{:S(2)}) collective-permute-start(bf16[16,768]{1,0:T(8,128)(2,1)S(1)} %slice.154), channel_id=1, source_target_pairs={{16,0},{24,8},{17,1},{25,9},{18,2},{26,10},{19,3},{27,11},{20,4},{... | collective-permute-start | bytes 73736 | tf_op jit(solution)/shard_map/ppermute | solution.py:533
  236.3 16.9 %collective-permute-start.9 = (bf16[528,768]{1,0:T(8,128)(2,1)}, bf16[528,768]{1,0:T(8,128)(2,1)S(1)}, u32[]{:S(2)}, u32[]{:S(2)}) collective-permute-start(bf16[528,768]{1,0:T(8,128)(2,1)} %get-tuple-element.169), channel_id=1, source_target_pairs={{0,16},{8,24},{1,17},{9,25},{2,18},{10,26},{3,19},{11,27},{4,20},{... | collective-permute-start | bytes 2433032 | tf_op jit(solution)/shard_map/ppermute | solution.py:533
  290.3 55.3 %collective-permute-start.11 = (bf16[528,768]{1,0:T(8,128)(2,1)}, bf16[528,768]{1,0:T(8,128)(2,1)S(1)}, u32[]{:S(2)}, u32[]{:S(2)}) collective-permute-start(bf16[528,768]{1,0:T(8,128)(2,1)} %get-tuple-element.195), channel_id=1, source_target_pairs={{16,0},{24,8},{17,1},{25,9},{18,2},{26,10},{19,3},{27,11},{20,4},{... | collective-permute-start | bytes 2433032 | tf_op jit(solution)/shard_map/ppermute | solution.py:533
  387.7 17.8 %collective-permute-start.12 = (bf16[528,768]{1,0:T(8,128)(2,1)}, bf16[528,768]{1,0:T(8,128)(2,1)S(1)}, u32[]{:S(2)}, u32[]{:S(2)}) collective-permute-start(bf16[528,768]{1,0:T(8,128)(2,1)} %get-tuple-element.205), channel_id=1, source_target_pairs={{16,0},{24,8},{17,1},{25,9},{18,2},{26,10},{19,3},{27,11},{20,4},{... | collective-permute-start | bytes 2433032 | tf_op jit(solution)/shard_map/ppermute | solution.py:533
  389.0 16.3 %collective-permute-start.13 = (bf16[512,768]{1,0:T(8,128)(2,1)S(1)}, bf16[512,768]{1,0:T(8,128)(2,1)S(1)}, u32[]{:S(2)}, u32[]{:S(2)}) collective-permute-start(bf16[512,768]{1,0:T(8,128)(2,1)S(1)} %copy-done), channel_id=1, source_target_pairs={{0,16},{8,24},{1,17},{9,25},{2,18},{10,26},{3,19},{11,27},{4,20},{... | collective-permute-start | bytes 2359304 | tf_op jit(solution)/shard_map/ppermute | solution.py:533
  394.4 11.1 %collective-permute-start.14 = (bf16[16,768]{1,0:T(8,128)(2,1)S(1)}, bf16[16,768]{1,0:T(8,128)(2,1)S(1)}, u32[]{:S(2)}, u32[]{:S(2)}) collective-permute-start(bf16[16,768]{1,0:T(8,128)(2,1)S(1)} %slice_select_fusion.3), channel_id=1, source_target_pairs={{0,16},{8,24},{1,17},{9,25},{2,18},{10,26},{3,19},{11,27},{4,20},{... | collective-permute-start | bytes 73736 | tf_op jit(solution)/shard_map/ppermute | solution.py:533
  447.6 23.1 %collective-permute-start.15 = (bf16[528,768]{1,0:T(8,128)(2,1)}, bf16[528,768]{1,0:T(8,128)(2,1)S(1)}, u32[]{:S(2)}, u32[]{:S(2)}) collective-permute-start(bf16[528,768]{1,0:T(8,128)(2,1)} %get-tuple-element.215), channel_id=1, source_target_pairs={{16,0},{24,8},{17,1},{25,9},{18,2},{26,10},{19,3},{27,11},{20,4},{... | collective-permute-start | bytes 2433032 | tf_op jit(solution)/shard_map/ppermute | solution.py:533
  449.0 65.3 %collective-permute-start.2 = (bf16[512,768]{1,0:T(8,128)(2,1)S(1)}, bf16[512,768]{1,0:T(8,128)(2,1)}, u32[]{:S(2)}, u32[]{:S(2)}) collective-permute-start(bf16[512,768]{1,0:T(8,128)(2,1)S(1)} %slice.146), channel_id=1, source_target_pairs={{16,0},{24,8},{17,1},{25,9},{18,2},{26,10},{19,3},{27,11},{20,4},{... | collective-permute-start | bytes 2359304 | tf_op jit(solution)/shard_map/ppermute | solution.py:533
  451.9 63.6 %collective-permute-start.8 = (bf16[512,768]{1,0:T(8,128)(2,1)}, bf16[512,768]{1,0:T(8,128)(2,1)}, u32[]{:S(2)}, u32[]{:S(2)}) collective-permute-start(bf16[512,768]{1,0:T(8,128)(2,1)} %slice.157), channel_id=1, source_target_pairs={{16,0},{24,8},{17,1},{25,9},{18,2},{26,10},{19,3},{27,11},{20,4},{... | collective-permute-start | bytes 2359304 | tf_op jit(solution)/shard_map/ppermute | solution.py:533
  453.9 9.6 %collective-permute-start.16 = (bf16[16,768]{1,0:T(8,128)(2,1)S(1)}, bf16[16,768]{1,0:T(8,128)(2,1)S(1)}, u32[]{:S(2)}, u32[]{:S(2)}) collective-permute-start(bf16[16,768]{1,0:T(8,128)(2,1)S(1)} %slice_select_fusion.2), channel_id=1, source_target_pairs={{0,16},{8,24},{1,17},{9,25},{2,18},{10,26},{3,19},{11,27},{4,20},{... | collective-permute-start | bytes 73736 | tf_op jit(solution)/shard_map/ppermute | solution.py:533
  462.1 55.9 %collective-permute-start.19 = (bf16[512,768]{1,0:T(8,128)(2,1)S(1)}, bf16[512,768]{1,0:T(8,128)(2,1)S(1)}, u32[]{:S(2)}, u32[]{:S(2)}) collective-permute-start(bf16[512,768]{1,0:T(8,128)(2,1)S(1)} %slice.166), channel_id=1, source_target_pairs={{0,16},{8,24},{1,17},{9,25},{2,18},{10,26},{3,19},{11,27},{4,20},{... | collective-permute-start | bytes 2359304 | tf_op jit(solution)/shard_map/ppermute | solution.py:533
  512.9 14.5 %collective-permute-start.17 = (bf16[528,768]{1,0:T(8,128)(2,1)}, bf16[528,768]{1,0:T(8,128)(2,1)S(1)}, u32[]{:S(2)}, u32[]{:S(2)}) collective-permute-start(bf16[528,768]{1,0:T(8,128)(2,1)} %get-tuple-element.225), channel_id=1, source_target_pairs={{16,0},{24,8},{17,1},{25,9},{18,2},{26,10},{19,3},{27,11},{20,4},{... | collective-permute-start | bytes 2433032 | tf_op jit(solution)/shard_map/ppermute | solution.py:533
  541.6 31.8 %copy-start.9 = (f32[5,2,768]{2,1,0:T(2,128)S(1)}, f32[5,2,768]{2,1,0:T(2,128)}, u32[]{:S(2)}) copy-start(f32[5,2,768]{2,1,0:T(2,128)} %get-tuple-element.245) | copy-start | bytes 92164
  541.6 31.9 %copy-start.5 = (bf16[528,768]{1,0:T(8,128)(2,1)S(1)}, bf16[528,768]{1,0:T(8,128)(2,1)}, u32[]{:S(2)}) copy-start(bf16[528,768]{1,0:T(8,128)(2,1)} %get-tuple-element.225) | copy-start | bytes 2433028
  572.1 255.8 %collective-permute-start.18 = (bf16[512,768]{1,0:T(8,128)(2,1)}, bf16[512,768]{1,0:T(8,128)(2,1)S(1)}, u32[]{:S(2)}, u32[]{:S(2)}) collective-permute-start(bf16[512,768]{1,0:T(8,128)(2,1)} %slice.164), channel_id=1, source_target_pairs={{0,16},{8,24},{1,17},{9,25},{2,18},{10,26},{3,19},{11,27},{4,20},{... | collective-permute-start | bytes 2359304 | tf_op jit(solution)/shard_map/ppermute | solution.py:533
  (15 other events, 244.7 us)
Sparse Core Ops, SparseCore 0:
  9.6 24.5 all-gather.2
  35.7 15.5 all-gather.4

commit v3 on v2

v3 whole, which is shorter than its diff:
```python
import functools

import jax
import jax.numpy as jnp
from jax import lax
from jax.experimental import pallas as pl
from jax.experimental.pallas import tpu as pltpu
from jax.sharding import PartitionSpec as P

HEADS = 12
DOCS = 4
NORM_EPSILON = 1e-06
NEGATIVE = -1e30
BF16 = jnp.bfloat16
F32 = jnp.float32
VMEM_BYTES = 60 * 2**20
GROUP = 4
FF_BLOCK = 1024
TILE = 16
MICROS = 4
MESH = pl.DeviceIdType.MESH


def mm(left, right, ca=1, cb=0):
    return lax.dot_general(
        left, right, (((ca,), (cb,)), ((), ())), preferred_element_type=F32
    )


def shape_of(shape, dtype=BF16):
    return jax.ShapeDtypeStruct(shape, dtype)


def anywhere():
    return pl.BlockSpec(memory_space=pl.ANY)


def on_chip():
    return pl.BlockSpec(memory_space=pltpu.VMEM)


def head_rows(block, group, head):
    lane = lax.broadcasted_iota(jnp.int32, (1, block.shape[1]), 1) // head
    return jnp.concatenate([jnp.where(lane == h, block, jnp.zeros_like(block)) for h in range(group)], axis=0)


def head_fold(stacked, group, head):
    total, width = stacked.shape
    rows = total // group
    lane = lax.broadcasted_iota(jnp.int32, (1, width), 1) // head
    out = stacked[:rows]
    for h in range(1, group):
        out = jnp.where(lane == h, stacked[h * rows:(h + 1) * rows], out)
    return out


def normalise(summed):
    center = summed - jnp.mean(summed, axis=-1, keepdims=True)
    variance = jnp.mean(center * center, axis=-1, keepdims=True)
    inverse = lax.rsqrt(variance + NORM_EPSILON)
    return center * inverse, inverse


def norm_back(g, n, inverse, gain):
    u = g * gain
    dz = inverse * (u - jnp.mean(u, axis=-1, keepdims=True) - n * jnp.mean(u * n, axis=-1, keepdims=True))
    return dz, jnp.sum(g * n, axis=0, keepdims=True), jnp.sum(g, axis=0, keepdims=True)


def layers_kernel(tokens_ref, cot_ref, proj_ref, down_ref, vec_ref, init_ref, fresh_ref, key_ref, query_ref,
                  out_ref, gtok_ref, gmem_ref, gvec_ref,
                  xs, qs, ks, vs, os_, n1s, y1s, n2s, hs, ss, ps, dfs, dbs, dqs, dks, dvs, das,
                  hop_ref, back_ref, tok_other, cot_other,
                  wa, w1, w2, vecs, x, q, k, v, o, n1, y1, n2, df, db, do, acc, y, hb, sb, pb, r1, r2,
                  mem_in, mem_grad,
                  share_local, share_send, share_recv, tok_send, tok_recv, cot_send, cot_recv,
                  hop_send, hop_recv, back_send, back_recv, mem_send, mem_recv, mg_send, mg_recv,
                  out_sem, out_send, out_recv, gt_sem, gt_send, gt_recv,
                  load_sem, save_sem, h_sem, s_sem, p_sem):
    section = lax.axis_index("section")
    stage = section // 2
    core = lax.rem(section, 2)
    first = stage == 0
    second = stage == 1
    mate = {"section": section + 1 - 2 * core}
    across = {"section": section + 2 - 4 * stage}
    segments, tokens, width = tokens_ref.shape
    rows = x.shape[0]
    hidden = proj_ref.shape[1]
    head = width // HEADS
    cols = GROUP * head
    groups = HEADS // GROUP
    blocks = hidden // FF_BLOCK
    halfd = down_ref.shape[0]
    micros = 2 * segments
    scale = head ** (-0.5)
    body_rows = pl.ds(0, tokens)
    last_rows = pl.ds(tokens, rows - tokens)

    def remote(source, target, send, recv, device):
        return pltpu.make_async_remote_copy(src_ref=source, dst_ref=target, send_sem=send, recv_sem=recv,
                                            device_id=device, device_id_type=MESH)

    local = pltpu.make_async_copy

    barrier = pltpu.get_barrier_semaphore()
    pl.semaphore_signal(barrier, inc=1, device_id=mate, device_id_type=MESH)
    pl.semaphore_signal(barrier, inc=1, device_id=across, device_id_type=MESH)
    pl.semaphore_wait(barrier, 2)

    down_rows = pl.ds(pl.multiple_of(core * halfd, 16), halfd)
    other_rows = pl.ds(pl.multiple_of((1 - core) * halfd, 16), halfd)
    down_away = remote(down_ref, w2.at[down_rows], share_send.at[1], share_recv.at[1], mate)
    vec_away = remote(vec_ref, vecs.at[core], share_send.at[2], share_recv.at[2], mate)
    proj_a = remote(proj_ref, wa, share_send.at[0], share_recv.at[0], mate)
    proj_b = remote(proj_ref, w1, share_send.at[0], share_recv.at[0], mate)
    proj_here_a = local(proj_ref, wa, share_local.at[0])
    proj_here_b = local(proj_ref, w1, share_local.at[0])
    down_here = local(down_ref, w2.at[down_rows], share_local.at[1])
    vec_here = local(vec_ref, vecs.at[core], share_local.at[2])

    @pl.when(core == 0)
    def _():
        proj_a.start()
        proj_here_a.start()

    @pl.when(core == 1)
    def _():
        proj_b.start()
        proj_here_b.start()

    vec_away.start()
    vec_here.start()
    down_away.start()
    down_here.start()

    def tok_copy(k_):
        return remote(tokens_ref.at[k_], tok_other.at[k_], tok_send.at[k_], tok_recv.at[k_], across)

    def cot_copy(k_):
        return remote(cot_ref.at[k_], cot_other.at[k_], cot_send.at[k_], cot_recv.at[k_], across)

    @pl.when(second)
    def _():
        for k_ in range(segments):
            tok_copy(k_).start()

    @pl.when(first)
    def _():
        cot_copy(segments - 1).start()

    vec_here.wait()
    vec_away.wait_recv()

    @pl.when(core == 0)
    def _():
        proj_here_a.wait()

    @pl.when(core == 1)
    def _():
        proj_a.wait_recv()

    def hop_copy(m):
        return remote(y.at[lax.rem(m, 2)], hop_ref.at[m], hop_send.at[m], hop_recv.at[m], across)

    def mem_copy(m):
        return remote(y.at[lax.rem(m, 2), last_rows], mem_in.at[m], mem_send.at[m], mem_recv.at[m], across)

    def out_here(m, seg):
        return local(y.at[lax.rem(m, 2), body_rows], out_ref.at[seg], out_sem.at[m])

    def out_away(m, seg):
        return remote(y.at[lax.rem(m, 2), body_rows], out_ref.at[seg], out_send.at[seg], out_recv.at[seg], across)

    kept = [(x, xs), (q, qs), (k, ks), (v, vs), (o, os_), (n1, n1s), (y1, y1s), (n2, n2s)]

    def saves(m):
        return [local(here, there.at[m], save_sem.at[i]) for i, (here, there) in enumerate(kept)]

    def band(g):
        return pl.ds(pl.multiple_of(g * cols, cols), cols)

    def h_save(m, j):
        b = lax.rem(j, 2)
        return local(hb.at[b], hs.at[m, :, pl.ds(pl.multiple_of(j * FF_BLOCK, FF_BLOCK), FF_BLOCK)], h_sem.at[b])

    def s_save(m, j):
        b = lax.rem(j, 2)
        return local(sb.at[b], ss.at[m, :, pl.ds(pl.multiple_of(j * FF_BLOCK, FF_BLOCK), FF_BLOCK)], s_sem.at[b])

    def p_save(m, g):
        b = lax.rem(g, 2)
        return local(pb.at[b], ps.at[m, g], p_sem.at[b])

    def forward(m, carry):
        item = lax.rem(m, 2)
        seg = m // 2

        @pl.when(m > 0)
        def _():
            for save in saves(m - 1):
                save.wait()

        body_load = [local(source.at[seg], x.at[body_rows], load_sem.at[0]) for source in (tokens_ref, tok_other)]
        whole_load = local(hop_ref.at[m], x, load_sem.at[0])

        @pl.when(first)
        def _():
            @pl.when(item == 0)
            def _():
                body_load[0].start()

            @pl.when(item == 1)
            def _():
                tok_copy(seg).wait_recv()
                body_load[1].start()

            @pl.when(seg == 0)
            def _():
                x[last_rows, :] = init_ref[...]

            @pl.when(seg > 0)
            def _():
                mem_copy(m - 2).wait_recv()
                x[last_rows, :] = jnp.where(fresh_ref[item] > 0, init_ref[...], mem_in[m - 2])

            body_load[0].wait()

        @pl.when(second)
        def _():
            hop_copy(m).wait_recv()
            whole_load.start()
            whole_load.wait()

        out = saves(m)
        out[0].start()

        def attend(g, carry2):
            here = band(g)
            xv = x[...]
            q[:, here] = mm(xv, wa[:, here]).astype(BF16)
            k[:, here] = mm(xv, wa[:, pl.ds(pl.multiple_of(width + g * cols, cols), cols)]).astype(BF16)
            v[:, here] = mm(xv, wa[:, pl.ds(pl.multiple_of(2 * width + g * cols, cols), cols)]).astype(BF16)

            @pl.when(g >= 2)
            def _():
                p_save(m, g - 2).wait()

            s = mm(k[:, here], head_rows(q[:, here] * scale, GROUP, head), 1, 1)
            seen = (key_ref[m, :, 0:1] & query_ref[m]) != 0
            s = jnp.where(seen, s, NEGATIVE)
            e = jnp.exp(s - jnp.max(s, axis=0, keepdims=True))
            p = (e * (1.0 / jnp.sum(e, axis=0, keepdims=True))).astype(BF16)
            pb[lax.rem(g, 2)] = p
            p_save(m, g).start()
            o[:, here] = head_fold(mm(p, v[:, here], 0, 0), GROUP, head).astype(BF16)
            return carry2

        lax.fori_loop(0, groups, attend, 0)
        for i in (1, 2, 3, 4):
            out[i].start()
        normed, inverse = normalise(x[...].astype(F32) + mm(o[...], wa[:, pl.ds(3 * width, width)]))
        n1[...] = normed.astype(BF16)
        r1[m] = jnp.broadcast_to(inverse, r1.shape[1:])
        y1v = (normed * vecs[0, 0:1, :] + vecs[0, 1:2, :]).astype(BF16)
        y1[...] = y1v
        acc[...] = y1v.astype(F32)
        out[5].start()
        out[6].start()
        p_save(m, groups - 2).wait()
        p_save(m, groups - 1).wait()

        @pl.when(m == 0)
        def _():
            @pl.when(core == 0)
            def _():
                proj_b.wait_recv()

            @pl.when(core == 1)
            def _():
                proj_here_b.wait()

            down_here.wait()
            remote(down_ref, w2.at[other_rows], share_send.at[1], share_recv.at[1], mate).wait_recv()

        def feed(j, carry2):
            b = lax.rem(j, 2)

            @pl.when(j >= 2)
            def _():
                h_save(m, j - 2).wait()
                s_save(m, j - 2).wait()

            half = FF_BLOCK // 2
            yv = y1[...]
            pre = [mm(yv, w1[:, pl.ds(pl.multiple_of(j * FF_BLOCK + i * half, half), half)]) for i in range(2)]
            for i in range(2):
                a = pre[i]
                gate = 0.5 * (1.0 + lax.erf(a * 0.7071067811865476))
                hb[b, :, i * half:(i + 1) * half] = (a * gate).astype(BF16)
                sb[b, :, i * half:(i + 1) * half] = (
                    gate + a * jnp.exp(-0.5 * a * a) * 0.3989422804014327).astype(BF16)
            h_save(m, j).start()
            s_save(m, j).start()
            acc[...] += mm(hb[b], w2[pl.ds(pl.multiple_of(j * FF_BLOCK, FF_BLOCK), FF_BLOCK), :])
            return carry2

        lax.fori_loop(0, blocks, feed, 0)

        normed, inverse = normalise(acc[...])
        n2[...] = normed.astype(BF16)
        r2[m] = jnp.broadcast_to(inverse, r2.shape[1:])

        @pl.when(m >= 2)
        def _():
            @pl.when(first)
            def _():
                hop_copy(m - 2).wait_send()

            @pl.when(second)
            def _():
                mem_copy(m - 2).wait_send()

                @pl.when(item == 0)
                def _():
                    out_away(m - 2, seg - 1).wait_send()

                @pl.when(item == 1)
                def _():
                    out_here(m - 2, seg - 1).wait()

        y[item] = (normed * vecs[1, 0:1, :] + vecs[1, 1:2, :]).astype(BF16)
        out[7].start()

        @pl.when(first)
        def _():
            hop_copy(m).start()

        @pl.when(second)
        def _():
            @pl.when(seg + 1 < segments)
            def _():
                mem_copy(m).start()

            @pl.when(item == 0)
            def _():
                out_away(m, seg).start()

            @pl.when(item == 1)
            def _():
                out_here(m, seg).start()

        for j in range(max(0, blocks - 2), blocks):
            h_save(m, j).wait()
            s_save(m, j).wait()
        return carry

    lax.fori_loop(0, micros, forward, 0)
    for save in saves(micros - 1):
        save.wait()

    @pl.when(first)
    def _():
        for k_ in reversed(range(segments - 1)):
            cot_copy(k_).start()
        for m in range(micros - 2, micros):
            hop_copy(m).wait_send()
        for k_ in range(segments):
            out_away(0, k_).wait_recv()

    @pl.when(second)
    def _():
        out_away(micros - 2, segments - 1).wait_send()
        out_here(micros - 1, segments - 1).wait()

    gmem_ref[...] = jnp.zeros(gmem_ref.shape, F32)
    gvec_ref[...] = jnp.zeros(gvec_ref.shape, F32)

    def back_copy(t):
        return remote(y.at[lax.rem(t, 2)], back_ref.at[t], back_send.at[t], back_recv.at[t], across)

    def mg_copy(t):
        return remote(y.at[lax.rem(t, 2), last_rows], mem_grad.at[t], mg_send.at[t], mg_recv.at[t], across)

    def gt_here(t, seg):
        return local(y.at[lax.rem(t, 2), body_rows], gtok_ref.at[seg], gt_sem.at[t])

    def gt_away(t, seg):
        return remote(y.at[lax.rem(t, 2), body_rows], gtok_ref.at[seg], gt_send.at[seg], gt_recv.at[seg], across)

    def s_load(m, j):
        b = lax.rem(j, 2)
        return local(ss.at[m, :, pl.ds(pl.multiple_of(j * FF_BLOCK, FF_BLOCK), FF_BLOCK)], sb.at[b], s_sem.at[b])

    def d_save(m, j):
        b = lax.rem(j, 2)
        return local(hb.at[b], das.at[m, :, pl.ds(pl.multiple_of(j * FF_BLOCK, FF_BLOCK), FF_BLOCK)], h_sem.at[b])

    def p_load(m, g):
        b = lax.rem(g, 2)
        return local(ps.at[m, g], pb.at[b], p_sem.at[b])

    def back_saves(m):
        pairs = [(df, dfs), (db, dbs), (x, dqs), (o, dks), (y1, dvs)]
        return [local(here, there.at[m], save_sem.at[i]) for i, (here, there) in enumerate(pairs)]

    def backward(t, carry):
        item = lax.rem(t, 2)
        seg = segments - 1 - t // 2
        m = 2 * seg + item
        before = 2 * (segments - 1 - (t - 1) // 2) + lax.rem(t - 1 + 2, 2)

        @pl.when(t > 0)
        def _():
            for save in back_saves(before):
                save.wait()

        loads = [local(source.at[m], here, load_sem.at[1 + i])
                 for i, (source, here) in enumerate([(n2s, n2), (qs, q), (ks, k), (vs, v), (n1s, n1)])]
        body_load = [local(source.at[seg], y1.at[body_rows], load_sem.at[0]) for source in (cot_ref, cot_other)]
        whole_load = local(back_ref.at[t], y1, load_sem.at[0])
        for load in loads:
            load.start()
        s_load(m, 0).start()
        s_load(m, 1).start()
        p_load(m, 0).start()
        p_load(m, 1).start()

        @pl.when(second)
        def _():
            @pl.when(item == 1)
            def _():
                body_load[0].start()

            @pl.when(item == 0)
            def _():
                cot_copy(seg).wait_recv()
                body_load[1].start()

            @pl.when(seg + 1 == segments)
            def _():
                y1[last_rows, :] = jnp.zeros((rows - tokens, width), BF16)

            @pl.when(seg + 1 < segments)
            def _():
                mg_copy(t - 2).wait_recv()
                got = mem_grad[t - 2]
                y1[last_rows, :] = jnp.where(fresh_ref[item] > 0, jnp.zeros_like(got), got)

            body_load[0].wait()

        @pl.when(first)
        def _():
            back_copy(t).wait_recv()
            whole_load.start()
            whole_load.wait()

        loads[0].wait()
        dz, gain_grad, bias_grad = norm_back(y1[...].astype(F32), n2[...].astype(F32), r2[m, :, 0:1], vecs[1, 0:1, :])
        gvec_ref[2:3, :] += gain_grad
        gvec_ref[3:4, :] += bias_grad
        df[...] = dz.astype(BF16)
        acc[...] = dz
        out = back_saves(m)
        out[0].start()

        def feed(j, carry2):
            b = lax.rem(j, 2)

            @pl.when(j >= 2)
            def _():
                d_save(m, j - 2).wait()

            s_load(m, j).wait()
            half = FF_BLOCK // 2
            dfv = df[...]
            dh = [mm(dfv, w2[pl.ds(pl.multiple_of(j * FF_BLOCK + i * half, half), half), :], 1, 1) for i in range(2)]
            for i in range(2):
                cut = slice(i * half, (i + 1) * half)
                hb[b, :, cut] = (dh[i] * sb[b, :, cut].astype(F32)).astype(BF16)
            d_save(m, j).start()

            @pl.when(j + 2 < blocks)
            def _():
                s_load(m, j + 2).start()

            acc[...] += mm(hb[b], w1[:, pl.ds(pl.multiple_of(j * FF_BLOCK, FF_BLOCK), FF_BLOCK)], 1, 1)
            return carry2

        lax.fori_loop(0, blocks, feed, 0)
        for load in loads[1:]:
            load.wait()
        dz, gain_grad, bias_grad = norm_back(acc[...].astype(BF16).astype(F32), n1[...].astype(F32), r1[m, :, 0:1],
                                             vecs[0, 0:1, :])
        gvec_ref[0:1, :] += gain_grad
        gvec_ref[1:2, :] += bias_grad
        db[...] = dz.astype(BF16)
        acc[...] = dz
        out[1].start()

        def attend(g, carry2):
            here = band(g)
            b = lax.rem(g, 2)
            p_load(m, g).wait()
            gv = mm(db[...], wa[here, pl.ds(3 * width, width)], 1, 1).astype(BF16)
            grads = head_rows(gv, GROUP, head)
            dp = mm(v[:, here], grads, 1, 1)
            p = pb[b]
            weight = p.astype(F32)
            ds = (weight * (dp - jnp.sum(weight * dp, axis=0, keepdims=True))).astype(BF16)
            dv = mm(p, grads).astype(BF16)
            dk = mm(ds, head_rows(q[:, here] * scale, GROUP, head)).astype(BF16)
            dq = (head_fold(mm(ds, k[:, here], 0, 0), GROUP, head) * scale).astype(BF16)

            @pl.when(g + 2 < groups)
            def _():
                p_load(m, g + 2).start()

            x[:, here] = dq
            o[:, here] = dk
            y1[:, here] = dv
            acc[...] += (mm(dq, wa[:, here], 1, 1)
                         + mm(dk, wa[:, pl.ds(pl.multiple_of(width + g * cols, cols), cols)], 1, 1)
                         + mm(dv, wa[:, pl.ds(pl.multiple_of(2 * width + g * cols, cols), cols)], 1, 1))
            return carry2

        lax.fori_loop(0, groups, attend, 0)
        for i in (2, 3, 4):
            out[i].start()

        @pl.when(t >= 2)
        def _():
            @pl.when(second)
            def _():
                back_copy(t - 2).wait_send()

            @pl.when(first)
            def _():
                mg_copy(t - 2).wait_send()

                @pl.when(item == 1)
                def _():
                    gt_away(t - 2, seg + 1).wait_send()

                @pl.when(item == 0)
                def _():
                    gt_here(t - 2, seg + 1).wait()

        dx = acc[...].astype(BF16)
        y[item] = dx

        @pl.when(second)
        def _():
            back_copy(t).start()

        @pl.when(first)
        def _():
            tail = dx[tokens:, :].astype(F32)

            @pl.when(seg > 0)
            def _():
                mg_copy(t).start()
                gmem_ref[...] += jnp.where(fresh_ref[item] > 0, tail, 0.0)

            @pl.when(seg == 0)
            def _():
                gmem_ref[...] += tail

            @pl.when(item == 0)
            def _():
                gt_here(t, seg).start()

            @pl.when(item == 1)
            def _():
                gt_away(t, seg).start()

        for j in range(max(0, blocks - 2), blocks):
            d_save(m, j).wait()
        return carry

    lax.fori_loop(0, micros, backward, 0)
    for save in back_saves(1):
        save.wait()

    @pl.when(second)
    def _():
        for t in range(micros - 2, micros):
            back_copy(t).wait_send()
        for k_ in range(segments):
            tok_copy(k_).wait_send()
            gt_away(1, k_).wait_recv()

    @pl.when(first)
    def _():
        gt_here(micros - 2, 0).wait()
        gt_away(micros - 1, 0).wait_send()
        for k_ in range(segments):
            cot_copy(k_).wait_send()

    proj_a.wait_send()
    down_away.wait_send()
    vec_away.wait_send()


def run_layers(tokens, cotangent, proj, down, vec, init, fresh, key_bits, query_bits):
    segments, seg_tokens, width = tokens.shape
    rows = seg_tokens + TILE
    hidden = proj.shape[1]
    micros = 2 * segments
    groups = HEADS // GROUP
    span = GROUP * rows
    stack = shape_of((micros, rows, width))
    wide = shape_of((micros, rows, hidden))
    low = pltpu.VMEM((rows, width), BF16)
    dma = pltpu.SemaphoreType.DMA
    pair = pltpu.VMEM((2, rows, FF_BLOCK), BF16)
    inverse = pltpu.VMEM((micros, rows, 128), F32)
    tails = pltpu.VMEM((2, TILE, width), BF16)
    return pl.pallas_call(
        layers_kernel,
        in_specs=[anywhere()] * 4 + [on_chip()] * 5,
        out_specs=[anywhere()] * 2 + [on_chip()] * 2 + [anywhere()] * 21,
        out_shape=[shape_of(tokens.shape), shape_of(tokens.shape), shape_of((TILE, width), F32),
                   shape_of((8, width), F32)]
        + [stack] * 8 + [wide] * 2 + [shape_of((micros, groups, rows, span))] + [stack] * 5 + [wide]
        + [stack] * 2 + [shape_of(tokens.shape)] * 2,
        scratch_shapes=[
            pltpu.VMEM((width, hidden), BF16), pltpu.VMEM((width, hidden), BF16), pltpu.VMEM((hidden, width), BF16),
            pltpu.VMEM((2, 2, width), F32)] + [low] * 11 + [
            pltpu.VMEM((rows, width), F32), pltpu.VMEM((2, rows, width), BF16), pair, pair,
            pltpu.VMEM((2, rows, span), BF16), inverse, inverse, tails, tails,
            dma((3,)), dma((3,)), dma((3,)), dma((segments,)), dma((segments,)), dma((segments,)), dma((segments,)),
            dma((micros,)), dma((micros,)), dma((micros,)), dma((micros,)), dma((2,)), dma((2,)), dma((2,)), dma((2,)),
            dma((micros,)), dma((segments,)), dma((segments,)), dma((micros,)), dma((segments,)), dma((segments,)),
            dma((6,)), dma((8,)), dma((2,)), dma((2,)), dma((2,))],
        compiler_params=pltpu.CompilerParams(vmem_limit_bytes=VMEM_BYTES, collective_id=1, has_side_effects=True),
        name="layers",
    )(tokens, cotangent, proj, down, vec, init, fresh, key_bits, query_bits)


def grad_kernel(*refs, lefts):
    left_refs, right_refs = refs[:lefts], refs[lefts:2 * lefts]
    out_ref = refs[-1]

    def multiply(left_ref, right_ref):
        left = left_ref[...].reshape(-1, left_ref.shape[2])
        right = right_ref[...].reshape(-1, right_ref.shape[2])
        out_ref[...] = mm(left, right, 0, 0).astype(out_ref.dtype)

    if lefts == 1:
        multiply(left_refs[0], right_refs[0])
    else:
        for t in range(lefts):
            pl.when(pl.program_id(0) == t)(functools.partial(multiply, left_refs[t], right_refs[t]))


def weight_grads(lefts, rights, tiles, left_moves, place, total, earlier, name):
    _, rows, width = rights[0].shape if left_moves else lefts[0].shape
    count = len(lefts)

    def spec(moves):
        if moves:
            return pl.BlockSpec((MICROS, rows, width), lambda t: (0, 0, t))
        return pl.BlockSpec((MICROS, rows, width), lambda t: (0, 0, 0), pipeline_mode=pl.Buffered(buffer_count=1))

    moving = count == 1
    extra = [] if earlier is None else [earlier]
    return pl.pallas_call(
        functools.partial(grad_kernel, lefts=count),
        grid=(tiles,),
        in_specs=[spec(moving and left_moves)] * count + [spec(moving and not left_moves)] * count
        + [pl.BlockSpec(memory_space=pl.ANY)] * len(extra),
        out_specs=pl.BlockSpec((None, width, width), lambda t: place(t) + (0,)),
        out_shape=shape_of((2, total, width)),
        input_output_aliases={2 * count: 0} if extra else {},
        compiler_params=pltpu.CompilerParams(vmem_limit_bytes=VMEM_BYTES),
        name=name,
    )(*lefts, *rights, *extra)


def widen_kernel(in_ref, out_ref):
    out_ref[...] = in_ref[...].astype(F32)


def widen(data, blocks, offset, by_column):
    width = data.shape[1]
    if by_column:
        shape, spec = (width, blocks * width), pl.BlockSpec((width, width), lambda b: (0, b))
    else:
        shape, spec = (blocks * width, width), pl.BlockSpec((width, width), lambda b: (b, 0))
    return pl.pallas_call(
        widen_kernel, grid=(blocks,),
        in_specs=[pl.BlockSpec((width, width), lambda b: (offset + b, 0))],
        out_specs=spec, out_shape=shape_of(shape, F32),
        compiler_params=pltpu.CompilerParams(vmem_limit_bytes=VMEM_BYTES), name="widen",
    )(data)


def ring_layout(n, want):
    subs = 2 if n <= 8 else 1
    unit = 2 * n * subs
    piece = -(-want // unit)
    piece += -piece % 16
    return subs, piece, unit * piece


def flipped(index, bit):
    return index + bit - 2 * bit * lax.rem(index // bit, 2)


def ring_kernel(data_ref, small_ref, out_ref, small_out, mine, got, final, start, slots, held, arrived,
                load_sem, store_sem, swap_send, swap_recv,
                sum_send, sum_recv, full_send, full_recv, small_send, small_recv, *, n, subs, piece, hops):
    section = lax.axis_index("section")
    data = lax.axis_index("dp")
    core = lax.rem(section, 2)
    partner = section + 1 - 2 * core
    half = n // 2

    def place(p):
        p = lax.rem(p + 2 * n, n)
        return jnp.where(p < half, 2 * p, 2 * (n - 1 - p) + 1)

    me = jnp.where(lax.rem(data, 2) == 0, data // 2, n - 1 - data // 2)
    peers = (place(me + 1), place(me - 1))
    signs = (1, -1)
    span = subs * piece

    def chunk(index):
        return lax.rem(index + 2 * n, n)

    def first_row(index, d):
        return pl.multiple_of((chunk(index) * 2 + d) * span, 16)

    loads, swaps = {}, {}
    for j in range(n):
        for d in (0, 1):
            rows = pl.ds(first_row(me - signs[d] * j, d), span)
            loads[j, d] = pltpu.make_async_copy(data_ref.at[core, rows], mine.at[rows], load_sem.at[d, j])
            loads[j, d].start()
    barrier = pltpu.get_barrier_semaphore()
    pl.semaphore_signal(barrier, inc=1, device_id={"section": partner}, device_id_type=pl.DeviceIdType.MESH)
    for d in (0, 1):
        pl.semaphore_signal(barrier, inc=1, device_id={"dp": peers[d]}, device_id_type=pl.DeviceIdType.MESH)
    friends = [{axis: flipped(section if axis == "section" else data, bit)} for axis, bit in hops]
    for friend in friends:
        pl.semaphore_signal(barrier, inc=1, device_id=friend, device_id_type=pl.DeviceIdType.MESH)
    pl.semaphore_wait(barrier, 3 + len(friends))
    held[0] = small_ref[...]
    smalls = []

    def start_small(i):
        smalls.append(pltpu.make_async_remote_copy(
            src_ref=held.at[i], dst_ref=arrived.at[i], send_sem=small_send.at[i], recv_sem=small_recv.at[i],
            device_id=friends[i], device_id_type=pl.DeviceIdType.MESH))
        smalls[i].start()

    def finish_small(i):
        smalls[i].wait_recv()
        total = held[i] + arrived[i]
        if i + 1 < len(friends):
            held[i + 1] = total
            start_small(i + 1)
        else:
            small_out[...] = total

    start_small(0)
    for j in range(n):
        for d in (0, 1):
            rows = pl.ds(first_row(me - signs[d] * j, d), span)
            swaps[j, d] = pltpu.make_async_remote_copy(
                src_ref=data_ref.at[1 - core, rows], dst_ref=got.at[rows],
                send_sem=swap_send.at[d, j], recv_sem=swap_recv.at[d, j],
                device_id={"section": partner}, device_id_type=pl.DeviceIdType.MESH)
            swaps[j, d].start()

    sums, fulls, stores = {}, {}, []

    def own(j, d, u):
        row = pl.multiple_of(first_row(me - signs[d] * j, d) + u * piece, 16)
        rows = pl.ds(row, piece)
        return mine[rows, :].astype(F32) + got[rows, :].astype(F32)

    for s in range(n):
        for d in (0, 1):
            loads[s, d].wait()
            swaps[s, d].wait_recv()
        for u in range(subs):
            for d in (0, 1):
                value = own(s, d, u)
                if s == 0:
                    source = start.at[d, u]
                else:
                    sums[s - 1, d, u].wait_recv()
                    source = slots.at[d, u, s - 1]
                    value = value + source[...].astype(F32)
                if s < n - 1:
                    source[...] = value.astype(BF16)
                    sums[s, d, u] = pltpu.make_async_remote_copy(
                        src_ref=source, dst_ref=slots.at[d, u, s],
                        send_sem=sum_send.at[d, u, s], recv_sem=sum_recv.at[d, u, s],
                        device_id={"dp": peers[d]}, device_id_type=pl.DeviceIdType.MESH)
                    sums[s, d, u].start()
                else:
                    row = pl.multiple_of(first_row(me - signs[d] * s, d) + u * piece, 16)
                    final[pl.ds(row, piece), :] = value.astype(BF16)
    waiting = list(range(len(friends)))
    for s in range(n):
        if s > 0 and waiting:
            finish_small(waiting.pop(0))
        for u in range(subs):
            for d in (0, 1):
                row = pl.multiple_of(first_row(me + signs[d] * (1 - s), d) + u * piece, 16)
                rows = pl.ds(row, piece)
                if s > 0:
                    fulls[s - 1, d, u].wait_recv()
                if s < n - 1:
                    fulls[s, d, u] = pltpu.make_async_remote_copy(
                        src_ref=final.at[rows], dst_ref=final.at[rows],
                        send_sem=full_send.at[d, u, s], recv_sem=full_recv.at[d, u, s],
                        device_id={"dp": peers[d]}, device_id_type=pl.DeviceIdType.MESH)
                    fulls[s, d, u].start()
                copy = pltpu.make_async_copy(final.at[rows], out_ref.at[rows], store_sem.at[d, u, s])
                copy.start()
                stores.append(copy)
    for i in waiting:
        finish_small(i)
    for copy in smalls:
        copy.wait_send()
    for copy in swaps.values():
        copy.wait_send()
    for copy in sums.values():
        copy.wait_send()
    for copy in fulls.values():
        copy.wait_send()
    for copy in stores:
        copy.wait()


def ring_sum(data, small, n, sections, subs, piece):
    total, width = data.shape[1:]
    hops = [("dp", 1 << i) for i in range(n.bit_length() - 1)] + [("section", 1 << i) for i in range(sections.bit_length() - 1)]
    dma = pltpu.SemaphoreType.DMA
    return pl.pallas_call(
        functools.partial(ring_kernel, n=n, subs=subs, piece=piece, hops=hops),
        in_specs=[pl.BlockSpec(memory_space=pl.ANY), pl.BlockSpec(memory_space=pltpu.VMEM)],
        out_specs=[pl.BlockSpec(memory_space=pl.ANY), pl.BlockSpec(memory_space=pltpu.VMEM)],
        out_shape=[shape_of((total, width)), shape_of(small.shape, F32)],
        scratch_shapes=[
            pltpu.VMEM((total, width), BF16), pltpu.VMEM((total, width), BF16), pltpu.VMEM((total, width), BF16),
            pltpu.VMEM((2, subs, piece, width), BF16), pltpu.VMEM((2, subs, n - 1, piece, width), BF16),
            pltpu.VMEM((len(hops),) + small.shape, F32), pltpu.VMEM((len(hops),) + small.shape, F32),
            dma((2, n)), dma((2, subs, n)), dma((2, n)), dma((2, n)),
            dma((2, subs, n - 1)), dma((2, subs, n - 1)), dma((2, subs, n - 1)), dma((2, subs, n - 1)),
            dma((len(hops),)), dma((len(hops),))],
        compiler_params=pltpu.CompilerParams(
            vmem_limit_bytes=VMEM_BYTES, collective_id=0, has_side_effects=True),
        name="ring_sum",
    )(data, small)


def body(tokens, doc_ids, reset_flags, memory_init, w_proj, vectors, w_down, cotangent):
    data_count = lax.axis_size("dp")
    section = lax.axis_index("section")
    data = lax.axis_index("dp")
    first = section < 2
    core = section % 2
    _, segments, seg_tokens, width = tokens.shape
    memory_count = memory_init.shape[0]
    hidden = w_proj.shape[2]
    pad = TILE - memory_count
    items = (core * data_count + data, (core + 2) * data_count + data)
    micros = [(item, k) for k in range(segments) for item in (0, 1)]
    flags = [lax.dynamic_index_in_dim(reset_flags, items[i], 0, keepdims=False) for i in (0, 1)]
    docs = jnp.stack([lax.dynamic_index_in_dim(doc_ids, items[item], 0, keepdims=False)[k] for item, k in micros])
    bits = jnp.left_shift(jnp.int32(1), docs)
    lines = jnp.ones((len(micros), 1), jnp.int32)
    every = (1 << DOCS) - 1
    key_bits = jnp.concatenate([bits, jnp.repeat(lines * every, memory_count, 1), jnp.repeat(lines * 0, pad, 1)], axis=1)
    query_bits = jnp.concatenate([bits, jnp.repeat(lines * every, TILE, 1)], axis=1)
    key_bits = jnp.broadcast_to(key_bits[:, :, None], key_bits.shape + (128,))
    query_bits = jnp.tile(query_bits, (1, GROUP))[:, None, :]
    fresh = jnp.stack([jnp.broadcast_to(flags[i][segments - 1], (TILE, width)) for i in (0, 1)]).astype(F32)
    init = jnp.concatenate([memory_init, jnp.zeros((pad, width), BF16)], axis=0)

    results = run_layers(tokens[0], cotangent[0], w_proj[0], w_down, vectors[0], init, fresh, key_bits, query_bits)
    block_rows, input_rows, grad_memory, grad_vec = results[:4]
    x_in, q, k_rows, v, o, n1, y1, n2, h, slope, p, df, db, dq, dk, dv, da = results[4:21]

    vec_pair = grad_vec[:4]
    nothing = jnp.zeros_like(vec_pair)
    small = jnp.concatenate([jnp.where(first, vec_pair, nothing), jnp.where(first, nothing, vec_pair), grad_memory],
                            axis=0)
    blocks = hidden // width
    half = w_down.shape[0] // width
    subs, piece, total = ring_layout(data_count, (blocks + half) * width)
    stack = weight_grads([h], [df], blocks, True, lambda t: (t // half, blocks + t % half), total, None, "grad_down")
    stack = weight_grads([y1], [da], blocks, False, lambda t: (1, t), total, stack, "grad_up")
    stack = weight_grads([x_in] * 3 + [o], [dq, dk, dv, db], blocks, False, lambda t: (0, t), total, stack, "grad_attn")
    summed, small = ring_sum(stack, small, data_count, lax.axis_size("section"), subs, piece)
    total_vec = lax.dynamic_slice(small, (2 * section, 0), (2, width))[None]
    share = width // 4
    memory_total = lax.dynamic_slice(small, (8, section * share), (memory_count, share))
    total_proj = widen(summed, blocks, 0, True)
    total_down = widen(summed, half, blocks, False)
    return (block_rows[None], input_rows[None], total_proj[None], total_vec, total_down, memory_total)


def solution(mesh):
    items = P(("section", "dp"), None, None, None)
    return jax.shard_map(
        body,
        mesh=mesh,
        in_specs=(items, P(), P(), P(), P("section", None, None), P("section", None, None),
                  P("section", None), items),
        out_specs=(items, items, P("section", None, None), P("section", None, None),
                   P("section", None), P(None, "section")),
        check_vma=False,
    )
```

time: 845 us -> 560 us (0.66)
  waiting for transfers between devices: 149 us -> 0 us
  blocking collectives: 47.3 us -> 0 us
  starting transfers between devices: 44.6 us -> 0 us
  other arithmetic: 29.8 us -> 3.51 us
  between operations: 16.4 us -> 0.73 us
  Pallas kernels: 533 us -> 542 us
    ppermute x20 -> x0, waiting for transfers between devices: 129 us -> none  [send(): return lax.ppermute(block, 'section', route)]
    psum x1 -> x0, blocking collectives: 45.3 us -> none  [body(): small = lax.psum(small, ('section', 'dp'))]
    ppermute x20 -> x0, starting transfers between devices: 44.5 us -> none  [send(): return lax.ppermute(block, 'section', route)]
    all_gather x2 -> x0, waiting for transfers between devices: 18.9 us -> none  [the longest x1 18.9 us: body(): proj = lax.all_gather(w_proj[0], 'section', axis=0, axis_index_groups=pairs)]
    select_n x15 -> x1, other arithmetic: 15.8 us -> 0.74 us  [body(): jnp.where(first, vec_pair, nothing)]
    another operation x14 -> x0, other arithmetic: 9.14 us -> none  [the longest x10 6.5 us: body(): info = jnp.stack([slot, valid]).astype(jnp.int32)]
    pallas_call x20 -> x1, Pallas kernels: 326 us -> 327 us  [run_layers(): pl.pallas_call(layers_kernel, in_specs=[anywhere()] * 4 + [on_chip()] * 5...]
  transfers between devices with their start and end apart: 22 -> 0, of which waited for: 11 -> 0; matrix products, arithmetic and copies ran while one was open for 4% -> 0% of each run, Pallas kernels for 36% -> 0%
where the time goes in v3:
time: 560 us; the launch traced here: 558 us
  Pallas kernels  542 us (97%)
  local copies, waits for them, and re-layouts  12 us (2%)
    pallas_call x1, Pallas kernels, run_layers(): pl.pallas_call(layers_kernel, in_specs=[anywhere()] * 4 + [on_chip()] * 5...  327 us
    pallas_call x1, Pallas kernels, ring_sum(): pl.pallas_call(functools.partial(ring_kernel, n=n, subs=subs, piece=piece...  151 us
    pallas_call x3, Pallas kernels, weight_grads(): pl.pallas_call(functools.partial(grad_kernel, lefts=count), grid=(tiles,)...  53.3 us

profile of v3, /device:TPU:0, one launch (start us, length us, event | category | flops | bytes accessed | tf_op | source)
XLA Modules:
  0.0 558.1 jit_solution(6193691106380809970)
XLA Ops:
  0.7 0.8 dynamic-slice_bitcast_fusion.4
  1.5 0.1 pad.8.clone
  1.6 1.3 broadcast_in_dim.22.key_ref
  2.9 0.7 tile.9.query_ref
  3.6 0.8 constant_dynamic-slice_fusion
  4.5 0.5 slice.35
  5.0 0.5 slice.36
  5.5 1.3 pad_convert_fusion
  6.8 0.7 stack.9.fresh_ref
  7.5 1.4 concatenate.12.init_ref
  8.9 327.5 %layers.1 = (bf16[2,512,768]{2,1,0:T(8,128)(2,1)}, bf16[2,512,768]{2,1,0:T(8,128)(2,1)}, f32[16,768]{1,0:T(8,128)}, f32[8,768]{1,0:T(8,128)}, bf16[4,528,768]{2,...) custom-call(bf16[2,512,768]{2,1,0:T(8,128)(2,1)} %bitcast.23, ...), custom_call_target="tpu_custom_call" | custom-call | tf_op jit(solution)/shard_map/layers/pallas_call | solution.py:619
  336.3 0.7 slice_select_fusion.1
  337.1 1.4 pad_maximum_fusion.small_ref
  338.5 15.9 %grad_down.1.refs_2_ = bf16[2,4608,768]{2,1,0:T(8,128)(2,1)} custom-call(bf16[4,528,3072]{2,1,0:T(8,128)(2,1)} %get-tuple-element.32.refs_0_, bf16[4,528,768]{2,1,0:T(8,128)(2,1)} %get-tuple-element.33.refs_1_), custom_call_target="tpu_custom_call" | custom-call | tf_op jit(solution)/shard_map/grad_down/pallas_call | solution.py:668
  354.5 15.9 %grad_up.1.refs_8_ = bf16[2,4608,768]{2,1,0:T(8,128)(2,1)} custom-call(bf16[4,528,768]{2,1,0:T(8,128)(2,1)} %get-tuple-element.30.refs_0_, bf16[4,528,3072]{2,1,0:T(8,128)(2,1)} %get-tuple-element.31.refs_1_, bf16[2,4608,768]{2,1,0:T(8,128)(2,1)} %grad_down.1.refs_2_), custom_call_target="tpu_custom_call", output_to_operand_aliasing={{}: (2, {})} | custom-call | tf_op jit(solution)/shard_map/grad_up/pallas_call | solution.py:668
  370.4 21.5 %grad_attn.1.data_ref = bf16[2,4608,768]{2,1,0:T(8,128)(2,1)} custom-call(bf16[4,528,768]{2,1,0:T(8,128)(2,1)} %get-tuple-element.24.refs_0_.refs_1_.refs_2_, bf16[4,528,768]{2,1,0:T(8,128)(2,1)} %get-tuple-element.24.refs_0_.refs_1_.refs_2_, bf16[4,528,768]{2,1,0:T(8,128)(2,1)} %get-tuple-element.24.refs_0_.refs_1_.refs_2_, ...), custom_call_target="tpu_custom_call", output_to_operand_aliasing={{}: (8, {})} | custom-call | tf_op jit(solution)/shard_map/grad_attn/pallas_call | solution.py:668
  391.8 150.9 %ring_sum.1 = (bf16[4608,768]{1,0:T(8,128)(2,1)}, f32[24,768]{1,0:T(8,128)}) custom-call(bf16[2,4608,768]{2,1,0:T(8,128)(2,1)} %grad_attn.1.data_ref, f32[24,768]{1,0:T(8,128)} %pad_maximum_fusion.small_ref), custom_call_target="tpu_custom_call" | custom-call | tf_op jit(solution)/shard_map/ring_sum/pallas_call | solution.py:844
  542.7 6.5 %widen.2 = f32[768,3072]{1,0:T(8,128)} custom-call(bf16[4608,768]{1,0:T(8,128)(2,1)} %get-tuple-element.36.in_ref), custom_call_target="tpu_custom_call" | custom-call | tf_op jit(solution)/shard_map/widen/pallas_call | solution.py:691
  549.2 3.7 widen.3
  552.9 1.5 constant_dynamic-slice_fusion.2
  554.5 1.3 dynamic-slice_bitcast_fusion
  555.8 0.0 copy-done.1
  555.8 1.1 copy.20
  556.9 1.1 copy.21
  (9 shorter events, 0.1 us)
Async XLA Ops:
  549.2 6.6 %copy-start.1 = (bf16[2,512,768]{2,1,0:T(8,128)(2,1)S(1)}, bf16[2,512,768]{2,1,0:T(8,128)(2,1)}, u32[]{:S(2)}) copy-start(bf16[2,512,768]{2,1,0:T(8,128)(2,1)} %get-tuple-element.22) | copy-start | bytes 4718596
  552.9 4.0 copy-start

commit v4 on v3

--- a/solution.py
+++ b/solution.py
@@ -638,44 +638,223 @@
     )(tokens, cotangent, proj, down, vec, init, fresh, key_bits, query_bits)
 
 
-def grad_kernel(*refs, lefts):
-    left_refs, right_refs = refs[:lefts], refs[lefts:2 * lefts]
-    out_ref = refs[-1]
-
-    def multiply(left_ref, right_ref):
-        left = left_ref[...].reshape(-1, left_ref.shape[2])
-        right = right_ref[...].reshape(-1, right_ref.shape[2])
-        out_ref[...] = mm(left, right, 0, 0).astype(out_ref.dtype)
-
-    if lefts == 1:
-        multiply(left_refs[0], right_refs[0])
-    else:
-        for t in range(lefts):
-            pl.when(pl.program_id(0) == t)(functools.partial(multiply, left_refs[t], right_refs[t]))
-
-
-def weight_grads(lefts, rights, tiles, left_moves, place, total, earlier, name):
-    _, rows, width = rights[0].shape if left_moves else lefts[0].shape
-    count = len(lefts)
-
-    def spec(moves):
-        if moves:
-            return pl.BlockSpec((MICROS, rows, width), lambda t: (0, 0, t))
-        return pl.BlockSpec((MICROS, rows, width), lambda t: (0, 0, 0), pipeline_mode=pl.Buffered(buffer_count=1))
-
-    moving = count == 1
-    extra = [] if earlier is None else [earlier]
+def flipped(index, bit):
+    return index + bit - 2 * bit * lax.rem(index // bit, 2)
+
+
+def ring_piece(n, width):
+    piece = -(-width // (2 * n))
+    return piece + -piece % 16
+
+
+def grads_kernel(xs, os_, y1s, hs, dqs, dks, dvs, dbs, das, dfs, small_ref, out_ref, small_out,
+                 lbuf, rbuf, mine, got, away, final, slots, held, arrived,
+                 left_sem, right_sem, swap_send, swap_recv, sum_send, sum_recv, full_send, full_recv,
+                 small_send, small_recv, store_sem, *, n, piece, hops, ups, halves):
+    section = lax.axis_index("section")
+    data = lax.axis_index("dp")
+    core = lax.rem(section, 2)
+    mate = {"section": section + 1 - 2 * core}
+    width = final.shape[2]
+    tiles = ups + halves
+    half = n // 2
+    micros, rows = lbuf.shape[1:3]
+
+    def place(p):
+        p = lax.rem(p + 2 * n, n)
+        return jnp.where(p < half, 2 * p, 2 * (n - 1 - p) + 1)
+
+    me = jnp.where(lax.rem(data, 2) == 0, data // 2, n - 1 - data // 2)
+    peers = ({"dp": place(me + 1)}, {"dp": place(me - 1)})
+    signs = (1, -1)
+
+    def remote(source, target, send, recv, device):
+        return pltpu.make_async_remote_copy(src_ref=source, dst_ref=target, send_sem=send, recv_sem=recv,
+                                            device_id=device, device_id_type=MESH)
+
+    def part(ref, column):
+        return ref.at[:, :, pl.ds(column * width, width)]
+
+    attn = [(xs, dqs), (xs, dks), (xs, dvs), (os_, dbs)] + [(part(hs, i), dfs) for i in range(halves)]
+    feed = [(y1s, part(das, i)) for i in range(ups)] + [(part(hs, halves + i), dfs) for i in range(halves)]
+
+    def loads(t, which):
+        b = t % 2
+        left, right = (attn, feed)[which][t // 2]
+        return (pltpu.make_async_copy(left, lbuf.at[b], left_sem.at[b]),
+                pltpu.make_async_copy(right, rbuf.at[b], right_sem.at[b]))
+
+    def start_load(t):
+        turn = core if t % 2 else 1 - core
+        for which in (0, 1):
+            @pl.when(turn == which)
+            def _():
+                for copy in loads(t, which):
+                    copy.start()
+
+    start_load(0)
+    barrier = pltpu.get_barrier_semaphore()
+    friends = [{axis: flipped(section if axis == "section" else data, bit)} for axis, bit in hops]
+    for device in [mate, *peers, *friends]:
+        pl.semaphore_signal(barrier, inc=1, device_id=device, device_id_type=MESH)
+    pl.semaphore_wait(barrier, 3 + len(friends))
+
+    held[0] = small_ref[...]
+
+    def small_copy(i):
+        return remote(held.at[i], arrived.at[i], small_send.at[i], small_recv.at[i], friends[i])
+
+    small_copy(0).start()
+
+    def finish_small(i):
+        small_copy(i).wait_recv()
+        total = held[i] + arrived[i]
+        if i + 1 < len(friends):
+            held[i + 1] = total
+            small_copy(i + 1).start()
+        else:
+            small_out[...] = total
+
+    def swap(j):
+        return remote(away.at[lax.rem(j, 2)], got.at[j, pl.ds(0, width)], swap_send.at[j], swap_recv.at[j], mate)
+
+    def piece_rows(index, d):
+        return pl.ds(pl.multiple_of((lax.rem(index + 2 * n, n) * 2 + d) * piece, 16), piece)
+
+    def sum_copy(i, d, s):
+        where = mine.at[i, piece_rows(me - signs[d] * s, d)]
+        return remote(where, slots.at[i, d, s], sum_send.at[i, d, s], sum_recv.at[i, d, s], peers[d])
+
+    def full_copy(i, d, s):
+        where = final.at[i, piece_rows(me + signs[d] * (1 - s), d)]
+        return remote(where, where, full_send.at[i, d, s], full_recv.at[i, d, s], peers[d])
+
+    def store(i):
+        return pltpu.make_async_copy(final.at[i], out_ref.at[i], store_sem.at[i])
+
+    def serve(i, s):
+        @pl.when(s == 0)
+        def _():
+            swap(i).wait_recv()
+
+        @pl.when((s >= 0) & (s < n))
+        def _():
+            for d in (0, 1):
+                here = piece_rows(me - signs[d] * s, d)
+                value = mine[i, here, :].astype(F32) + got[i, here, :].astype(F32)
+
+                @pl.when(s == 0)
+                def _():
+                    mine[i, here, :] = value.astype(BF16)
+                    sum_copy(i, d, s).start()
+
+                @pl.when(s > 0)
+                def _():
+                    sum_copy(i, d, s - 1).wait_recv()
+                    total = (value + slots[i, d, s - 1].astype(F32)).astype(BF16)
+
+                    @pl.when(s < n - 1)
+                    def _():
+                        mine[i, here, :] = total
+                        sum_copy(i, d, s).start()
+
+                    @pl.when(s == n - 1)
+                    def _():
+                        final[i, here, :] = total
+                        full_copy(i, d, 0).start()
+
+        @pl.when((s >= n) & (s < 2 * n - 1))
+        def _():
+            f = s - n + 1
+            for d in (0, 1):
+                full_copy(i, d, f - 1).wait_recv()
+
+                @pl.when(f < n - 1)
+                def _():
+                    full_copy(i, d, f).start()
+
+            @pl.when(f == n - 1)
+            def _():
+                store(i).start()
+
+    for t in range(2 * tiles):
+        if t + 1 < 2 * tiles:
+            start_load(t + 1)
+        b, j = t % 2, t // 2
+        for copy in loads(t, 0):
+            copy.wait()
+        tile = mm(lbuf[b].reshape(micros * rows, width), rbuf[b].reshape(micros * rows, width), 0, 0).astype(BF16)
+        if t % 2 == 0:
+            if j >= 2:
+                swap(j - 2).wait_send()
+            away[j % 2] = tile
+            swap(j).start()
+        else:
+            mine[j, 0:width, :] = tile
+        for i in range(tiles):
+            if t - 2 * i - 1 >= 0:
+                serve(i, jnp.int32(t - 2 * i - 1))
+
+    begin = 2 * tiles
+
+    def rest(t, carry):
+        for k in range(len(friends)):
+            @pl.when(t == begin + k)
+            def _():
+                finish_small(k)
+
+        def one(i, carry2):
+            serve(i, t - 2 * i - 1)
+            return carry2
+
+        lax.fori_loop(0, tiles, one, 0)
+        return carry
+
+    lax.fori_loop(begin, 2 * tiles - 1 + 2 * n - 1, rest, 0)
+
+    def finish(i, carry):
+        def sends(s, carry2):
+            for d in (0, 1):
+                sum_copy(i, d, s).wait_send()
+                full_copy(i, d, s).wait_send()
+            return carry2
+
+        lax.fori_loop(0, n - 1, sends, 0)
+        store(i).wait()
+        return carry
+
+    lax.fori_loop(0, tiles, finish, 0)
+    for j in range(tiles - 2, tiles):
+        swap(j).wait_send()
+    for i in range(len(friends)):
+        small_copy(i).wait_send()
+
+
+def weight_gradients(stacks, small, n, sections, width, ups, halves):
+    piece = ring_piece(n, width)
+    total = 2 * n * piece
+    micros, rows = stacks[0].shape[:2]
+    tiles = ups + halves
+    hops = [("dp", 1 << i) for i in range(n.bit_length() - 1)]
+    hops += [("section", 1 << i) for i in range(sections.bit_length() - 1)]
+    dma = pltpu.SemaphoreType.DMA
+    kept = pltpu.VMEM((tiles, total, width), BF16)
+    operand = pltpu.VMEM((2, micros, rows, width), BF16)
+    sums = pltpu.VMEM((len(hops),) + small.shape, F32)
     return pl.pallas_call(
-        functools.partial(grad_kernel, lefts=count),
-        grid=(tiles,),
-        in_specs=[spec(moving and left_moves)] * count + [spec(moving and not left_moves)] * count
-        + [pl.BlockSpec(memory_space=pl.ANY)] * len(extra),
-        out_specs=pl.BlockSpec((None, width, width), lambda t: place(t) + (0,)),
-        out_shape=shape_of((2, total, width)),
-        input_output_aliases={2 * count: 0} if extra else {},
-        compiler_params=pltpu.CompilerParams(vmem_limit_bytes=VMEM_BYTES),
-        name=name,
-    )(*lefts, *rights, *extra)
+        functools.partial(grads_kernel, n=n, piece=piece, hops=hops, ups=ups, halves=halves),
+        in_specs=[anywhere()] * len(stacks) + [on_chip()],
+        out_specs=[anywhere(), on_chip()],
+        out_shape=[shape_of((tiles, total, width)), shape_of(small.shape, F32)],
+        scratch_shapes=[
+            operand, operand, kept, kept, pltpu.VMEM((2, width, width), BF16), kept,
+            pltpu.VMEM((tiles, 2, n - 1, piece, width), BF16), sums, sums,
+            dma((2,)), dma((2,)), dma((tiles,)), dma((tiles,)),
+            dma((tiles, 2, n - 1)), dma((tiles, 2, n - 1)), dma((tiles, 2, n - 1)), dma((tiles, 2, n - 1)),
+            dma((len(hops),)), dma((len(hops),)), dma((tiles,))],
+        compiler_params=pltpu.CompilerParams(vmem_limit_bytes=VMEM_BYTES, collective_id=0, has_side_effects=True),
+        name="weight_gradients",
+    )(*stacks, small)
 
 
 def widen_kernel(in_ref, out_ref):
@@ -683,180 +862,17 @@
 
 
 def widen(data, blocks, offset, by_column):
-    width = data.shape[1]
+    width = data.shape[2]
     if by_column:
         shape, spec = (width, blocks * width), pl.BlockSpec((width, width), lambda b: (0, b))
     else:
         shape, spec = (blocks * width, width), pl.BlockSpec((width, width), lambda b: (b, 0))
     return pl.pallas_call(
         widen_kernel, grid=(blocks,),
-        in_specs=[pl.BlockSpec((width, width), lambda b: (offset + b, 0))],
+        in_specs=[pl.BlockSpec((None, width, width), lambda b: (offset + b, 0, 0))],
         out_specs=spec, out_shape=shape_of(shape, F32),
         compiler_params=pltpu.CompilerParams(vmem_limit_bytes=VMEM_BYTES), name="widen",
     )(data)
-
-
-def ring_layout(n, want):
-    subs = 2 if n <= 8 else 1
-    unit = 2 * n * subs
-    piece = -(-want // unit)
-    piece += -piece % 16
-    return subs, piece, unit * piece
-
-
-def flipped(index, bit):
-    return index + bit - 2 * bit * lax.rem(index // bit, 2)
-
-
-def ring_kernel(data_ref, small_ref, out_ref, small_out, mine, got, final, start, slots, held, arrived,
-                load_sem, store_sem, swap_send, swap_recv,
-                sum_send, sum_recv, full_send, full_recv, small_send, small_recv, *, n, subs, piece, hops):
-    section = lax.axis_index("section")
-    data = lax.axis_index("dp")
-    core = lax.rem(section, 2)
-    partner = section + 1 - 2 * core
-    half = n // 2
-
-    def place(p):
-        p = lax.rem(p + 2 * n, n)
-        return jnp.where(p < half, 2 * p, 2 * (n - 1 - p) + 1)
-
-    me = jnp.where(lax.rem(data, 2) == 0, data // 2, n - 1 - data // 2)
-    peers = (place(me + 1), place(me - 1))
-    signs = (1, -1)
-    span = subs * piece
-
-    def chunk(index):
-        return lax.rem(index + 2 * n, n)
-
-    def first_row(index, d):
-        return pl.multiple_of((chunk(index) * 2 + d) * span, 16)
-
-    loads, swaps = {}, {}
-    for j in range(n):
-        for d in (0, 1):
-            rows = pl.ds(first_row(me - signs[d] * j, d), span)
-            loads[j, d] = pltpu.make_async_copy(data_ref.at[core, rows], mine.at[rows], load_sem.at[d, j])
-            loads[j, d].start()
-    barrier = pltpu.get_barrier_semaphore()
-    pl.semaphore_signal(barrier, inc=1, device_id={"section": partner}, device_id_type=pl.DeviceIdType.MESH)
-    for d in (0, 1):
-        pl.semaphore_signal(barrier, inc=1, device_id={"dp": peers[d]}, device_id_type=pl.DeviceIdType.MESH)
-    friends = [{axis: flipped(section if axis == "section" else data, bit)} for axis, bit in hops]
-    for friend in friends:
-        pl.semaphore_signal(barrier, inc=1, device_id=friend, device_id_type=pl.DeviceIdType.MESH)
-    pl.semaphore_wait(barrier, 3 + len(friends))
-    held[0] = small_ref[...]
-    smalls = []
-
-    def start_small(i):
-        smalls.append(pltpu.make_async_remote_copy(
-            src_ref=held.at[i], dst_ref=arrived.at[i], send_sem=small_send.at[i], recv_sem=small_recv.at[i],
-            device_id=friends[i], device_id_type=pl.DeviceIdType.MESH))
-        smalls[i].start()
-
-    def finish_small(i):
-        smalls[i].wait_recv()
-        total = held[i] + arrived[i]
-        if i + 1 < len(friends):
-            held[i + 1] = total
-            start_small(i + 1)
-        else:
-            small_out[...] = total
-
-    start_small(0)
-    for j in range(n):
-        for d in (0, 1):
-            rows = pl.ds(first_row(me - signs[d] * j, d), span)
-            swaps[j, d] = pltpu.make_async_remote_copy(
-                src_ref=data_ref.at[1 - core, rows], dst_ref=got.at[rows],
-                send_sem=swap_send.at[d, j], recv_sem=swap_recv.at[d, j],
-                device_id={"section": partner}, device_id_type=pl.DeviceIdType.MESH)
-            swaps[j, d].start()
-
-    sums, fulls, stores = {}, {}, []
-
-    def own(j, d, u):
-        row = pl.multiple_of(first_row(me - signs[d] * j, d) + u * piece, 16)
-        rows = pl.ds(row, piece)
-        return mine[rows, :].astype(F32) + got[rows, :].astype(F32)
-
-    for s in range(n):
-        for d in (0, 1):
-            loads[s, d].wait()
-            swaps[s, d].wait_recv()
-        for u in range(subs):
-            for d in (0, 1):
-                value = own(s, d, u)
-                if s == 0:
-                    source = start.at[d, u]
-                else:
-                    sums[s - 1, d, u].wait_recv()
-                    source = slots.at[d, u, s - 1]
-                    value = value + source[...].astype(F32)
-                if s < n - 1:
-                    source[...] = value.astype(BF16)
-                    sums[s, d, u] = pltpu.make_async_remote_copy(
-                        src_ref=source, dst_ref=slots.at[d, u, s],
-                        send_sem=sum_send.at[d, u, s], recv_sem=sum_recv.at[d, u, s],
-                        device_id={"dp": peers[d]}, device_id_type=pl.DeviceIdType.MESH)
-                    sums[s, d, u].start()
-                else:
-                    row = pl.multiple_of(first_row(me - signs[d] * s, d) + u * piece, 16)
-                    final[pl.ds(row, piece), :] = value.astype(BF16)
-    waiting = list(range(len(friends)))
-    for s in range(n):
-        if s > 0 and waiting:
-            finish_small(waiting.pop(0))
-        for u in range(subs):
-            for d in (0, 1):
-                row = pl.multiple_of(first_row(me + signs[d] * (1 - s), d) + u * piece, 16)
-                rows = pl.ds(row, piece)
-                if s > 0:
-                    fulls[s - 1, d, u].wait_recv()
-                if s < n - 1:
-                    fulls[s, d, u] = pltpu.make_async_remote_copy(
-                        src_ref=final.at[rows], dst_ref=final.at[rows],
-                        send_sem=full_send.at[d, u, s], recv_sem=full_recv.at[d, u, s],
-                        device_id={"dp": peers[d]}, device_id_type=pl.DeviceIdType.MESH)
-                    fulls[s, d, u].start()
-                copy = pltpu.make_async_copy(final.at[rows], out_ref.at[rows], store_sem.at[d, u, s])
-                copy.start()
-                stores.append(copy)
-    for i in waiting:
-        finish_small(i)
-    for copy in smalls:
-        copy.wait_send()
-    for copy in swaps.values():
-        copy.wait_send()
-    for copy in sums.values():
-        copy.wait_send()
-    for copy in fulls.values():
-        copy.wait_send()
-    for copy in stores:
-        copy.wait()
-
-
-def ring_sum(data, small, n, sections, subs, piece):
-    total, width = data.shape[1:]
-    hops = [("dp", 1 << i) for i in range(n.bit_length() - 1)] + [("section", 1 << i) for i in range(sections.bit_length() - 1)]
-    dma = pltpu.SemaphoreType.DMA
-    return pl.pallas_call(
-        functools.partial(ring_kernel, n=n, subs=subs, piece=piece, hops=hops),
-        in_specs=[pl.BlockSpec(memory_space=pl.ANY), pl.BlockSpec(memory_space=pltpu.VMEM)],
-        out_specs=[pl.BlockSpec(memory_space=pl.ANY), pl.BlockSpec(memory_space=pltpu.VMEM)],
-        out_shape=[shape_of((total, width)), shape_of(small.shape, F32)],
-        scratch_shapes=[
-            pltpu.VMEM((total, width), BF16), pltpu.VMEM((total, width), BF16), pltpu.VMEM((total, width), BF16),
-            pltpu.VMEM((2, subs, piece, width), BF16), pltpu.VMEM((2, subs, n - 1, piece, width), BF16),
-            pltpu.VMEM((len(hops),) + small.shape, F32), pltpu.VMEM((len(hops),) + small.shape, F32),
-            dma((2, n)), dma((2, subs, n)), dma((2, n)), dma((2, n)),
-            dma((2, subs, n - 1)), dma((2, subs, n - 1)), dma((2, subs, n - 1)), dma((2, subs, n - 1)),
-            dma((len(hops),)), dma((len(hops),))],
-        compiler_params=pltpu.CompilerParams(
-            vmem_limit_bytes=VMEM_BYTES, collective_id=0, has_side_effects=True),
-        name="ring_sum",
-    )(data, small)
 
 
 def body(tokens, doc_ids, reset_flags, memory_init, w_proj, vectors, w_down, cotangent):
@@ -893,11 +909,8 @@
                             axis=0)
     blocks = hidden // width
     half = w_down.shape[0] // width
-    subs, piece, total = ring_layout(data_count, (blocks + half) * width)
-    stack = weight_grads([h], [df], blocks, True, lambda t: (t // half, blocks + t % half), total, None, "grad_down")
-    stack = weight_grads([y1], [da], blocks, False, lambda t: (1, t), total, stack, "grad_up")
-    stack = weight_grads([x_in] * 3 + [o], [dq, dk, dv, db], blocks, False, lambda t: (0, t), total, stack, "grad_attn")
-    summed, small = ring_sum(stack, small, data_count, lax.axis_size("section"), subs, piece)
+    summed, small = weight_gradients([x_in, o, y1, h, dq, dk, dv, db, da, df], small, data_count,
+                                     lax.axis_size("section"), width, blocks, half)
     total_vec = lax.dynamic_slice(small, (2 * section, 0), (2, width))[None]
     share = width // 4
     memory_total = lax.dynamic_slice(small, (8, section * share), (memory_count, share))

time: 560 us -> 537 us (0.959); the launches traced: 558 us -> 529 us
  Pallas kernels: 542 us -> 513 us
    pallas_call x6 -> x3, Pallas kernels: 214 us -> 185 us  [the longest x1 175 us: weight_gradients(): pl.pallas_call(functools.partial(grads_kernel, n=n, piece=piece, hops=hop...]
where the time goes in v4:
time: 537 us; the launch traced here: 529 us
  Pallas kernels  513 us (96%)
  local copies, waits for them, and re-layouts  12 us (2%)
    pallas_call x1, Pallas kernels, run_layers(): pl.pallas_call(layers_kernel, in_specs=[anywhere()] * 4 + [on_chip()] * 5...  328 us
    pallas_call x1, Pallas kernels, weight_gradients(): pl.pallas_call(functools.partial(grads_kernel, n=n, piece=piece, hops=hop...  175 us

profile of v4, /device:TPU:0, one launch (start us, length us, event | category | flops | bytes accessed | tf_op | source)
XLA Modules:
  0.0 529.4 jit_solution(9756520344110104798)
XLA Ops:
  0.7 0.8 dynamic-slice_bitcast_fusion.4
  1.5 0.1 pad.8.clone
  1.6 1.3 broadcast_in_dim.22.key_ref
  2.9 0.7 tile.9.query_ref
  3.6 0.8 constant_dynamic-slice_fusion
  4.5 0.5 slice.35
  5.0 0.5 slice.36
  5.5 1.3 pad_convert_fusion
  6.8 0.7 stack.9.fresh_ref
  7.5 1.4 concatenate.12.init_ref
  8.9 327.8 %layers.1 = (bf16[2,512,768]{2,1,0:T(8,128)(2,1)}, bf16[2,512,768]{2,1,0:T(8,128)(2,1)}, f32[16,768]{1,0:T(8,128)}, f32[8,768]{1,0:T(8,128)}, bf16[4,528,768]{2,...) custom-call(bf16[2,512,768]{2,1,0:T(8,128)(2,1)} %bitcast.23, ...), custom_call_target="tpu_custom_call" | custom-call | tf_op jit(solution)/shard_map/layers/pallas_call | solution.py:619
  336.7 0.7 slice_select_fusion.1
  337.5 1.4 pad_maximum_fusion.small_ref
  338.9 174.9 %weight_gradients.1 = (bf16[6,768,768]{2,1,0:T(8,128)(2,1)}, f32[24,768]{1,0:T(8,128)}) custom-call(bf16[4,528,768]{2,1,0:T(8,128)(2,1)} %get-tuple-element.24.xs, bf16[4,528,768]{2,1,0:T(8,128)(2,1)} %get-tuple-element.25.os_, bf16[4,528,768]{2,1,0:T(8,128)(2,1)} %get-tuple-element.26.y1s, bf16[4,528,3072]{2,1,0:T(8,128)(2,1)} %get-tuple-element.27.hs, ...), custom_call_target="tpu_custom_call" | custom-call | tf_op jit(solution)/shard_map/weight_gradients/pallas_call | solution.py:844
  513.8 6.5 %widen.2 = f32[768,3072]{1,0:T(8,128)} custom-call(bf16[6,768,768]{2,1,0:T(8,128)(2,1)} %get-tuple-element.36.in_ref), custom_call_target="tpu_custom_call" | custom-call | tf_op jit(solution)/shard_map/widen/pallas_call | solution.py:870
  520.3 0.0 copy-start.1
  520.3 3.7 widen.3
  524.0 0.0 copy-start
  524.0 1.5 constant_dynamic-slice_fusion.2
  525.6 1.3 dynamic-slice_bitcast_fusion
  526.9 0.0 copy-done.1
  526.9 1.1 copy.16
  528.0 0.0 copy-done
  528.0 1.1 copy.17
  (6 shorter events, 0.0 us)
Async XLA Ops:
  520.3 6.6 %copy-start.1 = (bf16[2,512,768]{2,1,0:T(8,128)(2,1)S(1)}, bf16[2,512,768]{2,1,0:T(8,128)(2,1)}, u32[]{:S(2)}) copy-start(bf16[2,512,768]{2,1,0:T(8,128)(2,1)} %get-tuple-element.22) | copy-start | bytes 4718596
  524.0 4.0 copy-start
